TPU v7x, 32 devices: a whole 2x2x4 slice. The times are simulated.
32 devices in a mesh: dp: 8 (over z, core), tensor: 4 (over y, x).
Axes of the slice: x: 2, y: 2, z: 4, core: 2. Of those that a mesh axis runs over, the one named last changes fastest.
Arguments:
- hidden_in: bfloat16 [6144, 2048], P(('dp', 'tensor')), may hold values from -6 to 6
- attn_gain: float32 [2048], replicated, may hold values from 0.5 to 1.5
- q_weight: bfloat16 [2048, 2048], P(None, 'tensor'), may hold values from -0.125 to 0.125
- q_bias: float32 [2048], P('tensor'), may hold values from -1.75 to 1.75
- k_weight: bfloat16 [2048, 2048], P(None, 'tensor'), may hold values from -0.125 to 0.125
- k_bias: float32 [2048], P('tensor'), may hold values from -1.75 to 1.75
- v_weight: bfloat16 [2048, 2048], P(None, 'tensor'), may hold values from -0.125 to 0.125
- v_bias: float32 [2048], P('tensor'), may hold values from -1.75 to 1.75
- o_weight: bfloat16 [2048, 2048], P('tensor'), may hold values from -0.75 to 0.75
- mlp_gain: float32 [2048], replicated, may hold values from 0.5 to 1.5
- expert_gate: bfloat16 [8, 2048, 1408], P('dp', None, 'tensor'), may hold values from -0.125 to 0.125
- expert_up: bfloat16 [8, 2048, 1408], P('dp', None, 'tensor'), may hold values from -0.125 to 0.125
- expert_down: bfloat16 [8, 1408, 2048], P('dp', 'tensor'), may hold values from -0.4375 to 0.4375
- shared_gate: bfloat16 [2048, 5632], P(None, 'tensor'), may hold values from -0.125 to 0.125
- shared_up: bfloat16 [2048, 5632], P(None, 'tensor'), may hold values from -0.125 to 0.125
- shared_down: bfloat16 [5632, 2048], P('tensor'), may hold values from -0.15625 to 0.15625
- shared_router: bfloat16 [2048], replicated, may hold values from -0.125 to 0.125
- routes: int32 [6144, 4], P('dp'), may hold values from 0 to 7, all different within a row; in each aligned block of 768 rows (0 to 767, 768 to 1535, ...) at most 480 rows name the same one
- gate_weights: float32 [6144, 4], P('dp'), may hold values from 0.1 to 0.4
- lengths: int32 [8, 2], replicated, may hold values from 1 to 128, 224 in all within a row
- loss_mask: int32 [6144], replicated, may hold values 0 or 1
- teacher: bfloat16 [6144, 2048], P(('dp', 'tensor')), may hold values from -9 to 9
- cotangent: bfloat16 [6144, 2048], P(('dp', 'tensor')), may hold values from -6 to 6
Outputs:
- block_out: bfloat16 [6144, 2048], P(('dp', 'tensor'))
- teacher_loss: float32 [], replicated
- input_grad: float32 [6144, 2048], P(('dp', 'tensor'))
- attn_gain_grad: float32 [2048], replicated
- q_weight_grad: float32 [2048, 2048], P(None, 'tensor')
- q_bias_grad: float32 [2048], P('tensor')
- k_weight_grad: float32 [2048, 2048], P(None, 'tensor')
- k_bias_grad: float32 [2048], P('tensor')
- v_weight_grad: float32 [2048, 2048], P(None, 'tensor')
- v_bias_grad: float32 [2048], P('tensor')
- o_weight_grad: float32 [2048, 2048], P('tensor')
- mlp_gain_grad: float32 [2048], replicated
- expert_gate_grad: float32 [8, 2048, 1408], P('dp', None, 'tensor')
- expert_up_grad: float32 [8, 2048, 1408], P('dp', None, 'tensor')
- expert_down_grad: float32 [8, 1408, 2048], P('dp', 'tensor')
- shared_gate_grad: float32 [2048, 5632], P(None, 'tensor')
- shared_up_grad: float32 [2048, 5632], P(None, 'tensor')
- shared_down_grad: float32 [5632, 2048], P('tensor')
- shared_router_grad: float32 [2048], replicated
Inputs may be any that keep to these rules, and one draw needn't show every extreme that they name: `routes`: in each aligned block of 768 rows (one group), no expert is named by more than 480 rows, a bound that some block reaches; a row names different experts.
All inputs are finite; a program needn't handle non-finite values.
Results may differ from a plain program's by a relative error of at most 0.035.
Values may be sent and summed in bfloat16 or wider, within the bound.
No kernel may reach another device: no remote copies, remote signals or barrier semaphores. Data moves between devices by JAX's collectives and lax.ppermute only.
A program may use at most 384 MiB of HBM per device.

v0:
```python
import math

import jax
import jax.numpy as jnp
from jax import lax
from jax.sharding import PartitionSpec as P

D = 2048
HD = 128
TOPK = 4
PROMPT = 512
SLOT = 128
CONTS = 2
GROUP = 768


EPSILON = 1e-06
ROTARY_BASE = 1000000.0
HIGHEST = lax.Precision.HIGHEST


def slot_layout(lengths_row):
    position = jnp.arange(GROUP, dtype=jnp.int32)
    offset = jnp.maximum(position - PROMPT, 0)
    in_prompt = position < PROMPT
    segment = jnp.where(in_prompt, 0, 1 + offset // SLOT)
    rotary_place = jnp.where(in_prompt, position, PROMPT + offset % SLOT)
    matches = segment[:, None] - 1 == jnp.arange(CONTS, dtype=jnp.int32)[None, :]
    length_here = jnp.sum(jnp.where(matches, lengths_row[None, :], 0), axis=1)
    living = in_prompt | (offset % SLOT < length_here)
    return (segment, rotary_place, living)


def visible_keys(segment, living):
    position = jnp.arange(GROUP, dtype=jnp.int32)
    causal = position[None, :] <= position[:, None]
    same_part = (segment[None, :] == segment[:, None]) | (segment[None, :] == 0)
    return causal & same_part & living[None, :]


def rotary_tables(rotary_place):
    freqs = jnp.exp(jnp.arange(HD // 2, dtype=jnp.float32) * (-2.0 * math.log(ROTARY_BASE) / HD))
    angles = rotary_place.astype(jnp.float32)[:, None] * freqs[None, :]
    angles = jnp.concatenate([angles, angles], axis=1)
    return (jnp.cos(angles), jnp.sin(angles))


def rotate(values, cosine, sine):
    half = values.shape[-1] // 2
    flipped = jnp.concatenate([-values[..., half:], values[..., :half]], axis=-1)
    return values * cosine[:, None, :] + flipped * sine[:, None, :]


def rotate_back(grads, cosine, sine):
    half = grads.shape[-1] // 2
    turned = grads * sine[:, None, :]
    flipped = jnp.concatenate([turned[..., half:], -turned[..., :half]], axis=-1)
    return grads * cosine[:, None, :] + flipped


def attention_scores(query_low, key_low, visible, scale):
    scores = (
        jnp.einsum("thd,shd->hts", query_low, key_low, preferred_element_type=jnp.float32) * scale
    )
    return jnp.where(visible[None], scores, -1e30)


def swiglu_back(grad_hidden, gate_in, up_in):
    squash = jax.nn.sigmoid(gate_in)
    gate_grad = grad_hidden * up_in * squash * (1.0 + gate_in * (1.0 - squash))
    up_grad = grad_hidden * gate_in * squash
    return (gate_grad.astype(jnp.bfloat16), up_grad.astype(jnp.bfloat16))


def expert_apply(rows, w_gate, w_up, w_down):
    wide = jnp.float32
    gate_in = jnp.einsum("bcd,df->bcf", rows, w_gate[0], preferred_element_type=wide)
    up_in = jnp.einsum("bcd,df->bcf", rows, w_up[0], preferred_element_type=wide)
    hidden = (jax.nn.silu(gate_in) * up_in).astype(jnp.bfloat16)
    output = jnp.einsum("bcf,fd->bcd", hidden, w_down[0], preferred_element_type=wide)
    return (output, gate_in, up_in, hidden)


def expert_backward(rows, grad_out, gate_in, up_in, hidden, w_gate, w_up, w_down):
    wide = jnp.float32
    grad_hidden = jnp.einsum("bcd,fd->bcf", grad_out, w_down[0], preferred_element_type=wide)
    down_grad = jnp.einsum("bcf,bcd->fd", hidden, grad_out, preferred_element_type=wide)[None]
    gate_grad_in, up_grad_in = swiglu_back(grad_hidden, gate_in, up_in)
    gate_grad = jnp.einsum("bcd,bcf->df", rows, gate_grad_in, preferred_element_type=wide)[None]
    up_grad = jnp.einsum("bcd,bcf->df", rows, up_grad_in, preferred_element_type=wide)[None]
    rows_grad = jnp.einsum(
        "bcf,df->bcd", gate_grad_in, w_gate[0], preferred_element_type=wide
    ) + jnp.einsum("bcf,df->bcd", up_grad_in, w_up[0], preferred_element_type=wide)
    return (rows_grad, gate_grad, up_grad, down_grad)


def shards(
    hidden_in,
    attn_gain,
    q_weight,
    q_bias,
    k_weight,
    k_bias,
    v_weight,
    v_bias,
    o_weight,
    mlp_gain,
    expert_gate,
    expert_up,
    expert_down,
    shared_gate,
    shared_up,
    shared_down,
    shared_router,
    routes,
    gate_weights,
    lengths,
    loss_mask,
    teacher,
    cotangent,
):
    wide = jnp.float32
    narrow = jnp.bfloat16
    data_index = lax.axis_index("dp")
    slice_index = lax.axis_index("tensor")
    own_rows = hidden_in.shape[0]
    heads = q_weight.shape[1] // HD
    experts = lax.axis_size("dp")
    capacity = 5 * GROUP * TOPK // (4 * experts)
    scale = 1.0 / math.sqrt(HD)
    all_layout = jax.vmap(slot_layout)(lengths)
    valid_all = all_layout[2].reshape(-1) & (loss_mask == 1)
    valid_count = jnp.sum(valid_all.astype(wide))
    valid_own = lax.dynamic_slice_in_dim(
        valid_all, data_index * GROUP + slice_index * own_rows, own_rows, 0
    )
    segment = lax.dynamic_index_in_dim(all_layout[0], data_index, 0, keepdims=False)
    rotary_place = lax.dynamic_index_in_dim(all_layout[1], data_index, 0, keepdims=False)
    living = lax.dynamic_index_in_dim(all_layout[2], data_index, 0, keepdims=False)
    visible = visible_keys(segment, living)
    cosine, sine = rotary_tables(rotary_place)
    group_rows = lax.all_gather(hidden_in, "tensor", axis=0, tiled=True)
    residual = group_rows.astype(wide)
    inverse_one = lax.rsqrt(jnp.mean(residual * residual, axis=1, keepdims=True) + EPSILON)
    normed_one = (residual * inverse_one * attn_gain).astype(narrow)
    query_lin = jnp.dot(normed_one, q_weight, preferred_element_type=wide) + q_bias
    key_lin = jnp.dot(normed_one, k_weight, preferred_element_type=wide) + k_bias
    value_low = (
        (jnp.dot(normed_one, v_weight, preferred_element_type=wide) + v_bias)
        .astype(narrow)
        .reshape(GROUP, heads, HD)
    )
    query_low = rotate(query_lin.reshape(GROUP, heads, HD), cosine, sine).astype(narrow)
    key_low = rotate(key_lin.reshape(GROUP, heads, HD), cosine, sine).astype(narrow)
    scores = attention_scores(query_low, key_low, visible, scale)
    top_score = jnp.max(scores, axis=2, keepdims=True)
    expo = jnp.exp(scores - top_score)
    total_expo = jnp.sum(expo, axis=2, keepdims=True)
    log_total = top_score + jnp.log(total_expo)
    probs_low = (expo / total_expo).astype(narrow)
    mixed = jnp.einsum("hts,shd->thd", probs_low, value_low, preferred_element_type=wide)
    mixed_low = mixed.reshape(GROUP, heads * HD).astype(narrow)
    head_part = jnp.dot(mixed_low, o_weight, preferred_element_type=wide)
    attn_total = lax.psum(
        head_part.astype(narrow).astype(wide).astype(jnp.bfloat16), "tensor"
    ).astype(jnp.float32)
    hidden_mid = residual + attn_total
    inverse_two = lax.rsqrt(jnp.mean(hidden_mid * hidden_mid, axis=1, keepdims=True) + EPSILON)
    normed_two = (hidden_mid * inverse_two * mlp_gain).astype(narrow)
    shared_gate_in = jnp.dot(normed_two, shared_gate, preferred_element_type=wide)
    shared_up_in = jnp.dot(normed_two, shared_up, preferred_element_type=wide)
    shared_hidden = (jax.nn.silu(shared_gate_in) * shared_up_in).astype(narrow)
    shared_out = jnp.dot(shared_hidden, shared_down, preferred_element_type=wide)
    router_gate = jax.nn.sigmoid(jnp.dot(normed_two, shared_router, preferred_element_type=wide))
    flat_routes = routes.reshape(-1)
    member = (flat_routes[:, None] == jnp.arange(experts, dtype=jnp.int32)[None, :]).astype(
        jnp.int32
    )
    earlier = jnp.sum((jnp.cumsum(member, axis=0) - member) * member, axis=1)
    slot_of = flat_routes * capacity + earlier
    slot_source = (
        jnp.full((experts * capacity,), GROUP * TOPK, jnp.int32)
        .at[slot_of]
        .set(jnp.arange(GROUP * TOPK, dtype=jnp.int32))
    )
    source_row = slot_source // TOPK
    padded_two = jnp.concatenate([normed_two, jnp.zeros((1, D), narrow)], axis=0)
    dispatched = padded_two[source_row].reshape(experts, capacity, D)
    slot_gate = jnp.concatenate([gate_weights.reshape(-1), jnp.zeros((1,), wide)], axis=0)[
        slot_source
    ]
    slot_pairs = slot_of.reshape(GROUP, TOPK)
    expert_rows = lax.all_to_all(dispatched, "dp", split_axis=0, concat_axis=0, tiled=True)
    expert_result, kept_gate, kept_up, kept_hidden = expert_apply(
        expert_rows, expert_gate, expert_up, expert_down
    )
    returned = lax.all_to_all(
        expert_result.astype(jnp.bfloat16), "dp", split_axis=0, concat_axis=0, tiled=True
    ).astype(expert_result.dtype)
    returned_flat = returned.reshape(experts * capacity, D)
    expert_mix = jnp.zeros((GROUP, D), wide)
    for which in range(TOPK):
        expert_mix = (
            expert_mix + gate_weights[:, which : which + 1] * returned_flat[slot_pairs[:, which]]
        )
    branch_total = router_gate[:, None] * shared_out + expert_mix
    branch_own = lax.psum_scatter(
        branch_total.astype(jnp.bfloat16), "tensor", scatter_dimension=0, tiled=True
    ).astype(jnp.float32)
    hidden_own = lax.dynamic_slice_in_dim(hidden_mid, slice_index * own_rows, own_rows, 0)
    result = hidden_own + branch_own
    difference = result - teacher.astype(wide)
    squared_own = jnp.sum(jnp.where(valid_own[:, None], difference * difference, 0.0))
    result_grad = cotangent.astype(wide) + jnp.where(
        valid_own[:, None], difference * (2.0 / (valid_count * D)), 0.0
    )
    grad_rows = lax.all_gather(result_grad.astype(narrow), "tensor", axis=0, tiled=True)
    grad_wide = grad_rows.astype(wide)
    gate_part = jnp.sum(grad_wide * shared_out, axis=1)
    grad_shared = (grad_wide * router_gate[:, None]).astype(narrow)
    shared_down_grad = jnp.einsum(
        "tf,td->fd", shared_hidden, grad_shared, preferred_element_type=wide
    )
    grad_hidden_shared = jnp.einsum(
        "td,fd->tf", grad_shared, shared_down, preferred_element_type=wide
    )
    grad_gate_shared, grad_up_shared = swiglu_back(grad_hidden_shared, shared_gate_in, shared_up_in)
    shared_gate_grad = jnp.einsum(
        "td,tf->df", normed_two, grad_gate_shared, preferred_element_type=wide
    )
    shared_up_grad = jnp.einsum(
        "td,tf->df", normed_two, grad_up_shared, preferred_element_type=wide
    )
    norm_two_part = jnp.einsum(
        "tf,df->td", grad_gate_shared, shared_gate, preferred_element_type=wide
    ) + jnp.einsum("tf,df->td", grad_up_shared, shared_up, preferred_element_type=wide)
    padded_grad = jnp.concatenate([grad_rows, jnp.zeros((1, D), narrow)], axis=0)
    grad_dispatched = (
        (padded_grad[source_row].astype(wide) * slot_gate[:, None])
        .astype(narrow)
        .reshape(experts, capacity, D)
    )
    grad_arrived = lax.all_to_all(grad_dispatched, "dp", split_axis=0, concat_axis=0, tiled=True)
    rows_grad, expert_gate_grad, expert_up_grad, expert_down_grad = expert_backward(
        expert_rows,
        grad_arrived,
        kept_gate,
        kept_up,
        kept_hidden,
        expert_gate,
        expert_up,
        expert_down,
    )
    grad_back = lax.all_to_all(
        rows_grad.astype(jnp.bfloat16), "dp", split_axis=0, concat_axis=0, tiled=True
    ).astype(rows_grad.dtype)
    grad_back_flat = grad_back.reshape(experts * capacity, D)
    for which in range(TOPK):
        norm_two_part = norm_two_part + grad_back_flat[slot_pairs[:, which]]
    norm_two_sum, gate_sum = (
        lax.psum(norm_two_part.astype(jnp.bfloat16), "tensor").astype(jnp.float32),
        lax.psum(gate_part.astype(jnp.bfloat16), "tensor").astype(jnp.float32),
    )
    logit_grad = gate_sum * router_gate * (1.0 - router_gate)
    normed_two_grad = norm_two_sum + logit_grad[:, None] * shared_router.astype(wide)[None, :]
    shared_router_grad = jnp.einsum(
        "t,td->d", logit_grad, normed_two.astype(wide), precision=HIGHEST
    )
    hat_two = hidden_mid * inverse_two
    mlp_gain_grad = jnp.sum(normed_two_grad * hat_two, axis=0)
    scaled_two = normed_two_grad * mlp_gain
    hidden_grad = grad_wide + inverse_two * (
        scaled_two - hat_two * jnp.mean(scaled_two * hat_two, axis=1, keepdims=True)
    )
    hidden_grad_low = hidden_grad.astype(narrow)
    o_weight_grad = jnp.einsum("tk,td->kd", mixed_low, hidden_grad_low, preferred_element_type=wide)
    mixed_grad = (
        jnp.einsum("td,kd->tk", hidden_grad_low, o_weight, preferred_element_type=wide)
        .astype(narrow)
        .reshape(GROUP, heads, HD)
    )
    scores_again = attention_scores(query_low, key_low, visible, scale)
    probs = jnp.exp(scores_again - log_total)
    probs_grad = jnp.einsum("thd,shd->hts", mixed_grad, value_low, preferred_element_type=wide)
    value_grad = jnp.einsum(
        "hts,thd->shd", probs.astype(narrow), mixed_grad, preferred_element_type=wide
    )
    inner = jnp.sum(probs * probs_grad, axis=2, keepdims=True)
    scores_grad = (probs * (probs_grad - inner)).astype(narrow)
    query_grad = (
        jnp.einsum("hts,shd->thd", scores_grad, key_low, preferred_element_type=wide) * scale
    )
    key_grad = (
        jnp.einsum("hts,thd->shd", scores_grad, query_low, preferred_element_type=wide) * scale
    )
    query_lin_grad = rotate_back(query_grad, cosine, sine).reshape(GROUP, heads * HD).astype(narrow)
    key_lin_grad = rotate_back(key_grad, cosine, sine).reshape(GROUP, heads * HD).astype(narrow)
    value_lin_grad = value_grad.reshape(GROUP, heads * HD).astype(narrow)
    q_weight_grad = jnp.einsum("td,tk->dk", normed_one, query_lin_grad, preferred_element_type=wide)
    k_weight_grad = jnp.einsum("td,tk->dk", normed_one, key_lin_grad, preferred_element_type=wide)
    v_weight_grad = jnp.einsum("td,tk->dk", normed_one, value_lin_grad, preferred_element_type=wide)
    q_bias_grad = jnp.sum(query_lin_grad.astype(wide), axis=0)
    k_bias_grad = jnp.sum(key_lin_grad.astype(wide), axis=0)
    v_bias_grad = jnp.sum(value_lin_grad.astype(wide), axis=0)
    normed_one_grad = lax.psum_scatter(
        (
            jnp.einsum("tk,dk->td", query_lin_grad, q_weight, preferred_element_type=wide)
            + jnp.einsum("tk,dk->td", key_lin_grad, k_weight, preferred_element_type=wide)
            + jnp.einsum("tk,dk->td", value_lin_grad, v_weight, preferred_element_type=wide)
        ).astype(jnp.bfloat16),
        "tensor",
        scatter_dimension=0,
        tiled=True,
    ).astype(jnp.float32)
    own_input = hidden_in.astype(wide)
    inverse_own = lax.rsqrt(jnp.mean(own_input * own_input, axis=1, keepdims=True) + EPSILON)
    hat_one = own_input * inverse_own
    gain_one_part = jnp.sum(normed_one_grad * hat_one, axis=0)
    scaled_one = normed_one_grad * attn_gain
    hidden_grad_own = lax.dynamic_slice_in_dim(hidden_grad, slice_index * own_rows, own_rows, 0)
    input_grad = hidden_grad_own + inverse_own * (
        scaled_one - hat_one * jnp.mean(scaled_one * hat_one, axis=1, keepdims=True)
    )
    summed = (
        lax.psum(q_weight_grad.astype(jnp.bfloat16), "dp").astype(jnp.float32),
        lax.psum(q_bias_grad.astype(jnp.bfloat16), "dp").astype(jnp.float32),
        lax.psum(k_weight_grad.astype(jnp.bfloat16), "dp").astype(jnp.float32),
        lax.psum(k_bias_grad.astype(jnp.bfloat16), "dp").astype(jnp.float32),
        lax.psum(v_weight_grad.astype(jnp.bfloat16), "dp").astype(jnp.float32),
        lax.psum(v_bias_grad.astype(jnp.bfloat16), "dp").astype(jnp.float32),
        lax.psum(o_weight_grad.astype(jnp.bfloat16), "dp").astype(jnp.float32),
        lax.psum(mlp_gain_grad.astype(jnp.bfloat16), "dp").astype(jnp.float32),
        lax.psum(shared_gate_grad.astype(jnp.bfloat16), "dp").astype(jnp.float32),
        lax.psum(shared_up_grad.astype(jnp.bfloat16), "dp").astype(jnp.float32),
        lax.psum(shared_down_grad.astype(jnp.bfloat16), "dp").astype(jnp.float32),
        lax.psum(shared_router_grad.astype(jnp.bfloat16), "dp").astype(jnp.float32),
    )
    attn_gain_grad, squared_total = lax.psum((gain_one_part, squared_own), ("dp", "tensor"))
    teacher_loss = squared_total / (valid_count * D)
    return (
        result.astype(narrow),
        teacher_loss,
        input_grad,
        attn_gain_grad,
        summed[0],
        summed[1],
        summed[2],
        summed[3],
        summed[4],
        summed[5],
        summed[6],
        summed[7],
        expert_gate_grad,
        expert_up_grad,
        expert_down_grad,
        summed[8],
        summed[9],
        summed[10],
        summed[11],
    )


def solution(mesh):
    return jax.shard_map(
        shards,
        mesh=mesh,
        in_specs=(
            P(("dp", "tensor"), None),
            P(),
            P(None, "tensor"),
            P("tensor"),
            P(None, "tensor"),
            P("tensor"),
            P(None, "tensor"),
            P("tensor"),
            P("tensor", None),
            P(),
            P("dp", None, "tensor"),
            P("dp", None, "tensor"),
            P("dp", "tensor", None),
            P(None, "tensor"),
            P(None, "tensor"),
            P("tensor", None),
            P(),
            P("dp", None),
            P("dp", None),
            P(),
            P(),
            P(("dp", "tensor"), None),
            P(("dp", "tensor"), None),
        ),
        out_specs=(
            P(("dp", "tensor"), None),
            P(),
            P(("dp", "tensor"), None),
            P(),
            P(None, "tensor"),
            P("tensor"),
            P(None, "tensor"),
            P("tensor"),
            P(None, "tensor"),
            P("tensor"),
            P("tensor", None),
            P(),
            P("dp", None, "tensor"),
            P("dp", None, "tensor"),
            P("dp", "tensor", None),
            P(None, "tensor"),
            P(None, "tensor"),
            P("tensor", None),
            P(),
        ),
        check_vma=False,
    )
```

profile of v0, /device:TPU:0, one launch (start us, length us, event | category | flops | bytes accessed | tf_op | source)
XLA Modules:
  0.0 2751.0 jit_solution(12109795124816306607)
XLA Ops:
  12.7 43.9 %all-gather.3.cloned.1.call-done = bf16[768,2048]{1,0:T(8,128)(2,1)} async-done(((bf16[192,2048]{1,0:T(8,128)(2,1)}), bf16[768,2048]{1,0:T(8,128)(2,1)}) %all-gather.3.cloned.1.call-update) | async-done | bytes 3145744 | tf_op jit(solution)/shard_map/all_gather | solution.py:142
  99.7 68.7 %all-reduce.9.cloned.1.call-done = bf16[768,2048]{1,0:T(8,128)(2,1)} async-done(((bf16[768,2048]{1,0:T(8,128)(2,1)}), bf16[768,2048]{1,0:T(8,128)(2,1)}) %all-reduce.9.cloned.1.call-update) | async-done | bytes 3145744 | tf_op jit(solution)/shard_map/psum | solution.py:164
  180.9 31.8 %gather_fusion = bf16[3840,2048]{1,0:T(8,128)(2,1)} fusion(bf16[769,2048]{1,0:T(8,128)(2,1)} %concatenate.35, s32[4096]{0:T(1024)S(1)} %pad_clamp_fusion.1), kind=kCustom, calls=%fused_computation | custom fusion | bytes 31472640 | tf_op jit(solution)/shard_map/gather | solution.py:188
  212.7 347.0 %all_to_all.20 = bf16[8,480,2048]{2,1,0:T(8,128)(2,1)S(1)} all-to-all(bf16[8,480,2048]{2,1,0:T(8,128)(2,1)} %bitcast.151), channel_id=1, replica_groups=mesh['dp'=8,'tensor'=4] {'dp'}, dimensions={0} | all-to-all | bytes 31457280 | tf_op jit(solution)/shard_map/all_to_all | solution.py:193
  618.9 320.2 %all-to-all-done.1 = bf16[8,480,2048]{2,1,0:T(8,128)(2,1)} async-done(((bf16[8,480,2048]{2,1,0:T(8,128)(2,1)}), bf16[8,480,2048]{2,1,0:T(8,128)(2,1)}, u32[]{:S(2)}, u32[]{:S(2)}) %all-to-all-start.1) | async-done | bytes 15728672 | tf_op jit(solution)/shard_map/all_to_all | solution.py:197
  939.1 17.9 bitcast_convert_fusion.1
  974.2 17.2 gather_fusion.3
  1008.5 17.3 gather_fusion.1
  1044.2 40.5 %reduce-scatter.3.cloned.1.call-done = bf16[192,2048]{1,0:T(8,128)(2,1)} async-done(((bf16[768,2048]{1,0:T(8,128)(2,1)}), bf16[192,2048]{1,0:T(8,128)(2,1)}) %reduce-scatter.3.cloned.1.call-update) | async-done | bytes 786448 | tf_op jit(solution)/shard_map/reduce_scatter | solution.py:207
  1089.5 20.2 gather_fusion.6
  1109.7 23.4 all-gather.5.cloned.1.call-done
  1137.1 31.8 %gather_fusion.5 = bf16[3840,2048]{1,0:T(8,128)(2,1)} fusion(bf16[769,2048]{1,0:T(8,128)(2,1)} %concatenate.36, s32[4096]{0:T(1024)S(1)} %copy-done.48), kind=kCustom, calls=%fused_computation.5 | custom fusion | bytes 31472640 | tf_op jit(solution)/shard_map/gather | solution.py:239
  1177.7 346.9 %all_to_all.21 = bf16[8,480,2048]{2,1,0:T(8,128)(2,1)} all-to-all(bf16[8,480,2048]{2,1,0:T(8,128)(2,1)S(1)} %fusion), channel_id=1, replica_groups=mesh['dp'=8,'tensor'=4] {'dp'}, dimensions={0} | all-to-all | bytes 31457280 | tf_op jit(solution)/shard_map/all_to_all | solution.py:243
  1524.7 17.9 multiply_convert_fusion.2
  1557.1 18.1 add_convert_fusion
  1604.4 317.6 %all-to-all-done.3 = bf16[8,480,2048]{2,1,0:T(8,128)(2,1)} async-done(((bf16[8,480,2048]{2,1,0:T(8,128)(2,1)}), bf16[8,480,2048]{2,1,0:T(8,128)(2,1)}, u32[]{:S(2)}, u32[]{:S(2)}) %all-to-all-start.3) | async-done | bytes 15728672 | tf_op jit(solution)/shard_map/all_to_all | solution.py:254
  1922.0 17.8 bitcast_convert_fusion
  1939.9 17.1 gather_fusion.10
  1974.1 17.2 gather_fusion.8
  1991.3 17.5 gather_fusion.7
  2039.1 71.6 %all-reduce.11.cloned.1.call-done = bf16[768,2048]{1,0:T(8,128)(2,1)} async-done(((bf16[768,2048]{1,0:T(8,128)(2,1)}), bf16[768,2048]{1,0:T(8,128)(2,1)}) %all-reduce.11.cloned.1.call-update) | async-done | bytes 3145744 | tf_op jit(solution)/shard_map/psum | solution.py:261
  2232.1 30.8 %all-reduce.3 = (bf16[512]{0:T(512)(128)(2,1)S(1)}, bf16[512]{0:T(512)(128)(2,1)S(1)}, bf16[512]{0:T(512)(128)(2,1)S(1)}, bf16[2048]{0:T(1024)(128)(2,1)S(1)}, bf16[2048]{0:T(1024)(128)(2,1)S(1)}) all-reduce(bf16[512]{0:T(512)(128)(2,1)S(1)} %bitcast.182, ...), channel_id=1, replica_groups=mesh['dp'=8,'tensor'=4] {'dp'}, use_global_device_ids=true, to_apply=%region_26.27 | all-reduce | flops 5632 | bytes 22528 | tf_op jit(solution)/shard_map/psum | solution.py:326
  2267.6 39.1 %all-reduce.2 = (f32[]{:T(128)}, f32[2048]{0:T(1024)}) all-reduce(f32[]{:T(128)} %get-tuple-element.56, f32[2048]{0:T(1024)S(1)} %get-tuple-element.21), channel_id=1, replica_groups=mesh['dp'=8,'tensor'=4] {'dp','tensor'}, use_global_device_ids=true, to_apply=%region_12.13 | all-reduce | flops 2049 | bytes 16392 | tf_op jit(solution)/shard_map/psum | solution.py:338
  2310.8 401.6 %all-reduce.13.cloned.1.call-done = (bf16[2048,512]{1,0:T(8,128)(2,1)}, bf16[2048,512]{1,0:T(8,128)(2,1)}, bf16[2048,512]{1,0:T(8,128)(2,1)}, bf16[512,2048]{1,0...) async-done(((bf16[2048,512]{1,0:T(8,128)(2,1)}, bf16[2048,512]{1,0:T(8,128)(2,1)}, bf16[2048,512]{1,0:T(8,128)(2,1)}, ...) | async-done | bytes 25690128 | tf_op jit(solution)/shard_map/psum | solution.py:325
  (369 shorter events, 439.3 us)
Async XLA Ops:
  7.2 70.3 %copy-start = (bf16[512,2048]{1,0:T(8,128)(2,1)S(1)}, bf16[512,2048]{1,0:T(8,128)(2,1)}, u32[]{:S(2)}) copy-start(bf16[512,2048]{1,0:T(8,128)(2,1)} %param.31) | copy-start | bytes 6291460
  7.2 52.0 %copy-start.71 = (f32[2048]{0:T(1024)S(1)}, f32[2048]{0:T(1024)}, u32[]{:S(2)}) copy-start(f32[2048]{0:T(1024)} %param.24) | copy-start | bytes 24580
  7.2 49.4 %all-gather.3.cloned.1.call-start = ((), (), s32[]{:S(2)}) async-start(), calls=%async_computation.6 | async-start | bytes 3932160 | tf_op jit(solution)/shard_map/all_gather | solution.py:142
  8.0 160.5 %all-reduce.9.cloned.1.call-start = ((), (), s32[]{:S(2)}) async-start(), calls=%async_computation.7 | async-start | bytes 6291456 | tf_op jit(solution)/shard_map/psum | solution.py:164
  99.7 81.2 %copy-start.47 = (s32[4096]{0:T(1024)}, s32[4096]{0:T(1024)S(1)}, u32[]{:S(2)}) copy-start(s32[4096]{0:T(1024)S(1)} %pad_clamp_fusion.1) | copy-start | bytes 49156
  99.7 75.4 %copy-start.51 = (f32[2048]{0:T(1024)S(1)}, f32[2048]{0:T(1024)}, u32[]{:S(2)}) copy-start(f32[2048]{0:T(1024)} %param.32) | copy-start | bytes 24580
  212.7 347.0 %copy-start.40 = (bf16[1,2048,352]{1,2,0:T(8,128)(2,1)S(1)}, bf16[1,2048,352]{1,2,0:T(8,128)(2,1)}, u32[]{:S(2)}) copy-start(bf16[1,2048,352]{1,2,0:T(8,128)(2,1)} %param.33) | copy-start | bytes 4325380
  592.0 347.0 %all-to-all-start.1 = ((bf16[8,480,2048]{2,1,0:T(8,128)(2,1)}), bf16[8,480,2048]{2,1,0:T(8,128)(2,1)}, u32[]{:S(2)}, u32[]{:S(2)}) async-start(bf16[8,480,2048]{2,1,0:T(8,128)(2,1)} %convolution_convert_fusion), calls=%async_computation.1 | async-start | bytes 31457280 | tf_op jit(solution)/shard_map/all_to_all | solution.py:197
  597.9 486.8 %reduce-scatter.3.cloned.1.call-start = ((), (), s32[]{:S(2)}) async-start(), calls=%async_computation.8 | async-start | bytes 3932160 | tf_op jit(solution)/shard_map/reduce_scatter | solution.py:207
  598.8 392.6 %copy-start.63 = (s32[1024]{0:T(1024)}, s32[1024]{0:T(1024)S(1)}, u32[]{:S(2)}) copy-start(s32[1024]{0:T(1024)S(1)} %get-tuple-element.99) | copy-start | bytes 12292
  598.8 409.7 %copy-start.61 = (s32[1024]{0:T(1024)}, s32[1024]{0:T(1024)S(1)}, u32[]{:S(2)}) copy-start(s32[1024]{0:T(1024)S(1)} %get-tuple-element.100) | copy-start | bytes 12292
  598.8 358.2 %copy-start.67 = (s32[1024]{0:T(1024)}, s32[1024]{0:T(1024)S(1)}, u32[]{:S(2)}) copy-start(s32[1024]{0:T(1024)S(1)} %get-tuple-element.97) | copy-start | bytes 12292
  598.9 375.3 %copy-start.65 = (s32[1024]{0:T(1024)}, s32[1024]{0:T(1024)S(1)}, u32[]{:S(2)}) copy-start(s32[1024]{0:T(1024)S(1)} %get-tuple-element.98) | copy-start | bytes 12292
  601.9 979.0 %copy-start.79 = (f32[768]{0:T(1024)}, f32[768]{0:T(1024)S(1)}, u32[]{:S(2)}) copy-start(f32[768]{0:T(1024)S(1)} %add_divide_fusion.2) | copy-start | bytes 9220
  1025.9 58.8 %copy-start.46 = (bf16[192,2048]{1,0:T(8,128)(2,1)S(1)}, bf16[192,2048]{1,0:T(8,128)(2,1)}, u32[]{:S(2)}) copy-start(bf16[192,2048]{1,0:T(8,128)(2,1)} %param.45) | copy-start | bytes 2359300
  1042.6 90.5 %all-gather.5.cloned.1.call-start = ((), (), s32[]{:S(2)}) async-start(), calls=%async_computation.9 | async-start | bytes 3932160 | tf_op jit(solution)/shard_map/all_gather | solution.py:217
  1177.7 346.9 %copy-start.82 = (bf16[1,352,2048]{2,1,0:T(8,128)(2,1)S(1)}, bf16[1,352,2048]{2,1,0:T(8,128)(2,1)}, u32[]{:S(2)}) copy-start(bf16[1,352,2048]{2,1,0:T(8,128)(2,1)} %param.35) | copy-start | bytes 4325380
  1575.2 346.8 %all-to-all-start.3 = ((bf16[8,480,2048]{2,1,0:T(8,128)(2,1)}), bf16[8,480,2048]{2,1,0:T(8,128)(2,1)}, u32[]{:S(2)}, u32[]{:S(2)}) async-start(bf16[8,480,2048]{2,1,0:T(8,128)(2,1)} %add_convert_fusion), calls=%async_computation.4 | async-start | bytes 31457280 | tf_op jit(solution)/shard_map/all_to_all | solution.py:254
  1580.8 529.8 %all-reduce.11.cloned.1.call-start = ((), (), s32[]{:S(2)}) async-start(), calls=%async_computation.10 | async-start | bytes 6291456 | tf_op jit(solution)/shard_map/psum | solution.py:261
  1604.4 335.5 %copy-start.68 = (s32[1024]{0:T(1024)S(1)}, s32[1024]{0:T(1024)}, u32[]{:S(2)}) copy-start(s32[1024]{0:T(1024)} %copy-done.67) | copy-start | bytes 12292
  2025.3 240.5 %reduce-scatter.5.cloned.1.call-start = ((), (), s32[]{:S(2)}) async-start(), calls=%async_computation.11 | async-start | bytes 3932160 | tf_op jit(solution)/shard_map/reduce_scatter | solution.py:305
  2025.4 85.3 %copy-start.52 = (f32[2048]{0:T(1024)S(1)}, f32[2048]{0:T(1024)}, u32[]{:S(2)}) copy-start(f32[2048]{0:T(1024)} %param.32) | copy-start | bytes 24580
  2025.4 85.2 %copy-start.55 = (f32[768]{0:T(1024)S(1)}, f32[768]{0:T(1024)}, u32[]{:S(2)}) copy-start(f32[768]{0:T(1024)} %copy-done.54) | copy-start | bytes 9220
  2157.3 555.1 %all-reduce.13.cloned.1.call-start = ((), (), s32[]{:S(2)}) async-start(), calls=%async_computation.12 | async-start | bytes 51380224 | tf_op jit(solution)/shard_map/psum | solution.py:325
  (94 other events, 806.7 us)
Sparse Core Ops, SparseCore 0:
  9.9 46.6 all-gather.2
  81.2 87.1 all-reduce.8
  1042.8 41.8 reduce-scatter.2
  1089.1 43.9 all-gather.4
  2025.4 85.2 all-reduce.10
  2157.4 43.9 reduce-scatter.4
  2206.0 506.3 all-reduce.12
where the time goes:
time: 2760 us; the launch traced here: 2750 us
  waiting for transfers between devices  1290 us (47%)
  blocking collectives  773 us (28%)
  matrix products  267 us (10%)
  local copies, waits for them, and re-layouts  256 us (9%)
  other arithmetic  137 us (5%)
    psum x1, waiting for transfers between devices, shards(): lax.psum(q_weight_grad.astype(jnp.bfloat16), 'dp').astype(jnp.float32)  402 us
    all_to_all x1, blocking collectives, shards(): lax.all_to_all(dispatched, 'dp', split_axis=0, concat_axis=0, tiled=True)  347 us
    all_to_all x1, blocking collectives, shards(): lax.all_to_all(grad_dispatched, 'dp', split_axis=0, concat_axis=0, tiled=...  347 us
    all_to_all x1, waiting for transfers between devices, shards(): lax.all_to_all(expert_result.astype(jnp.bfloat16), 'dp', split_axis=0, co...  320 us
    all_to_all x1, waiting for transfers between devices, shards(): lax.all_to_all(rows_grad.astype(jnp.bfloat16), 'dp', split_axis=0, concat...  318 us
    psum x1, waiting for transfers between devices, shards(): lax.psum(norm_two_part.astype(jnp.bfloat16), 'tensor').astype(jnp.float32)  71.6 us
    gather x4, local copies, waits for them, and re-layouts, shards(): norm_two_part = norm_two_part + grad_back_flat[slot_pairs[:, which]]  68.9 us
    gather x4, local copies, waits for them, and re-layouts, shards(): returned_flat[slot_pairs[:, which]]  68.8 us
  transfers between devices with their start and end apart: 9, of which 8 were waited for; matrix products, arithmetic and copies ran while one was open for 6% of the time, Pallas kernels for 0%

commit v1 on v0

v1 whole, which is shorter than its diff:
```python
import math

import jax
import jax.numpy as jnp
from jax import lax
from jax.sharding import PartitionSpec as P

D = 2048
HD = 128
PROMPT = 512
SLOT = 128
CONTS = 2
GROUP = 768


EPSILON = 1e-06
ROTARY_BASE = 1000000.0
WIDE = jnp.float32
NARROW = jnp.bfloat16


def slot_layout(lengths_row, position):
    offset = jnp.maximum(position - PROMPT, 0)
    in_prompt = position < PROMPT
    segment = jnp.where(in_prompt, 0, 1 + offset // SLOT)
    rotary_place = jnp.where(in_prompt, position, PROMPT + offset % SLOT)
    matches = segment[:, None] - 1 == jnp.arange(CONTS, dtype=jnp.int32)[None, :]
    length_here = jnp.sum(jnp.where(matches, lengths_row[None, :], 0), axis=1)
    living = in_prompt | (offset % SLOT < length_here)
    return (segment, rotary_place, living)


def visible_keys(position, segment, living):
    causal = position[None, :] <= position[:, None]
    same_part = (segment[None, :] == segment[:, None]) | (segment[None, :] == 0)
    return causal & same_part & living[None, :]


def rotary_tables(rotary_place):
    freqs = jnp.exp(jnp.arange(HD // 2, dtype=jnp.float32) * (-2.0 * math.log(ROTARY_BASE) / HD))
    angles = rotary_place.astype(jnp.float32)[:, None] * freqs[None, :]
    angles = jnp.concatenate([angles, angles], axis=1)
    return (jnp.cos(angles), jnp.sin(angles))


def rotate(values, cosine, sine):
    half = values.shape[-1] // 2
    flipped = jnp.concatenate([-values[..., half:], values[..., :half]], axis=-1)
    return values * cosine[:, None, :] + flipped * sine[:, None, :]


def rotate_back(grads, cosine, sine):
    half = grads.shape[-1] // 2
    turned = grads * sine[:, None, :]
    flipped = jnp.concatenate([turned[..., half:], -turned[..., :half]], axis=-1)
    return grads * cosine[:, None, :] + flipped


def attention_scores(query_low, key_low, visible, scale):
    scores = (
        jnp.einsum("thd,shd->hts", query_low, key_low, preferred_element_type=jnp.float32) * scale
    )
    return jnp.where(visible[None], scores, -1e30)


def dot_nt(left, right):
    return lax.dot_general(left, right, (((1,), (1,)), ((), ())), preferred_element_type=WIDE)


def dot_nn(left, right):
    return lax.dot_general(left, right, (((1,), (0,)), ((), ())), preferred_element_type=WIDE)


def dot_tn(left, right):
    return lax.dot_general(left, right, (((0,), (0,)), ((), ())), preferred_element_type=WIDE)


def after(value, *others):
    return lax.optimization_barrier((value,) + others)[0]


def flip(value, bit):
    size = lax.axis_size("tensor")
    return lax.ppermute(value, "tensor", [(i, i ^ bit) for i in range(size)])


def split_at(rows):
    return rows // 32 * 16


def plane_gather(value):
    size = lax.axis_size("tensor")
    if size == 4:
        cut = split_at(value.shape[0])
        one, two = flip(value, 1), flip(value, 2)
        low, high = flip(two[:cut], 1), flip(one[cut:], 2)
        return [value, one, two, jnp.concatenate([low, high], axis=0)]
    blocks, bit = [value], 1
    while bit < size:
        blocks = blocks + [flip(block, bit) for block in blocks]
        bit *= 2
    return blocks


def plane_scatter(parts):
    size = lax.axis_size("tensor")
    if size == 4:
        cut = split_at(parts[3].shape[0])
        far = parts[3].astype(NARROW)
        low, high = flip(far[:cut], 1), flip(far[cut:], 2)
        two = jnp.concatenate(
            [(parts[2][:cut].astype(WIDE) + low.astype(WIDE)).astype(NARROW), parts[2][cut:].astype(NARROW)], axis=0
        )
        one = jnp.concatenate(
            [parts[1][:cut].astype(NARROW), (parts[1][cut:].astype(WIDE) + high.astype(WIDE)).astype(NARROW)], axis=0
        )
        return parts[0].astype(WIDE) + flip(one, 1).astype(WIDE) + flip(two, 2).astype(WIDE)
    parts = [part.astype(WIDE) for part in parts]
    bit = size // 2
    while bit >= 1:
        parts = [parts[j] + flip(parts[bit + j].astype(NARROW), bit).astype(WIDE) for j in range(bit)]
        bit //= 2
    return parts[0]


def ring_order(chips):
    odd = list(range(1, chips, 2))
    even = list(range(2, chips, 2))
    return [0] + odd + even[::-1]


def ring_next(value):
    chips = lax.axis_size("dp") // 2
    order = ring_order(chips)
    pairs = [
        (2 * order[i] + c, 2 * order[(i + 1) % chips] + c) for i in range(chips) for c in range(2)
    ]
    return lax.ppermute(value, "dp", pairs)


def swap_core(value):
    size = lax.axis_size("dp")
    return lax.ppermute(value, "dp", [(i, i ^ 1) for i in range(size)])


def ring_sources():
    chips = lax.axis_size("dp") // 2
    order = ring_order(chips)
    index = lax.axis_index("dp")
    chip, core = index // 2, index % 2
    sources = []
    for step in range(chips):
        table = [0] * chips
        for place, here in enumerate(order):
            table[here] = order[(place - step) % chips]
        source = jnp.asarray(table, jnp.int32)[chip]
        sources.append((2 * source + core, 2 * source + 1 - core))
    return sources


def ring_gather(value):
    chips = lax.axis_size("dp") // 2
    held = [value]
    for _ in range(chips - 1):
        held.append(ring_next(held[-1]))
    return [(block, swap_core(block)) for block in held]


def ring_scatter(parts):
    chips = len(parts)
    total = None
    for step in list(range(1, chips)) + [0]:
        mine, other = parts[step]
        here = mine.astype(WIDE) + swap_core(other.astype(NARROW)).astype(WIDE)
        if total is not None:
            here = here + total.astype(WIDE)
        if step == 0:
            return here
        total = ring_next(here.astype(NARROW))


def shards(
    hidden_in,
    attn_gain,
    q_weight,
    q_bias,
    k_weight,
    k_bias,
    v_weight,
    v_bias,
    o_weight,
    mlp_gain,
    expert_gate,
    expert_up,
    expert_down,
    shared_gate,
    shared_up,
    shared_down,
    shared_router,
    routes,
    gate_weights,
    lengths,
    loss_mask,
    teacher,
    cotangent,
):
    wide = WIDE
    narrow = NARROW
    data_index = lax.axis_index("dp")
    slice_index = lax.axis_index("tensor")
    n_dp = lax.axis_size("dp")
    n_tensor = lax.axis_size("tensor")
    rows = hidden_in.shape[0]
    heads = q_weight.shape[1] // HD
    f_expert = expert_gate.shape[2]
    f_shared = shared_gate.shape[1] // n_dp
    scale = 1.0 / math.sqrt(HD)

    position = jnp.concatenate(
        [(slice_index ^ j) * rows + jnp.arange(rows, dtype=jnp.int32) for j in range(n_tensor)]
    )
    own_lengths = lax.dynamic_index_in_dim(lengths, data_index, 0, keepdims=False)
    segment, rotary_place, living = slot_layout(own_lengths, position)
    visible = visible_keys(position, segment, living)
    cosine, sine = rotary_tables(rotary_place)
    every = jnp.arange(GROUP, dtype=jnp.int32)
    living_all = jax.vmap(lambda row: slot_layout(row, every)[2])(lengths)
    valid_count = jnp.sum((living_all.reshape(-1) & (loss_mask == 1)).astype(wide))
    own_mask = lax.dynamic_slice_in_dim(loss_mask, data_index * GROUP + slice_index * rows, rows, 0)
    valid_own = living[:rows] & (own_mask == 1)

    own_routes = lax.dynamic_slice_in_dim(routes, slice_index * rows, rows, 0)
    own_gates = lax.dynamic_slice_in_dim(gate_weights, slice_index * rows, rows, 0)
    mixing = jnp.sum(
        jnp.where(
            own_routes[:, :, None] == jnp.arange(n_dp, dtype=jnp.int32)[None, None, :],
            own_gates[:, :, None],
            0.0,
        ),
        axis=1,
    )
    mixing_all = lax.all_gather(mixing.T, "dp", axis=0)
    mixing_here = lax.dynamic_index_in_dim(mixing_all, data_index, 1, keepdims=False)
    sources = ring_sources()
    mix_steps = [
        jnp.concatenate(
            [lax.dynamic_index_in_dim(mixing_here, s, 0, keepdims=False) for s in pair]
        )
        for pair in sources
    ]

    own_input = hidden_in.astype(wide)
    inverse_one = lax.rsqrt(jnp.mean(own_input * own_input, axis=1, keepdims=True) + EPSILON)
    hat_one = own_input * inverse_one
    normed_one_blocks = plane_gather((hat_one * attn_gain).astype(narrow))
    normed_one = jnp.concatenate(normed_one_blocks, axis=0)

    def pack(expert_rows, shared_rows):
        return jnp.concatenate([expert_rows, shared_rows], axis=0)

    shared_at = data_index * f_shared
    own_gate = pack(
        expert_gate[0].T, lax.dynamic_slice_in_dim(shared_gate, shared_at, f_shared, 1).T
    )
    own_up = pack(expert_up[0].T, lax.dynamic_slice_in_dim(shared_up, shared_at, f_shared, 1).T)
    own_down = pack(expert_down[0], lax.dynamic_slice_in_dim(shared_down, shared_at, f_shared, 0))

    def unpack(blocks):
        return jnp.concatenate(
            [block[:f_expert] for block in blocks] + [block[f_expert:] for block in blocks], axis=0
        )

    own_gate = after(own_gate, normed_one_blocks[-1])
    gate_blocks = plane_gather(own_gate)
    own_up = after(own_up, gate_blocks[-1])
    up_blocks = plane_gather(own_up)

    query_lin = dot_nn(normed_one, q_weight) + q_bias
    key_lin = dot_nn(normed_one, k_weight) + k_bias
    value_low = (dot_nn(normed_one, v_weight) + v_bias).astype(narrow).reshape(GROUP, heads, HD)
    query_low = rotate(query_lin.reshape(GROUP, heads, HD), cosine, sine).astype(narrow)
    key_low = rotate(key_lin.reshape(GROUP, heads, HD), cosine, sine).astype(narrow)
    scores = attention_scores(query_low, key_low, visible, scale)
    top_score = jnp.max(scores, axis=2, keepdims=True)
    expo = jnp.exp(scores - top_score)
    total_expo = jnp.sum(expo, axis=2, keepdims=True)
    log_total = top_score + jnp.log(total_expo)
    probs_low = (expo / total_expo).astype(narrow)
    mixed = jnp.einsum("hts,shd->thd", probs_low, value_low, preferred_element_type=wide)
    mixed_low = mixed.reshape(GROUP, heads * HD).astype(narrow)
    head_part = dot_nn(mixed_low, o_weight).astype(narrow)
    attn_own = plane_scatter([head_part[j * rows : (j + 1) * rows] for j in range(n_tensor)])

    hidden_mid = own_input + attn_own
    inverse_two = lax.rsqrt(jnp.mean(hidden_mid * hidden_mid, axis=1, keepdims=True) + EPSILON)
    hat_two = hidden_mid * inverse_two
    normed_two = (hat_two * mlp_gain).astype(narrow)

    own_down = after(own_down, up_blocks[-1])
    down_blocks = plane_gather(own_down)
    w_gate, w_up, w_down = unpack(gate_blocks), unpack(up_blocks), unpack(down_blocks)
    f_all = w_gate.shape[0]
    f_cut = f_expert * n_tensor

    router_wide = shared_router.astype(wide)
    x_steps, gate_steps, up_steps, hidden_steps, factor_steps, router_steps, out_steps = (
        [] for _ in range(7)
    )
    for step, pair in enumerate(ring_gather(normed_two)):
        x = jnp.concatenate(pair, axis=0)
        router_gate = jax.nn.sigmoid(jnp.sum(x.astype(wide) * router_wide, axis=1))
        gate_in = dot_nt(x, w_gate)
        up_in = dot_nt(x, w_up)
        is_expert = lax.broadcasted_iota(jnp.int32, (1, f_all), 1) < f_cut
        factor = jnp.where(is_expert, mix_steps[step][:, None], router_gate[:, None])
        hidden = (jax.nn.silu(gate_in) * up_in * factor).astype(narrow)
        out = dot_nn(hidden, w_down).astype(narrow)
        x_steps.append(x)
        gate_steps.append(gate_in)
        up_steps.append(up_in)
        hidden_steps.append(hidden)
        factor_steps.append(factor)
        router_steps.append(router_gate)
        out_steps.append((out[:rows], out[rows:]))
    branch_own = ring_scatter(out_steps)
    result = hidden_mid + branch_own

    difference = result - teacher.astype(wide)
    squared_own = jnp.sum(jnp.where(valid_own[:, None], difference * difference, 0.0))
    result_grad = cotangent.astype(wide) + jnp.where(
        valid_own[:, None], difference * (2.0 / (valid_count * D)), 0.0
    )
    grad_own = result_grad.astype(narrow)

    router_grad_part = jnp.zeros((D,), wide)
    g_steps, gate_grads, up_grads, dx_steps = ([] for _ in range(4))
    for step, pair in enumerate(ring_gather(grad_own)):
        g = jnp.concatenate(pair, axis=0)
        gate_in, up_in = gate_steps[step], up_steps[step]
        grad_plain = dot_nt(g, w_down)
        squash = jax.nn.sigmoid(gate_in)
        grad_hidden = grad_plain * factor_steps[step]
        gate_grad = (grad_hidden * up_in * squash * (1.0 + gate_in * (1.0 - squash))).astype(narrow)
        up_grad = (grad_hidden * gate_in * squash).astype(narrow)
        shared_cols = lax.broadcasted_iota(jnp.int32, (1, f_all), 1) >= f_cut
        logit_part = jnp.sum(
            jnp.where(shared_cols, grad_hidden * gate_in * squash * up_in, 0.0), axis=1
        ) * (1.0 - router_steps[step])
        dx = dot_nn(gate_grad, w_gate) + dot_nn(up_grad, w_up)
        dx = (dx + logit_part[:, None] * router_wide[None, :]).astype(narrow)
        router_grad_part = router_grad_part + jnp.sum(
            logit_part[:, None] * x_steps[step].astype(wide), axis=0
        )
        g_steps.append(g)
        gate_grads.append(gate_grad)
        up_grads.append(up_grad)
        dx_steps.append((dx[:rows], dx[rows:]))
    normed_two_grad = ring_scatter(dx_steps)

    x_all = jnp.concatenate(x_steps, axis=0)
    g_all = jnp.concatenate(g_steps, axis=0)
    down_full = dot_tn(jnp.concatenate(hidden_steps, axis=0), g_all).astype(narrow)
    gate_full = dot_tn(jnp.concatenate(gate_grads, axis=0), x_all).astype(narrow)
    up_full = dot_tn(jnp.concatenate(up_grads, axis=0), x_all).astype(narrow)

    def shared_sum(full):
        own = plane_scatter(
            [full[f_cut + j * f_shared : f_cut + (j + 1) * f_shared] for j in range(n_tensor)]
        ).astype(narrow)
        whole = jnp.zeros((n_dp * f_shared, D), narrow)
        for pair, at in zip(ring_gather(own), sources):
            for block, source in zip(pair, at):
                whole = lax.dynamic_update_slice_in_dim(whole, block, source * f_shared, 0)
        return whole

    def expert_sum(full):
        return plane_scatter([full[j * f_expert : (j + 1) * f_expert] for j in range(n_tensor)])

    shared_down_grad = shared_sum(down_full).astype(wide)
    shared_gate_grad = shared_sum(gate_full).T.astype(wide)
    shared_up_grad = shared_sum(up_full).T.astype(wide)

    grad_wide = grad_own.astype(wide)
    mlp_gain_part = jnp.sum(normed_two_grad * hat_two, axis=0)
    scaled_two = normed_two_grad * mlp_gain
    hidden_grad = grad_wide + inverse_two * (
        scaled_two - hat_two * jnp.mean(scaled_two * hat_two, axis=1, keepdims=True)
    )
    hidden_grad_low = jnp.concatenate(plane_gather(hidden_grad.astype(narrow)), axis=0)

    o_grad = dot_tn(hidden_grad_low, mixed_low)
    mixed_grad = dot_nt(hidden_grad_low, o_weight).astype(narrow).reshape(GROUP, heads, HD)
    scores_again = attention_scores(query_low, key_low, visible, scale)
    probs = jnp.exp(scores_again - log_total)
    probs_grad = jnp.einsum("thd,shd->hts", mixed_grad, value_low, preferred_element_type=wide)
    value_grad = jnp.einsum(
        "hts,thd->shd", probs.astype(narrow), mixed_grad, preferred_element_type=wide
    )
    inner = jnp.sum(probs * probs_grad, axis=2, keepdims=True)
    scores_grad = (probs * (probs_grad - inner)).astype(narrow)
    query_grad = (
        jnp.einsum("hts,shd->thd", scores_grad, key_low, preferred_element_type=wide) * scale
    )
    key_grad = (
        jnp.einsum("hts,thd->shd", scores_grad, query_low, preferred_element_type=wide) * scale
    )
    query_lin_grad = rotate_back(query_grad, cosine, sine).reshape(GROUP, heads * HD).astype(narrow)
    key_lin_grad = rotate_back(key_grad, cosine, sine).reshape(GROUP, heads * HD).astype(narrow)
    value_lin_grad = value_grad.reshape(GROUP, heads * HD).astype(narrow)
    norm_one_part = (
        dot_nt(query_lin_grad, q_weight)
        + dot_nt(key_lin_grad, k_weight)
        + dot_nt(value_lin_grad, v_weight)
    ).astype(narrow)
    normed_one_grad = plane_scatter(
        [norm_one_part[j * rows : (j + 1) * rows] for j in range(n_tensor)]
    )
    attn_gain_part = jnp.sum(normed_one_grad * hat_one, axis=0)
    scaled_one = normed_one_grad * attn_gain
    input_grad = hidden_grad + inverse_one * (
        scaled_one - hat_one * jnp.mean(scaled_one * hat_one, axis=1, keepdims=True)
    )

    width = heads * HD
    attn_grads = jnp.concatenate(
        [
            dot_tn(normed_one, query_lin_grad).astype(narrow),
            dot_tn(normed_one, key_lin_grad).astype(narrow),
            dot_tn(normed_one, value_lin_grad).astype(narrow),
            o_grad.astype(narrow),
        ],
        axis=1,
    )
    piece = D // n_dp
    attn_sum = ring_scatter(
        [
            tuple(lax.dynamic_slice_in_dim(attn_grads, s * piece, piece, 0) for s in pair)
            for pair in sources
        ]
    ).astype(narrow)
    attn_whole = jnp.zeros((D, 4 * width), narrow)
    for pair, at in zip(ring_gather(attn_sum), sources):
        for block, source in zip(pair, at):
            attn_whole = lax.dynamic_update_slice_in_dim(attn_whole, block, source * piece, 0)
    attn_whole = attn_whole.astype(wide)

    expert_down_grad = expert_sum(down_full)[None]
    expert_gate_grad = expert_sum(gate_full).T[None]
    expert_up_grad = expert_sum(up_full).T[None]

    bias_part = jnp.concatenate(
        [
            jnp.sum(query_lin_grad.astype(wide), axis=0),
            jnp.sum(key_lin_grad.astype(wide), axis=0),
            jnp.sum(value_lin_grad.astype(wide), axis=0),
        ]
    )
    bias_spread = lax.dynamic_update_slice_in_dim(
        jnp.zeros((n_tensor, 3 * width), wide), bias_part[None], slice_index, 0
    )
    small = lax.psum(
        jnp.concatenate(
            [
                attn_gain_part,
                mlp_gain_part,
                router_grad_part,
                jnp.broadcast_to(squared_own, (128,)),
                bias_spread.reshape(-1),
            ]
        ),
        ("dp", "tensor"),
    )
    attn_gain_grad, mlp_gain_grad, shared_router_grad = (small[i * D : (i + 1) * D] for i in range(3))
    teacher_loss = small[3 * D] / (valid_count * D)
    biases = lax.dynamic_index_in_dim(
        small[3 * D + 128 :].reshape(n_tensor, 3 * width), slice_index, 0, keepdims=False
    )
    return (
        result.astype(narrow),
        teacher_loss,
        input_grad,
        attn_gain_grad,
        attn_whole[:, :width],
        biases[:width],
        attn_whole[:, width : 2 * width],
        biases[width : 2 * width],
        attn_whole[:, 2 * width : 3 * width],
        biases[2 * width :],
        attn_whole[:, 3 * width :].T,
        mlp_gain_grad,
        expert_gate_grad,
        expert_up_grad,
        expert_down_grad,
        shared_gate_grad,
        shared_up_grad,
        shared_down_grad,
        shared_router_grad,
    )


def solution(mesh):
    return jax.shard_map(
        shards,
        mesh=mesh,
        in_specs=(
            P(("dp", "tensor"), None),
            P(),
            P(None, "tensor"),
            P("tensor"),
            P(None, "tensor"),
            P("tensor"),
            P(None, "tensor"),
            P("tensor"),
            P("tensor", None),
            P(),
            P("dp", None, "tensor"),
            P("dp", None, "tensor"),
            P("dp", "tensor", None),
            P(None, "tensor"),
            P(None, "tensor"),
            P("tensor", None),
            P(),
            P("dp", None),
            P("dp", None),
            P(),
            P(),
            P(("dp", "tensor"), None),
            P(("dp", "tensor"), None),
        ),
        out_specs=(
            P(("dp", "tensor"), None),
            P(),
            P(("dp", "tensor"), None),
            P(),
            P(None, "tensor"),
            P("tensor"),
            P(None, "tensor"),
            P("tensor"),
            P(None, "tensor"),
            P("tensor"),
            P("tensor", None),
            P(),
            P("dp", None, "tensor"),
            P("dp", None, "tensor"),
            P("dp", "tensor", None),
            P(None, "tensor"),
            P(None, "tensor"),
            P("tensor", None),
            P(),
        ),
        check_vma=False,
    )
```

time: 2760 us -> 1310 us (0.47)
  waiting for transfers between devices: 1290 us -> 535 us
  blocking collectives: 773 us -> 55.9 us
  starting transfers between devices: 11.8 us -> 101 us
  local copies, waits for them, and re-layouts: 256 us -> 174 us
    all_to_all x2 -> x0, blocking collectives: 694 us -> none  [the longest x1 347 us: shards(): lax.all_to_all(dispatched, 'dp', split_axis=0, concat_axis=0, tiled=True)]
    all_to_all x2 -> x0, waiting for transfers between devices: 638 us -> none  [the longest x1 320 us: shards(): lax.all_to_all(expert_result.astype(jnp.bfloat16), 'dp', split_axis=0, co...]
    psum x3 -> x0, waiting for transfers between devices: 542 us -> none  [the longest x1 402 us: shards(): lax.psum(q_weight_grad.astype(jnp.bfloat16), 'dp').astype(jnp.float32)]
    ppermute x0 -> x115, waiting for transfers between devices: none -> 535 us  [the longest x27 304 us: ring_next(): return lax.ppermute(value, 'dp', pairs)]
    gather x11 -> x0, local copies, waits for them, and re-layouts: 222 us -> none  [the longest x4 68.9 us: shards(): norm_two_part = norm_two_part + grad_back_flat[slot_pairs[:, which]]]
    ppermute x0 -> x115, starting transfers between devices: none -> 101 us  [the longest x52 58.9 us: flip(): return lax.ppermute(value, 'tensor', [(i, i ^ bit) for i in range(size)])]
    unnamed x221 -> x358, local copies, waits for them, and re-layouts: 13.9 us -> 86.6 us
    all_gather x2 -> x0, waiting for transfers between devices: 67.3 us -> none  [the longest x1 43.9 us: shards(): group_rows = lax.all_gather(hidden_in, 'tensor', axis=0, tiled=True)]
  transfers between devices with their start and end apart: 9 -> 115, of which waited for: 8 -> 52; matrix products, arithmetic and copies ran while one was open for 6% -> 29% of each run, Pallas kernels for 0% -> 0%
where the time goes in v1:
time: 1310 us; the launch traced here: 1300 us
  waiting for transfers between devices  535 us (41%)
  matrix products  278 us (21%)
  local copies, waits for them, and re-layouts  174 us (13%)
  other arithmetic  149 us (11%)
  starting transfers between devices  101 us (8%)
  blocking collectives  55.9 us (4%)
    ppermute x27, waiting for transfers between devices, ring_next(): return lax.ppermute(value, 'dp', pairs)  304 us
    ppermute x52, waiting for transfers between devices, flip(): return lax.ppermute(value, 'tensor', [(i, i ^ bit) for i in range(size)])  230 us
    dot_general x16, matrix products, dot_nt(): lax.dot_general(left, right, (((1,), (1,)), ((), ())), preferred_element_...  127 us
    unnamed x358, local copies, waits for them, and re-layouts  86.6 us
    dot_general x7, matrix products, dot_tn(): lax.dot_general(left, right, (((0,), (0,)), ((), ())), preferred_element_...  67.9 us
    dot_general x16, matrix products, dot_nn(): lax.dot_general(left, right, (((1,), (0,)), ((), ())), preferred_element_...  66.6 us
    ppermute x52, starting transfers between devices, flip(): return lax.ppermute(value, 'tensor', [(i, i ^ bit) for i in range(size)])  58.9 us
    psum x1, blocking collectives, shards(): lax.psum(jnp.concatenate([attn_gain_part, mlp_gain_part, router_grad_part...  40.2 us
  transfers between devices with their start and end apart: 115, of which 52 were waited for; matrix products, arithmetic and copies ran while one was open for 29% of the time, Pallas kernels for 0%

profile of v1, /device:TPU:0, one launch (start us, length us, event | category | flops | bytes accessed | tf_op | source)
XLA Modules:
  0.0 1301.3 jit_solution(5591573528902026615)
XLA Ops:
  29.0 15.7 %all-gather = f32[64,192]{1,0:T(8,128)} all-gather(f32[8,192]{1,0:T(8,128)S(1)} %bitcast.182), channel_id=2, replica_groups=mesh['dp'=8,'tensor'=4] {'dp'}, dimensions={0}, use_global_device_ids=true | all-gather | bytes 55296 | tf_op jit(solution)/shard_map/all_gather | solution.py:242
  59.8 20.9 %collective-permute-done.2 = bf16[96,2048]{1,0:T(8,128)(2,1)S(1)} collective-permute-done((bf16[96,2048]{1,0:T(8,128)(2,1)S(1)}, bf16[96,2048]{1,0:T(8,128)(2,1)S(1)}, u32[]{:S(2)}, u32[]{:S(2)}) %collective-permute-start.2) | collective-permute-done | bytes 393248 | tf_op jit(solution)/shard_map/ppermute | solution.py:84
  142.5 16.3 %collective-permute-done.22 = bf16[192,2048]{1,0:T(8,128)(2,1)S(1)} collective-permute-done((bf16[192,2048]{1,0:T(8,128)(2,1)S(1)}, bf16[192,2048]{1,0:T(8,128)(2,1)S(1)}, u32[]{:S(2)}, u32[]{:S(2)}) %collective-permute-start.22) | collective-permute-done | bytes 786464 | tf_op jit(solution)/shard_map/ppermute | solution.py:138
  263.4 16.4 %fusion.27 = (bf16[384,2112]{0,1:T(8,128)(2,1)}, bf16[384,2112]{0,1:T(8,128)(2,1)}, bf16[384,2112]{0,1:T(8,128)(2,1)}, bf16[384,2112]{0,1:T(8,128)(2,1)}, f32[384,2112]{0,1:T(8,128)}) fusion(f32[384,2112]{0,1:T(8,128)} %fusion.96, f32[384]{0:T(512)S(1)} %add_divide_fusion.7, f32[384]{0:T(512)S(1)} %copy-done.123, pred[2112]{0:T(1024)(128)(4,1)S(1)} %copy-done.119, ...), kind=kOutput, calls=%fused_computation.57 | convolution fusion | flops 3350986752 | bytes 42678336 | tf_op jit(solution)/shard_map/dot_general | solution.py:67
  279.7 27.8 %collective-permute-done.17 = bf16[528,2048]{1,0:T(8,128)(2,1)S(1)} collective-permute-done((bf16[528,2048]{1,0:T(8,128)(2,1)S(1)}, bf16[528,2048]{1,0:T(8,128)(2,1)S(1)}, u32[]{:S(2)}, u32[]{:S(2)}) %collective-permute-start.17) | collective-permute-done | bytes 2162720 | tf_op jit(solution)/shard_map/ppermute | solution.py:84
  313.9 18.9 %collective-permute-done.19 = bf16[256,2048]{1,0:T(8,128)(2,1)S(1)} collective-permute-done((bf16[256,2048]{1,0:T(8,128)(2,1)S(1)}, bf16[256,2048]{1,0:T(8,128)(2,1)S(1)}, u32[]{:S(2)}, u32[]{:S(2)}) %collective-permute-start.19) | collective-permute-done | bytes 1048608 | tf_op jit(solution)/shard_map/ppermute | solution.py:84
  350.7 13.2 %collective-permute-done.31 = bf16[192,2048]{1,0:T(8,128)(2,1)S(1)} collective-permute-done((bf16[192,2048]{1,0:T(8,128)(2,1)S(1)}, bf16[192,2048]{1,0:T(8,128)(2,1)S(1)}, u32[]{:S(2)}, u32[]{:S(2)}) %collective-permute-start.31) | collective-permute-done | bytes 786464 | tf_op jit(solution)/shard_map/ppermute | solution.py:138
  389.5 15.1 %collective-permute-done.33 = bf16[192,2048]{1,0:T(8,128)(2,1)} collective-permute-done((bf16[192,2048]{1,0:T(8,128)(2,1)}, bf16[192,2048]{1,0:T(8,128)(2,1)}, u32[]{:S(2)}, u32[]{:S(2)}) %collective-permute-start.33) | collective-permute-done | bytes 786464 | tf_op jit(solution)/shard_map/ppermute | solution.py:138
  474.5 26.1 %select_reduce_fusion.3 = (f32[384]{0:T(512)S(1)}, f32[384]{0:T(512)S(1)}, f32[384]{0:T(512)}, f32[384]{0:T(512)}, bf16[384,2112]{0,1:T(8,128)(2,1)}, /*index=5*...) fusion(f32[384,2112]{0,1:T(8,128)} %get-tuple-element.229, ...), kind=kOutput, calls=%fused_computation.70 | convolution fusion | flops 3378558976 | bytes 58897536 | tf_op jit(solution)/shard_map/dot_general | solution.py:67
  500.6 19.9 %convolution_convert_fusion.2 = bf16[2112,2048]{1,0:T(8,128)(2,1)} fusion(bf16[1536,2048]{1,0:T(8,128)(2,1)} %get-tuple-element.185, bf16[384,2112]{0,1:T(8,128)(2,1)} %get-tuple-element.119, bf16[384,2112]{0,1:T(8,128)(2,1)} %get-tuple-element.120, bf16[384,2112]{0,1:T(8,128)(2,1)} %get-tuple-element.121, bf16[384,2112]{0,1:T(8,128)(2,1)} %get-tuple-element.118), kind=kOutput, calls=%fused_computation.4 | convolution fusion | flops 13317832704 | bytes 21430272 | tf_op jit(solution)/shard_map/dot_general | solution.py:75
  548.9 19.7 %convolution_convert_fusion.1 = bf16[2112,2048]{1,0:T(8,128)(2,1)} fusion(bf16[1536,2048]{1,0:T(8,128)(2,1)} %get-tuple-element.185, bf16[384,2112]{0,1:T(8,128)(2,1)} %get-tuple-element.159, bf16[384,2112]{0,1:T(8,128)(2,1)} %get-tuple-element.160, bf16[384,2112]{0,1:T(8,128)(2,1)} %get-tuple-element.161, bf16[384,2112]{0,1:T(8,128)(2,1)} %get-tuple-element.162), kind=kOutput, calls=%fused_computation.3 | convolution fusion | flops 13317832704 | bytes 21430272 | tf_op jit(solution)/shard_map/dot_general | solution.py:75
  573.7 19.7 %convolution_convert_fusion = bf16[2112,2048]{1,0:T(8,128)(2,1)} fusion(bf16[1536,2048]{1,0:T(8,128)(2,1)} %constant_dynamic-update-slice_fusion.29, bf16[384,2112]{0,1:T(8,128)(2,1)} %get-tuple-element.224, bf16[384,2112]{0,1:T(8,128)(2,1)} %get-tuple-element.225, bf16[384,2112]{0,1:T(8,128)(2,1)} %get-tuple-element.226, ...), kind=kOutput, calls=%fused_computation.2 | convolution fusion | flops 13317832704 | bytes 21430272 | tf_op jit(solution)/shard_map/dot_general | solution.py:75
  788.4 16.2 %collective-permute-done.46 = bf16[192,2048]{1,0:T(8,128)(2,1)S(1)} collective-permute-done((bf16[192,2048]{1,0:T(8,128)(2,1)S(1)}, bf16[192,2048]{1,0:T(8,128)(2,1)S(1)}, u32[]{:S(2)}, u32[]{:S(2)}) %collective-permute-start.46) | collective-permute-done | bytes 786464 | tf_op jit(solution)/shard_map/ppermute | solution.py:138
  820.6 14.9 %collective-permute-done.100 = bf16[176,2048]{1,0:T(8,128)(2,1)S(1)} collective-permute-done((bf16[176,2048]{1,0:T(8,128)(2,1)S(1)}, bf16[176,2048]{1,0:T(8,128)(2,1)S(1)}, u32[]{:S(2)}, u32[]{:S(2)}) %collective-permute-start.100) | collective-permute-done | bytes 720928 | tf_op jit(solution)/shard_map/ppermute | solution.py:138
  837.6 13.3 %collective-permute-done.111 = bf16[176,2048]{1,0:T(8,128)(2,1)S(1)} collective-permute-done((bf16[176,2048]{1,0:T(8,128)(2,1)S(1)}, bf16[176,2048]{1,0:T(8,128)(2,1)S(1)}, u32[]{:S(2)}, u32[]{:S(2)}) %collective-permute-start.111) | collective-permute-done | bytes 720928 | tf_op jit(solution)/shard_map/ppermute | solution.py:138
  851.6 16.2 %collective-permute-done.47 = bf16[192,2048]{1,0:T(8,128)(2,1)S(1)} collective-permute-done((bf16[192,2048]{1,0:T(8,128)(2,1)S(1)}, bf16[192,2048]{1,0:T(8,128)(2,1)S(1)}, u32[]{:S(2)}, u32[]{:S(2)}) %collective-permute-start.47) | collective-permute-done | bytes 786464 | tf_op jit(solution)/shard_map/ppermute | solution.py:138
  884.9 13.9 %collective-permute-done.102 = bf16[176,2048]{1,0:T(8,128)(2,1)} collective-permute-done((bf16[176,2048]{1,0:T(8,128)(2,1)S(1)}, bf16[176,2048]{1,0:T(8,128)(2,1)}, u32[]{:S(2)}, u32[]{:S(2)}) %collective-permute-start.102) | collective-permute-done | bytes 720928 | tf_op jit(solution)/shard_map/ppermute | solution.py:138
  923.3 27.1 %collective-permute-done.49 = bf16[192,2048]{1,0:T(8,128)(2,1)S(1)} collective-permute-done((bf16[192,2048]{1,0:T(8,128)(2,1)S(1)}, bf16[192,2048]{1,0:T(8,128)(2,1)S(1)}, u32[]{:S(2)}, u32[]{:S(2)}) %collective-permute-start.49) | collective-permute-done | bytes 786464 | tf_op jit(solution)/shard_map/ppermute | solution.py:84
  960.9 27.1 %collective-permute-done.51 = bf16[96,2048]{1,0:T(8,128)(2,1)S(1)} collective-permute-done((bf16[96,2048]{1,0:T(8,128)(2,1)S(1)}, bf16[96,2048]{1,0:T(8,128)(2,1)S(1)}, u32[]{:S(2)}, u32[]{:S(2)}) %collective-permute-start.51) | collective-permute-done | bytes 393248 | tf_op jit(solution)/shard_map/ppermute | solution.py:84
  1055.0 13.7 %collective-permute-done.60 = bf16[256,2048]{0,1:T(8,128)(2,1)} collective-permute-done((bf16[256,2048]{0,1:T(8,128)(2,1)}, bf16[256,2048]{0,1:T(8,128)(2,1)}, u32[]{:S(2)}, u32[]{:S(2)}) %collective-permute-start.60) | collective-permute-done | bytes 1048608 | tf_op jit(solution)/shard_map/ppermute | solution.py:138
  1080.1 17.4 %collective-permute-done.61 = bf16[256,2048]{0,1:T(8,128)(2,1)} collective-permute-done((bf16[256,2048]{0,1:T(8,128)(2,1)}, bf16[256,2048]{0,1:T(8,128)(2,1)}, u32[]{:S(2)}, u32[]{:S(2)}) %collective-permute-start.61) | collective-permute-done | bytes 1048608 | tf_op jit(solution)/shard_map/ppermute | solution.py:138
  1106.0 20.4 %collective-permute-done.62 = bf16[256,2048]{0,1:T(8,128)(2,1)S(1)} collective-permute-done((bf16[256,2048]{0,1:T(8,128)(2,1)S(1)}, bf16[256,2048]{0,1:T(8,128)(2,1)S(1)}, u32[]{:S(2)}, u32[]{:S(2)}) %collective-permute-start.62) | collective-permute-done | bytes 1048608 | tf_op jit(solution)/shard_map/ppermute | solution.py:138
  1180.4 40.2 %psum.7 = f32[12416]{0:T(1024)S(1)} all-reduce(f32[12416]{0:T(1024)S(1)} %constant_dynamic-update-slice_fusion.69), channel_id=1, replica_groups=mesh['dp'=8,'tensor'=4] {'dp','tensor'}, use_global_device_ids=true, to_apply=%region_28.29 | all-reduce | flops 12416 | bytes 99328 | tf_op jit(solution)/shard_map/psum | solution.py:461
  1231.9 16.4 %collective-permute-done.68 = bf16[256,2048]{0,1:T(8,128)(2,1)} collective-permute-done((bf16[256,2048]{0,1:T(8,128)(2,1)}, bf16[256,2048]{0,1:T(8,128)(2,1)}, u32[]{:S(2)}, u32[]{:S(2)}) %collective-permute-start.68) | collective-permute-done | bytes 1048608 | tf_op jit(solution)/shard_map/ppermute | solution.py:138
  (824 shorter events, 826.5 us)
Async XLA Ops:
  5.3 49.5 %collective-permute-start = (bf16[192,2048]{1,0:T(8,128)(2,1)}, bf16[192,2048]{1,0:T(8,128)(2,1)}, u32[]{:S(2)}, u32[]{:S(2)}) collective-permute-start(bf16[192,2048]{1,0:T(8,128)(2,1)} %get-tuple-element.117), channel_id=1, source_target_pairs={{0,1},{1,0},{2,3},{3,2},{4,5},{5,4},{6,7},{7,6},{8,9},{9,8},{10,11... | collective-permute-start | bytes 2359304 | tf_op jit(solution)/shard_map/ppermute | solution.py:84
  19.1 102.6 %collective-permute-start.9 = (bf16[528,2048]{1,0:T(8,128)(2,1)}, bf16[528,2048]{1,0:T(8,128)(2,1)}, u32[]{:S(2)}, u32[]{:S(2)}) collective-permute-start(bf16[528,2048]{1,0:T(8,128)(2,1)} %pad_maximum_fusion.1), channel_id=1, source_target_pairs={{0,1},{1,0},{2,3},{3,2},{4,5},{5,4},{6,7},{7,6},{8,9},{9,8},{10,11... | collective-permute-start | bytes 6488072 | tf_op jit(solution)/shard_map/ppermute | solution.py:84
  19.6 99.3 %collective-permute-start.10 = (bf16[528,2048]{1,0:T(8,128)(2,1)}, bf16[528,2048]{1,0:T(8,128)(2,1)}, u32[]{:S(2)}, u32[]{:S(2)}) collective-permute-start(bf16[528,2048]{1,0:T(8,128)(2,1)} %pad_maximum_fusion.1), channel_id=1, source_target_pairs={{0,2},{1,3},{2,0},{3,1},{4,6},{5,7},{6,4},{7,5},{8,10},{9,11},{10,... | collective-permute-start | bytes 6488072 | tf_op jit(solution)/shard_map/ppermute | solution.py:84
  162.7 52.0 %collective-permute-start.13 = (bf16[528,2048]{1,0:T(8,128)(2,1)S(1)}, bf16[528,2048]{1,0:T(8,128)(2,1)S(1)}, u32[]{:S(2)}, u32[]{:S(2)}) collective-permute-start(bf16[528,2048]{1,0:T(8,128)(2,1)S(1)} %pad_maximum_fusion.2), channel_id=1, source_target_pairs={{0,1},{1,0},{2,3},{3,2},{4,5},{5,4},{6,7},{7,6},{8,9},{9,8},{10,11... | collective-permute-start | bytes 6488072 | tf_op jit(solution)/shard_map/ppermute | solution.py:84
  163.4 48.9 %collective-permute-start.14 = (bf16[528,2048]{1,0:T(8,128)(2,1)S(1)}, bf16[528,2048]{1,0:T(8,128)(2,1)S(1)}, u32[]{:S(2)}, u32[]{:S(2)}) collective-permute-start(bf16[528,2048]{1,0:T(8,128)(2,1)S(1)} %pad_maximum_fusion.2), channel_id=1, source_target_pairs={{0,2},{1,3},{2,0},{3,1},{4,6},{5,7},{6,4},{7,5},{8,10},{9,11},{10,... | collective-permute-start | bytes 6488072 | tf_op jit(solution)/shard_map/ppermute | solution.py:84
  261.8 48.5 %collective-permute-start.18 = (bf16[528,2048]{1,0:T(8,128)(2,1)S(1)}, bf16[528,2048]{1,0:T(8,128)(2,1)}, u32[]{:S(2)}, u32[]{:S(2)}) collective-permute-start(bf16[528,2048]{1,0:T(8,128)(2,1)S(1)} %pad_maximum_fusion.3), channel_id=1, source_target_pairs={{0,2},{1,3},{2,0},{3,1},{4,6},{5,7},{6,4},{7,5},{8,10},{9,11},{10,... | collective-permute-start | bytes 6488072 | tf_op jit(solution)/shard_map/ppermute | solution.py:84
  602.9 60.6 %collective-permute-start.44 = (bf16[192,2048]{1,0:T(8,128)(2,1)S(1)}, bf16[192,2048]{1,0:T(8,128)(2,1)S(1)}, u32[]{:S(2)}, u32[]{:S(2)}) collective-permute-start(bf16[192,2048]{1,0:T(8,128)(2,1)S(1)} %slice.645), channel_id=1, source_target_pairs={{0,4},{4,0},{8,12},{12,8},{16,20},{20,16},{24,28},{28,24},{1,5},{5... | collective-permute-start | bytes 2359304 | tf_op jit(solution)/shard_map/ppermute | solution.py:143
  609.9 101.7 %collective-permute-start.42 = (bf16[192,2048]{1,0:T(8,128)(2,1)}, bf16[192,2048]{1,0:T(8,128)(2,1)}, u32[]{:S(2)}, u32[]{:S(2)}) collective-permute-start(bf16[192,2048]{1,0:T(8,128)(2,1)} %slice.643), channel_id=1, source_target_pairs={{0,4},{4,0},{8,12},{12,8},{16,20},{20,16},{24,28},{28,24},{1,5},{5... | collective-permute-start | bytes 2359304 | tf_op jit(solution)/shard_map/ppermute | solution.py:143
  691.6 96.7 %collective-permute-start.40 = (bf16[192,2048]{1,0:T(8,128)(2,1)}, bf16[192,2048]{1,0:T(8,128)(2,1)}, u32[]{:S(2)}, u32[]{:S(2)}) collective-permute-start(bf16[192,2048]{1,0:T(8,128)(2,1)} %slice.641), channel_id=1, source_target_pairs={{0,4},{4,0},{8,12},{12,8},{16,20},{20,16},{24,28},{28,24},{1,5},{5... | collective-permute-start | bytes 2359304 | tf_op jit(solution)/shard_map/ppermute | solution.py:143
  711.6 139.4 %collective-permute-start.35 = (bf16[192,2048]{1,0:T(8,128)(2,1)}, bf16[192,2048]{1,0:T(8,128)(2,1)S(1)}, u32[]{:S(2)}, u32[]{:S(2)}) collective-permute-start(bf16[192,2048]{1,0:T(8,128)(2,1)} %slice.639), channel_id=1, source_target_pairs={{0,4},{4,0},{8,12},{12,8},{16,20},{20,16},{24,28},{28,24},{1,5},{5... | collective-permute-start | bytes 2359304 | tf_op jit(solution)/shard_map/ppermute | solution.py:143
  820.0 47.8 %collective-permute-start.47 = (bf16[192,2048]{1,0:T(8,128)(2,1)S(1)}, bf16[192,2048]{1,0:T(8,128)(2,1)S(1)}, u32[]{:S(2)}, u32[]{:S(2)}) collective-permute-start(bf16[192,2048]{1,0:T(8,128)(2,1)S(1)} %add_convert_fusion.9), channel_id=1, source_target_pairs={{0,8},{4,12},{8,24},{12,28},{24,16},{28,20},{16,0},{20,4},{1,9},{5... | collective-permute-start | bytes 2359304 | tf_op jit(solution)/shard_map/ppermute | solution.py:138
  835.5 80.2 %collective-permute-start.73 = (bf16[352,2048]{1,0:T(8,128)(2,1)}, bf16[352,2048]{1,0:T(8,128)(2,1)S(1)}, u32[]{:S(2)}, u32[]{:S(2)}) collective-permute-start(bf16[352,2048]{1,0:T(8,128)(2,1)} %pad_maximum_fusion.7), channel_id=1, source_target_pairs={{0,2},{1,3},{2,0},{3,1},{4,6},{5,7},{6,4},{7,5},{8,10},{9,11},{10,... | collective-permute-start | bytes 4325384 | tf_op jit(solution)/shard_map/ppermute | solution.py:84
  836.2 80.8 %collective-permute-start.71 = (bf16[352,2048]{1,0:T(8,128)(2,1)S(1)}, bf16[352,2048]{1,0:T(8,128)(2,1)S(1)}, u32[]{:S(2)}, u32[]{:S(2)}) collective-permute-start(bf16[352,2048]{1,0:T(8,128)(2,1)S(1)} %pad_maximum_fusion.6), channel_id=1, source_target_pairs={{0,1},{1,0},{2,3},{3,2},{4,5},{5,4},{6,7},{7,6},{8,9},{9,8},{10,11... | collective-permute-start | bytes 4325384 | tf_op jit(solution)/shard_map/ppermute | solution.py:84
  898.8 130.1 %collective-permute-start.77 = (bf16[352,2048]{1,0:T(8,128)(2,1)}, bf16[352,2048]{1,0:T(8,128)(2,1)}, u32[]{:S(2)}, u32[]{:S(2)}) collective-permute-start(bf16[352,2048]{1,0:T(8,128)(2,1)} %pad_maximum_fusion.9), channel_id=1, source_target_pairs={{0,2},{1,3},{2,0},{3,1},{4,6},{5,7},{6,4},{7,5},{8,10},{9,11},{10,... | collective-permute-start | bytes 4325384 | tf_op jit(solution)/shard_map/ppermute | solution.py:84
  900.6 51.2 %collective-permute-start.48 = (bf16[192,2048]{1,0:T(8,128)(2,1)S(1)}, bf16[192,2048]{1,0:T(8,128)(2,1)S(1)}, u32[]{:S(2)}, u32[]{:S(2)}) collective-permute-start(bf16[192,2048]{1,0:T(8,128)(2,1)S(1)} %get-tuple-element.110), channel_id=1, source_target_pairs={{0,1},{1,0},{2,3},{3,2},{4,5},{5,4},{6,7},{7,6},{8,9},{9,8},{10,11... | collective-permute-start | bytes 2359304 | tf_op jit(solution)/shard_map/ppermute | solution.py:84
  915.7 113.7 %collective-permute-start.75 = (bf16[352,2048]{1,0:T(8,128)(2,1)}, bf16[352,2048]{1,0:T(8,128)(2,1)}, u32[]{:S(2)}, u32[]{:S(2)}) collective-permute-start(bf16[352,2048]{1,0:T(8,128)(2,1)} %pad_maximum_fusion.8), channel_id=1, source_target_pairs={{0,1},{1,0},{2,3},{3,2},{4,5},{5,4},{6,7},{7,6},{8,9},{9,8},{10,11... | collective-permute-start | bytes 4325384 | tf_op jit(solution)/shard_map/ppermute | solution.py:84
  918.1 116.1 %collective-permute-start.81 = (bf16[352,2048]{1,0:T(8,128)(2,1)}, bf16[352,2048]{1,0:T(8,128)(2,1)}, u32[]{:S(2)}, u32[]{:S(2)}) collective-permute-start(bf16[352,2048]{1,0:T(8,128)(2,1)} %pad_maximum_fusion.11), channel_id=1, source_target_pairs={{0,2},{1,3},{2,0},{3,1},{4,6},{5,7},{6,4},{7,5},{8,10},{9,11},{10,... | collective-permute-start | bytes 4325384 | tf_op jit(solution)/shard_map/ppermute | solution.py:84
  959.4 75.3 %collective-permute-start.79 = (bf16[352,2048]{1,0:T(8,128)(2,1)}, bf16[352,2048]{1,0:T(8,128)(2,1)}, u32[]{:S(2)}, u32[]{:S(2)}) collective-permute-start(bf16[352,2048]{1,0:T(8,128)(2,1)} %pad_maximum_fusion.10), channel_id=1, source_target_pairs={{0,1},{1,0},{2,3},{3,2},{4,5},{5,4},{6,7},{7,6},{8,9},{9,8},{10,11... | collective-permute-start | bytes 4325384 | tf_op jit(solution)/shard_map/ppermute | solution.py:84
  988.0 51.3 %collective-permute-start.92 = (bf16[176,2048]{1,0:T(8,128)(2,1)}, bf16[176,2048]{1,0:T(8,128)(2,1)}, u32[]{:S(2)}, u32[]{:S(2)}) collective-permute-start(bf16[176,2048]{1,0:T(8,128)(2,1)} %collective-permute-done.91), channel_id=1, source_target_pairs={{0,4},{4,0},{8,12},{12,8},{16,20},{20,16},{24,28},{28,24},{1,5},{5... | collective-permute-start | bytes 2162696 | tf_op jit(solution)/shard_map/ppermute | solution.py:143
  1028.9 70.7 %collective-permute-start.103 = (bf16[176,2048]{1,0:T(8,128)(2,1)}, bf16[176,2048]{1,0:T(8,128)(2,1)}, u32[]{:S(2)}, u32[]{:S(2)}) collective-permute-start(bf16[176,2048]{1,0:T(8,128)(2,1)} %collective-permute-done.102), channel_id=1, source_target_pairs={{0,4},{4,0},{8,12},{12,8},{16,20},{20,16},{24,28},{28,24},{1,5},{5... | collective-permute-start | bytes 2162696 | tf_op jit(solution)/shard_map/ppermute | solution.py:143
  1034.2 128.6 %collective-permute-start.114 = (bf16[176,2048]{1,0:T(8,128)(2,1)}, bf16[176,2048]{1,0:T(8,128)(2,1)}, u32[]{:S(2)}, u32[]{:S(2)}) collective-permute-start(bf16[176,2048]{1,0:T(8,128)(2,1)} %collective-permute-done.113), channel_id=1, source_target_pairs={{0,4},{4,0},{8,12},{12,8},{16,20},{20,16},{24,28},{28,24},{1,5},{5... | collective-permute-start | bytes 2162696 | tf_op jit(solution)/shard_map/ppermute | solution.py:143
  1102.8 74.4 %collective-permute-start.55 = (bf16[192,2048]{1,0:T(8,128)(2,1)}, bf16[192,2048]{1,0:T(8,128)(2,1)}, u32[]{:S(2)}, u32[]{:S(2)}) collective-permute-start(bf16[192,2048]{1,0:T(8,128)(2,1)} %pad_maximum_fusion.15), channel_id=1, source_target_pairs={{0,2},{1,3},{2,0},{3,1},{4,6},{5,7},{6,4},{7,5},{8,10},{9,11},{10,... | collective-permute-start | bytes 2359304 | tf_op jit(solution)/shard_map/ppermute | solution.py:84
  1105.0 72.3 %collective-permute-start.53 = (bf16[192,2048]{1,0:T(8,128)(2,1)}, bf16[192,2048]{1,0:T(8,128)(2,1)}, u32[]{:S(2)}, u32[]{:S(2)}) collective-permute-start(bf16[192,2048]{1,0:T(8,128)(2,1)} %pad_maximum_fusion.14), channel_id=1, source_target_pairs={{0,1},{1,0},{2,3},{3,2},{4,5},{5,4},{6,7},{7,6},{8,9},{9,8},{10,11... | collective-permute-start | bytes 2359304 | tf_op jit(solution)/shard_map/ppermute | solution.py:84
  1173.8 47.5 %collective-permute-start.66 = (bf16[256,2048]{0,1:T(8,128)(2,1)}, bf16[256,2048]{0,1:T(8,128)(2,1)}, u32[]{:S(2)}, u32[]{:S(2)}) collective-permute-start(bf16[256,2048]{0,1:T(8,128)(2,1)} %collective-permute-done.64), channel_id=1, source_target_pairs={{0,8},{4,12},{8,24},{12,28},{24,16},{28,20},{16,0},{20,4},{1,9},{5... | collective-permute-start | bytes 3145736 | tf_op jit(solution)/shard_map/ppermute | solution.py:138
  (246 other events, 4612.4 us)

commit v2 on v1

--- a/solution.py
+++ b/solution.py
@@ -1,8 +1,11 @@
+import functools
 import math
 
 import jax
 import jax.numpy as jnp
 from jax import lax
+from jax.experimental import pallas as pl
+from jax.experimental.pallas import tpu as pltpu
 from jax.sharding import PartitionSpec as P
 
 D = 2048
@@ -17,6 +20,7 @@
 ROTARY_BASE = 1000000.0
 WIDE = jnp.float32
 NARROW = jnp.bfloat16
+VMEM_BYTES = 60 * 1024 * 1024
 
 
 def slot_layout(lengths_row, position):
@@ -143,19 +147,22 @@
     return lax.ppermute(value, "dp", [(i, i ^ 1) for i in range(size)])
 
 
-def ring_sources():
+def ring_chips():
     chips = lax.axis_size("dp") // 2
     order = ring_order(chips)
-    index = lax.axis_index("dp")
-    chip, core = index // 2, index % 2
+    chip = lax.axis_index("dp") // 2
     sources = []
     for step in range(chips):
         table = [0] * chips
         for place, here in enumerate(order):
             table[here] = order[(place - step) % chips]
-        source = jnp.asarray(table, jnp.int32)[chip]
-        sources.append((2 * source + core, 2 * source + 1 - core))
+        sources.append(jnp.asarray(table, jnp.int32)[chip])
     return sources
+
+
+def ring_sources():
+    core = lax.axis_index("dp") % 2
+    return [(2 * chip + core, 2 * chip + 1 - core) for chip in ring_chips()]
 
 
 def ring_gather(value):
@@ -177,6 +184,394 @@
         if step == 0:
             return here
         total = ring_next(here.astype(NARROW))
+
+
+def plane_bits():
+    size = lax.axis_size("tensor")
+    bits = [1 << i for i in range(size.bit_length() - 1)]
+    return bits[:1] + bits[2:], bits[1:2]
+
+
+def bits_gather(value, bits):
+    blocks = [value]
+    for bit in bits:
+        blocks = blocks + [flip(block, bit) for block in blocks]
+    return blocks
+
+
+def bits_scatter(parts, bits):
+    for bit in bits[::-1]:
+        half = len(parts) // 2
+        parts = [
+            parts[j].astype(WIDE) + flip(parts[half + j].astype(NARROW), bit).astype(WIDE)
+            for j in range(half)
+        ]
+    return parts[0]
+
+
+def bits_offsets(bits):
+    offsets = [0]
+    for bit in bits:
+        offsets = offsets + [offset ^ bit for offset in offsets]
+    return offsets
+
+
+def chain_gather(value):
+    held = [value]
+    for _ in range(lax.axis_size("dp") // 2 - 1):
+        held.append(ring_next(held[-1]))
+    return held
+
+
+def chain_scatter(parts):
+    total = None
+    for step in list(range(1, len(parts))) + [0]:
+        here = parts[step].astype(WIDE)
+        if total is not None:
+            here = here + total.astype(WIDE)
+        if step == 0:
+            return here
+        total = ring_next(here.astype(NARROW))
+
+
+def sum_over_dp(vector):
+    both = vector + swap_core(vector)
+    chips = lax.axis_size("dp") // 2
+    held = [both]
+    for _ in range(chips - 1):
+        held.append(ring_next(held[-1]))
+    stacked = jnp.stack(held)
+    places = jnp.stack(ring_chips())
+    ordered = [
+        jnp.sum(jnp.where((places == chip)[:, None], stacked, 0.0), axis=0) for chip in range(chips)
+    ]
+    return sum(ordered[1:], ordered[0])
+
+
+def sum_over_plane(vector):
+    bit = 1
+    while bit < lax.axis_size("tensor"):
+        vector = vector + flip(vector, bit)
+        bit *= 2
+    return vector
+
+
+class Copies:
+    def __init__(self, sems):
+        self.sems, self.used = sems, 0
+
+    def start(self, source, target):
+        copy = pltpu.make_async_copy(source, target, self.sems.at[self.used])
+        self.used += 1
+        copy.start()
+        return copy
+
+
+def weight_places(parts, count, cut):
+    half = count // 2
+    left = parts - cut
+    chunks = [
+        [(b, 0, cut, b * cut) for b in range(half)],
+        [(b, 0, cut, (b - half) * cut) for b in range(half, count)],
+        [(b, cut, left, b * left) for b in range(count)],
+    ]
+    sizes = [half * cut, half * cut, count * left]
+    starts = [0, half * cut, count * cut]
+    return [
+        (start, size, [(b, at, n, start + place) for b, at, n, place in chunk])
+        for start, size, chunk in zip(starts, sizes, chunks)
+    ]
+
+
+def forward_body(rows, count, places, blocks, *refs):
+    x_refs, refs = refs[:count], refs[count:]
+    weights, refs = [refs[n * blocks : (n + 1) * blocks] for n in range(3)], refs[3 * blocks :]
+    mix_one, mix_two, router = refs[:3]
+    out_refs, refs = refs[3 : 3 + count], refs[3 + count :]
+    gate_ref, up_ref, hidden_ref, factor_ref = refs[:4]
+    xs, gate_s, up_s, down_s, ys, gs, us, hs, sems = refs[4:]
+    copies = Copies(sems)
+    x_in = [copies.start(x_refs[i], xs.at[pl.ds(i * rows, rows)]) for i in range(count)]
+    w_in = [
+        [
+            [
+                copies.start(weights[n][b].at[pl.ds(at, size)], held.at[pl.ds(place, size)])
+                for b, at, size, place in pieces
+            ]
+            for n, held in enumerate((gate_s, up_s, down_s))
+        ]
+        for _, _, pieces in places
+    ]
+    for copy in x_in:
+        copy.wait()
+    x = xs[...]
+    router_gate = jax.nn.sigmoid(jnp.sum(x.astype(WIDE) * router[...], axis=1, keepdims=True))
+    factor_ref[...] = router_gate
+    total, away = None, []
+    for (start, size, _), arriving, factor in zip(
+        places, w_in, (mix_one[...], mix_two[...], router_gate)
+    ):
+        span = pl.ds(start, size)
+        for copy in arriving[0]:
+            copy.wait()
+        gate_in = dot_nt(x, gate_s[span])
+        for copy in arriving[1]:
+            copy.wait()
+        up_in = dot_nt(x, up_s[span])
+        hidden = (gate_in * jax.nn.sigmoid(gate_in) * up_in * factor).astype(NARROW)
+        gs[:, start : start + size] = gate_in.astype(NARROW)
+        us[:, start : start + size] = up_in.astype(NARROW)
+        hs[:, start : start + size] = hidden
+        for copy in arriving[2]:
+            copy.wait()
+        part = dot_nn(hidden, down_s[span])
+        total = part if total is None else total + part
+    ys[...] = total.astype(NARROW)
+    away = [copies.start(ys.at[pl.ds(i * rows, rows)], out_refs[i]) for i in range(count)]
+    away += [copies.start(gs, gate_ref), copies.start(us, up_ref), copies.start(hs, hidden_ref)]
+    for copy in away:
+        copy.wait()
+
+
+def forward_step(x_blocks, weights, mix_one, mix_two, router, cut):
+    count, (rows, width) = len(x_blocks), x_blocks[0].shape
+    blocks, parts = len(weights[0]), weights[0][0].shape[0]
+    places = weight_places(parts, blocks, cut)
+    total, hidden = count * rows, blocks * parts
+    anywhere, local = pl.BlockSpec(memory_space=pl.ANY), pl.BlockSpec(memory_space=pltpu.VMEM)
+    shape = jax.ShapeDtypeStruct
+    outs = pl.pallas_call(
+        functools.partial(forward_body, rows, count, places, blocks),
+        out_shape=[shape((rows, width), NARROW)] * count
+        + [shape((total, hidden), NARROW)] * 3
+        + [shape((total, 1), WIDE)],
+        in_specs=[anywhere] * (count + 3 * blocks) + [local] * 3,
+        out_specs=[anywhere] * (count + 3) + [local],
+        scratch_shapes=[pltpu.VMEM((total, width), NARROW)]
+        + [pltpu.VMEM((hidden, width), NARROW)] * 3
+        + [pltpu.VMEM((total, width), NARROW)]
+        + [pltpu.VMEM((total, hidden), NARROW)] * 3
+        + [pltpu.SemaphoreType.DMA((2 * count + 6 * blocks + 3,))],
+        compiler_params=pltpu.CompilerParams(vmem_limit_bytes=VMEM_BYTES),
+        cost_estimate=pl.CostEstimate(
+            flops=6 * total * hidden * width,
+            bytes_accessed=6 * hidden * width + 4 * total * width + 6 * total * hidden,
+            transcendentals=total * hidden,
+        ),
+        name="ffn_forward",
+    )(*x_blocks, *[w for held in weights for w in held], mix_one, mix_two, router)
+    return outs[:count], outs[count], outs[count + 1], outs[count + 2], outs[count + 3]
+
+
+def backward_body(rows, count, places, blocks, *refs):
+    g_refs, refs = refs[:count], refs[count:]
+    weights, refs = [refs[n * blocks : (n + 1) * blocks] for n in range(3)], refs[3 * blocks :]
+    (gate_ref, up_ref, mix_one, mix_two, rg, router), refs = refs[:6], refs[6:]
+    out_refs, refs = refs[:count], refs[count:]
+    gate_out, up_out, logit_ref = refs[:3]
+    xs, gate_s, up_s, down_s, ys, gs, us, sems = refs[3:]
+    copies = Copies(sems)
+    g_in = [copies.start(g_refs[i], xs.at[pl.ds(i * rows, rows)]) for i in range(count)]
+    w_in, kept = [], []
+    for start, size, pieces in places:
+        arriving = [
+            [
+                copies.start(weights[n][b].at[pl.ds(at, n_rows)], held.at[pl.ds(place, n_rows)])
+                for b, at, n_rows, place in pieces
+            ]
+            for n, held in ((2, down_s), (0, gate_s), (1, up_s))
+        ]
+        w_in.append(arriving)
+        if not kept:
+            kept = [copies.start(gate_ref, gs), copies.start(up_ref, us)]
+    for copy in g_in:
+        copy.wait()
+    grad = xs[...]
+    total = None
+    for (start, size, _), arriving, factor in zip(
+        places, w_in, (mix_one[...], mix_two[...], rg[...])
+    ):
+        span = pl.ds(start, size)
+        for copy in arriving[0]:
+            copy.wait()
+        grad_hidden = dot_nt(grad, down_s[span]) * factor
+        if total is None:
+            for copy in kept:
+                copy.wait()
+        gate_in = gs[:, start : start + size].astype(WIDE)
+        up_in = us[:, start : start + size].astype(WIDE)
+        squash = jax.nn.sigmoid(gate_in)
+        up_grad = grad_hidden * gate_in * squash
+        gate_grad = grad_hidden * up_in * squash * (1.0 + gate_in * (1.0 - squash))
+        logit = jnp.sum(up_grad * up_in, axis=1, keepdims=True)
+        gate_grad, up_grad = gate_grad.astype(NARROW), up_grad.astype(NARROW)
+        gs[:, start : start + size] = gate_grad
+        us[:, start : start + size] = up_grad
+        for copy in arriving[1] + arriving[2]:
+            copy.wait()
+        part = dot_nn(gate_grad, gate_s[span]) + dot_nn(up_grad, up_s[span])
+        total = part if total is None else total + part
+    logit = logit * (1.0 - rg[...])
+    logit_ref[...] = logit
+    ys[...] = (total + logit * router[...]).astype(NARROW)
+    away = [copies.start(ys.at[pl.ds(i * rows, rows)], out_refs[i]) for i in range(count)]
+    away += [copies.start(gs, gate_out), copies.start(us, up_out)]
+    for copy in away:
+        copy.wait()
+
+
+def backward_step(g_blocks, weights, gate_in, up_in, mix_one, mix_two, rg, router, cut):
+    count, (rows, width) = len(g_blocks), g_blocks[0].shape
+    blocks, parts = len(weights[0]), weights[0][0].shape[0]
+    places = weight_places(parts, blocks, cut)
+    total, hidden = count * rows, blocks * parts
+    anywhere, local = pl.BlockSpec(memory_space=pl.ANY), pl.BlockSpec(memory_space=pltpu.VMEM)
+    shape = jax.ShapeDtypeStruct
+    outs = pl.pallas_call(
+        functools.partial(backward_body, rows, count, places, blocks),
+        out_shape=[shape((rows, width), NARROW)] * count
+        + [shape((total, hidden), NARROW)] * 2
+        + [shape((total, 1), WIDE)],
+        in_specs=[anywhere] * (count + 3 * blocks + 2) + [local] * 4,
+        out_specs=[anywhere] * (count + 2) + [local],
+        scratch_shapes=[pltpu.VMEM((total, width), NARROW)]
+        + [pltpu.VMEM((hidden, width), NARROW)] * 3
+        + [pltpu.VMEM((total, width), NARROW)]
+        + [pltpu.VMEM((total, hidden), NARROW)] * 2
+        + [pltpu.SemaphoreType.DMA((2 * count + 6 * blocks + 4,))],
+        compiler_params=pltpu.CompilerParams(vmem_limit_bytes=VMEM_BYTES),
+        cost_estimate=pl.CostEstimate(
+            flops=6 * total * hidden * width,
+            bytes_accessed=6 * hidden * width + 4 * total * width + 8 * total * hidden,
+            transcendentals=total * hidden,
+        ),
+        name="ffn_backward",
+    )(
+        *g_blocks,
+        *[w for held in weights for w in held],
+        gate_in,
+        up_in,
+        mix_one,
+        mix_two,
+        rg,
+        router,
+    )
+    return outs[:count], outs[count], outs[count + 1], outs[count + 2]
+
+
+def weight_body(rows, steps, blocks, places, tiles, parts, *refs):
+    x_refs, refs = refs[: steps * blocks], refs[steps * blocks :]
+    left_refs, refs = refs[:steps], refs[steps:]
+    mine_ref, other_ref, xs, ls, os, sems = refs
+    copies = Copies(sems)
+    part = blocks * rows
+    arrived = []
+    for s in range(steps):
+        for i in range(blocks):
+            place = pl.ds((s * blocks + i) * rows, rows)
+            arrived.append(copies.start(x_refs[s * blocks + i], xs.at[place]))
+        arrived.append(copies.start(left_refs[s], ls.at[pl.ds(s * part, part)]))
+    for copy in arrived:
+        copy.wait()
+    moves = [
+        (place, n_rows, b, at)
+        for _, _, chunk in places
+        for b, at, n_rows, place in chunk
+    ]
+    half = (1 + max(b for _, _, b, _ in moves)) // 2
+    away, ready = [], 0
+    for start, size in tiles:
+        os[pl.ds(start, size)] = dot_tn(ls[:, start : start + size], xs[...]).astype(NARROW)
+        for at, n_rows, b, offset in moves:
+            if ready < at + n_rows <= start + size:
+                target = mine_ref if b < half else other_ref
+                goal = target.at[pl.ds((b % half) * parts + offset, n_rows)]
+                away.append(copies.start(os.at[pl.ds(at, n_rows)], goal))
+        ready = start + size
+    for copy in away:
+        copy.wait()
+
+
+def weight_grads(x_blocks, lefts, parts, cut, blocks_of):
+    steps, blocks = len(x_blocks), len(x_blocks[0])
+    rows, width = x_blocks[0][0].shape
+    total, hidden = steps * blocks * rows, lefts[0].shape[1]
+    places = weight_places(parts, blocks_of, cut)
+    tiles = [(at, min(512, hidden - at)) for at in range(0, hidden, 512)]
+    anywhere = pl.BlockSpec(memory_space=pl.ANY)
+    return pl.pallas_call(
+        functools.partial(weight_body, rows, steps, blocks, places, tiles, parts),
+        out_shape=[jax.ShapeDtypeStruct((hidden // 2, width), NARROW)] * 2,
+        in_specs=[anywhere] * (steps * (blocks + 1)),
+        out_specs=[anywhere] * 2,
+        scratch_shapes=[
+            pltpu.VMEM((total, width), NARROW),
+            pltpu.VMEM((total, hidden), NARROW),
+            pltpu.VMEM((hidden, width), NARROW),
+            pltpu.SemaphoreType.DMA((steps * (blocks + 1) + 2 * blocks_of,)),
+        ],
+        compiler_params=pltpu.CompilerParams(vmem_limit_bytes=VMEM_BYTES),
+        cost_estimate=pl.CostEstimate(
+            flops=2 * total * hidden * width,
+            bytes_accessed=2 * total * width + 2 * (total + width) * hidden,
+            transcendentals=0,
+        ),
+        name="weight_grads",
+    )(*[b for step in x_blocks for b in step], *lefts)
+
+
+def assemble_body(count, splits, *refs):
+    places, blocks, outs = refs[0], refs[1 : 1 + count], refs[1 + count : 1 + count + splits]
+    held, sems = refs[1 + count + splits :]
+    rows = blocks[0].shape[0]
+    copies = Copies(sems)
+    moved = []
+    for i in range(count):
+        place = pl.multiple_of(places[i], rows)
+        moved.append(copies.start(blocks[i], held.at[pl.ds(place, rows)]))
+    for copy in moved:
+        copy.wait()
+    width = held.shape[1] // splits
+    for j in range(splits):
+        outs[j][...] = held[:, j * width : (j + 1) * width].astype(WIDE)
+
+
+def assemble(blocks, places, splits):
+    count, (rows, width) = len(blocks), blocks[0].shape
+    shape = jax.ShapeDtypeStruct((count * rows, width // splits), WIDE)
+    local = pl.BlockSpec(memory_space=pltpu.VMEM)
+    return pl.pallas_call(
+        functools.partial(assemble_body, count, splits),
+        out_shape=[shape] * splits,
+        in_specs=[pl.BlockSpec(memory_space=pltpu.SMEM)]
+        + [pl.BlockSpec(memory_space=pl.ANY)] * count,
+        out_specs=[local] * splits,
+        scratch_shapes=[
+            pltpu.VMEM((count * rows, width), NARROW),
+            pltpu.SemaphoreType.DMA((count,)),
+        ],
+        compiler_params=pltpu.CompilerParams(vmem_limit_bytes=VMEM_BYTES),
+        name="assemble",
+    )(places, *blocks)
+
+
+def turn_body(x_ref, out_ref):
+    out_ref[...] = x_ref[...].astype(WIDE).T
+
+
+def turn(value):
+    rows, width = value.shape
+    if rows % 128:
+        return value.T.astype(WIDE)
+    return pl.pallas_call(
+        turn_body,
+        grid=(width // 256,),
+        out_shape=jax.ShapeDtypeStruct((width, rows), WIDE),
+        in_specs=[pl.BlockSpec((rows, 256), lambda i: (0, i))],
+        out_specs=pl.BlockSpec((256, rows), lambda i: (i, 0)),
+        compiler_params=pltpu.CompilerParams(vmem_limit_bytes=VMEM_BYTES),
+        name="turn",
+    )(value)
 
 
 def shards(
@@ -214,6 +609,7 @@
     heads = q_weight.shape[1] // HD
     f_expert = expert_gate.shape[2]
     f_shared = shared_gate.shape[1] // n_dp
+    f_pad = -(-f_shared // 16) * 16
     scale = 1.0 / math.sqrt(HD)
 
     position = jnp.concatenate(
@@ -229,26 +625,6 @@
     own_mask = lax.dynamic_slice_in_dim(loss_mask, data_index * GROUP + slice_index * rows, rows, 0)
     valid_own = living[:rows] & (own_mask == 1)
 
-    own_routes = lax.dynamic_slice_in_dim(routes, slice_index * rows, rows, 0)
-    own_gates = lax.dynamic_slice_in_dim(gate_weights, slice_index * rows, rows, 0)
-    mixing = jnp.sum(
-        jnp.where(
-            own_routes[:, :, None] == jnp.arange(n_dp, dtype=jnp.int32)[None, None, :],
-            own_gates[:, :, None],
-            0.0,
-        ),
-        axis=1,
-    )
-    mixing_all = lax.all_gather(mixing.T, "dp", axis=0)
-    mixing_here = lax.dynamic_index_in_dim(mixing_all, data_index, 1, keepdims=False)
-    sources = ring_sources()
-    mix_steps = [
-        jnp.concatenate(
-            [lax.dynamic_index_in_dim(mixing_here, s, 0, keepdims=False) for s in pair]
-        )
-        for pair in sources
-    ]
-
     own_input = hidden_in.astype(wide)
     inverse_one = lax.rsqrt(jnp.mean(own_input * own_input, axis=1, keepdims=True) + EPSILON)
     hat_one = own_input * inverse_one
@@ -256,6 +632,8 @@
     normed_one = jnp.concatenate(normed_one_blocks, axis=0)
 
     def pack(expert_rows, shared_rows):
+        if f_pad != f_shared:
+            shared_rows = jnp.pad(shared_rows, ((0, f_pad - f_shared), (0, 0)))
         return jnp.concatenate([expert_rows, shared_rows], axis=0)
 
     shared_at = data_index * f_shared
@@ -265,15 +643,40 @@
     own_up = pack(expert_up[0].T, lax.dynamic_slice_in_dim(shared_up, shared_at, f_shared, 1).T)
     own_down = pack(expert_down[0], lax.dynamic_slice_in_dim(shared_down, shared_at, f_shared, 0))
 
-    def unpack(blocks):
-        return jnp.concatenate(
-            [block[:f_expert] for block in blocks] + [block[f_expert:] for block in blocks], axis=0
+    w_bits, r_bits = plane_bits()
+
+    def both_cores(blocks):
+        return blocks + [swap_core(block) for block in blocks]
+
+    own_gate, own_up, normed_one = lax.optimization_barrier((own_gate, own_up, normed_one))
+    gate_blocks = bits_gather(own_gate, w_bits)
+    up_blocks = bits_gather(own_up, w_bits)
+
+    row_slices = [slice_index ^ offset for offset in bits_offsets(r_bits)]
+    mixing = jnp.sum(
+        jnp.where(
+            routes[None, :, :] == jnp.arange(n_dp, dtype=jnp.int32)[:, None, None],
+            gate_weights[None, :, :],
+            0.0,
+        ),
+        axis=2,
+    )
+    mixing = after(mixing, normed_one_blocks[-1])
+    mixing_all = jnp.stack(chain_gather(mixing))
+    experts = jnp.arange(n_dp, dtype=jnp.int32)
+    slices = jnp.arange(n_tensor, dtype=jnp.int32)
+
+    def mixing_of(expert):
+        chosen = jnp.sum(
+            jnp.where((experts == expert)[None, :, None], mixing_all, 0.0), axis=1
+        ).reshape(-1, n_tensor, rows)
+        chosen = jnp.stack(
+            [jnp.sum(jnp.where((slices == at)[None, :, None], chosen, 0.0), axis=1) for at in row_slices],
+            axis=1,
         )
-
-    own_gate = after(own_gate, normed_one_blocks[-1])
-    gate_blocks = plane_gather(own_gate)
-    own_up = after(own_up, gate_blocks[-1])
-    up_blocks = plane_gather(own_up)
+        return chosen.reshape(-1, len(row_slices) * rows, 1)
+
+    mix_one, mix_two = mixing_of(data_index), mixing_of(data_index ^ 1)
 
     query_lin = dot_nn(normed_one, q_weight) + q_bias
     key_lin = dot_nn(normed_one, k_weight) + k_bias
@@ -288,41 +691,55 @@
     probs_low = (expo / total_expo).astype(narrow)
     mixed = jnp.einsum("hts,shd->thd", probs_low, value_low, preferred_element_type=wide)
     mixed_low = mixed.reshape(GROUP, heads * HD).astype(narrow)
+    mixed_low = after(mixed_low, *gate_blocks, *up_blocks)
     head_part = dot_nn(mixed_low, o_weight).astype(narrow)
     attn_own = plane_scatter([head_part[j * rows : (j + 1) * rows] for j in range(n_tensor)])
 
+    attn_own, own_down = lax.optimization_barrier((attn_own, own_down))
+    down_blocks = bits_gather(own_down, w_bits)
     hidden_mid = own_input + attn_own
     inverse_two = lax.rsqrt(jnp.mean(hidden_mid * hidden_mid, axis=1, keepdims=True) + EPSILON)
     hat_two = hidden_mid * inverse_two
     normed_two = (hat_two * mlp_gain).astype(narrow)
 
-    own_down = after(own_down, up_blocks[-1])
-    down_blocks = plane_gather(own_down)
-    w_gate, w_up, w_down = unpack(gate_blocks), unpack(up_blocks), unpack(down_blocks)
-    f_all = w_gate.shape[0]
-    f_cut = f_expert * n_tensor
-
-    router_wide = shared_router.astype(wide)
-    x_steps, gate_steps, up_steps, hidden_steps, factor_steps, router_steps, out_steps = (
-        [] for _ in range(7)
-    )
-    for step, pair in enumerate(ring_gather(normed_two)):
-        x = jnp.concatenate(pair, axis=0)
-        router_gate = jax.nn.sigmoid(jnp.sum(x.astype(wide) * router_wide, axis=1))
-        gate_in = dot_nt(x, w_gate)
-        up_in = dot_nt(x, w_up)
-        is_expert = lax.broadcasted_iota(jnp.int32, (1, f_all), 1) < f_cut
-        factor = jnp.where(is_expert, mix_steps[step][:, None], router_gate[:, None])
-        hidden = (jax.nn.silu(gate_in) * up_in * factor).astype(narrow)
-        out = dot_nn(hidden, w_down).astype(narrow)
-        x_steps.append(x)
-        gate_steps.append(gate_in)
-        up_steps.append(up_in)
-        hidden_steps.append(hidden)
-        factor_steps.append(factor)
-        router_steps.append(router_gate)
-        out_steps.append((out[:rows], out[rows:]))
-    branch_own = ring_scatter(out_steps)
+    weights = [both_cores(blocks) for blocks in (gate_blocks, up_blocks, down_blocks)]
+    n_blocks, n_hidden = len(weights[0]), len(weights[0]) // 2
+    places = weight_places(f_expert + f_shared, n_blocks, f_expert)
+
+    router_row = shared_router.astype(wide)[None]
+    x_chain = chain_gather(normed_two)
+    chips = len(x_chain)
+    x_steps = [bits_gather(block, r_bits) for block in x_chain]
+    forward, out_sums, total = {}, {}, None
+    order = list(range(1, chips)) + [0]
+    for place, step in enumerate(order):
+        x, ready = x_steps[step], []
+        if place == 0:
+            ready = [x_chain[order[1]], *x_steps[0]]
+        if place >= 1:
+            ready = list(forward[order[place - 1]][0])
+            ready += x_steps[order[min(place + 1, chips - 1)]]
+        if place >= 2:
+            done = order[place - 2]
+            out_sums[done] = bits_scatter(forward[done][0], r_bits)
+            ready.append(out_sums[done])
+            if total is not None:
+                ready.append(total)
+        x = list(lax.optimization_barrier((*x, *ready)))
+        if place >= 2:
+            kept = x[len(x) - (2 if total is not None else 1) :]
+            here = kept[0].astype(wide)
+            if total is not None:
+                here = here + kept[1].astype(wide)
+            total = ring_next(here.astype(narrow))
+        x = x[: len(x_steps[step])]
+        forward[step] = forward_step(
+            x, weights, mix_one[step], mix_two[step], router_row, f_expert
+        )
+    for done in order[-2:]:
+        out_sums[done] = bits_scatter(forward[done][0], r_bits)
+    total = ring_next((out_sums[order[-2]].astype(wide) + total.astype(wide)).astype(narrow))
+    branch_own = out_sums[0].astype(wide) + total.astype(wide)
     result = hidden_mid + branch_own
 
     difference = result - teacher.astype(wide)
@@ -332,53 +749,81 @@
     )
     grad_own = result_grad.astype(narrow)
 
-    router_grad_part = jnp.zeros((D,), wide)
-    g_steps, gate_grads, up_grads, dx_steps = ([] for _ in range(4))
-    for step, pair in enumerate(ring_gather(grad_own)):
-        g = jnp.concatenate(pair, axis=0)
-        gate_in, up_in = gate_steps[step], up_steps[step]
-        grad_plain = dot_nt(g, w_down)
-        squash = jax.nn.sigmoid(gate_in)
-        grad_hidden = grad_plain * factor_steps[step]
-        gate_grad = (grad_hidden * up_in * squash * (1.0 + gate_in * (1.0 - squash))).astype(narrow)
-        up_grad = (grad_hidden * gate_in * squash).astype(narrow)
-        shared_cols = lax.broadcasted_iota(jnp.int32, (1, f_all), 1) >= f_cut
-        logit_part = jnp.sum(
-            jnp.where(shared_cols, grad_hidden * gate_in * squash * up_in, 0.0), axis=1
-        ) * (1.0 - router_steps[step])
-        dx = dot_nn(gate_grad, w_gate) + dot_nn(up_grad, w_up)
-        dx = (dx + logit_part[:, None] * router_wide[None, :]).astype(narrow)
-        router_grad_part = router_grad_part + jnp.sum(
-            logit_part[:, None] * x_steps[step].astype(wide), axis=0
+    g_chain = chain_gather(grad_own)
+    g_steps = [bits_gather(block, r_bits) for block in g_chain]
+    backward, dx_sums, total = [], {}, None
+    for step in range(chips):
+        g, ready = g_steps[step], []
+        if step + 1 < chips:
+            ready.append(g_chain[step + 1])
+        if step >= 1:
+            ready += list(backward[step - 1][0])
+        if step >= 2:
+            dx_sums[step - 2] = bits_scatter(backward[step - 2][0], r_bits)
+            ready.append(dx_sums[step - 2])
+        flat = list(lax.optimization_barrier((*g, *ready)))
+        if step >= 2:
+            dx_sums[step - 2] = flat[-1]
+        backward.append(
+            backward_step(
+                flat[: len(g)],
+                weights,
+                forward[step][1],
+                forward[step][2],
+                mix_one[step],
+                mix_two[step],
+                forward[step][4],
+                router_row,
+                f_expert,
+            )
         )
-        g_steps.append(g)
-        gate_grads.append(gate_grad)
-        up_grads.append(up_grad)
-        dx_steps.append((dx[:rows], dx[rows:]))
-    normed_two_grad = ring_scatter(dx_steps)
-
-    x_all = jnp.concatenate(x_steps, axis=0)
-    g_all = jnp.concatenate(g_steps, axis=0)
-    down_full = dot_tn(jnp.concatenate(hidden_steps, axis=0), g_all).astype(narrow)
-    gate_full = dot_tn(jnp.concatenate(gate_grads, axis=0), x_all).astype(narrow)
-    up_full = dot_tn(jnp.concatenate(up_grads, axis=0), x_all).astype(narrow)
-
-    def shared_sum(full):
-        own = plane_scatter(
-            [full[f_cut + j * f_shared : f_cut + (j + 1) * f_shared] for j in range(n_tensor)]
-        ).astype(narrow)
-        whole = jnp.zeros((n_dp * f_shared, D), narrow)
-        for pair, at in zip(ring_gather(own), sources):
-            for block, source in zip(pair, at):
-                whole = lax.dynamic_update_slice_in_dim(whole, block, source * f_shared, 0)
-        return whole
-
-    def expert_sum(full):
-        return plane_scatter([full[j * f_expert : (j + 1) * f_expert] for j in range(n_tensor)])
-
-    shared_down_grad = shared_sum(down_full).astype(wide)
-    shared_gate_grad = shared_sum(gate_full).T.astype(wide)
-    shared_up_grad = shared_sum(up_full).T.astype(wide)
+    gate_grads = [item[1] for item in backward]
+    up_grads = [item[2] for item in backward]
+    hidden_steps = [forward[step][3] for step in range(chips)]
+
+    def core_sum(mine, other):
+        return (mine.astype(wide) + swap_core(other).astype(wide)).astype(narrow)
+
+    def shared_part(both):
+        size = f_expert + f_pad
+        own = bits_scatter(
+            [both[j * size + f_expert : (j + 1) * size] for j in range(n_hidden)], w_bits
+        )
+        return own[:f_shared].astype(narrow)
+
+    def expert_part(both):
+        size = f_expert + f_pad
+        return bits_scatter([both[j * size : j * size + f_expert] for j in range(n_hidden)], w_bits)
+
+    def held_until(steps, *others):
+        count = len(steps[0])
+        flat = lax.optimization_barrier((*[b for blocks in steps for b in blocks], *others))
+        blocks = flat[: count * len(steps)]
+        held = [list(blocks[i * count : (i + 1) * count]) for i in range(len(steps))]
+        return held, flat[count * len(steps) :]
+
+    total = None
+    for step in range(1, chips - 2):
+        here = dx_sums[step].astype(wide)
+        total = ring_next((here if total is None else here + total.astype(wide)).astype(narrow))
+    dx_sums[chips - 2] = bits_scatter(backward[chips - 2][0], r_bits)
+    held, (dx_sums[chips - 2], total, *_) = held_until(
+        g_steps, dx_sums[chips - 2], total, *backward[-1][0]
+    )
+    down_full = weight_grads(held, hidden_steps, f_expert + f_pad, f_expert, n_blocks)
+    total = ring_next((dx_sums[chips - 2].astype(wide) + total.astype(wide)).astype(narrow))
+    dx_sums[chips - 1] = bits_scatter(backward[chips - 1][0], r_bits)
+    held, (dx_sums[chips - 1], total, *down_full) = held_until(
+        x_steps, dx_sums[chips - 1], total, *down_full
+    )
+    gate_full = weight_grads(held, gate_grads, f_expert + f_pad, f_expert, n_blocks)
+    total = ring_next((dx_sums[chips - 1].astype(wide) + total.astype(wide)).astype(narrow))
+    normed_two_grad = dx_sums[0].astype(wide) + total.astype(wide)
+    down_both = core_sum(*down_full)
+    held, (normed_two_grad, down_both, *gate_full) = held_until(
+        x_steps, normed_two_grad, down_both, *gate_full
+    )
+    up_full = weight_grads(held, up_grads, f_expert + f_pad, f_expert, n_blocks)
 
     grad_wide = grad_own.astype(wide)
     mlp_gain_part = jnp.sum(normed_two_grad * hat_two, axis=0)
@@ -386,9 +831,35 @@
     hidden_grad = grad_wide + inverse_two * (
         scaled_two - hat_two * jnp.mean(scaled_two * hat_two, axis=1, keepdims=True)
     )
-    hidden_grad_low = jnp.concatenate(plane_gather(hidden_grad.astype(narrow)), axis=0)
-
-    o_grad = dot_tn(hidden_grad_low, mixed_low)
+    router_grad_part = sum(
+        jnp.sum(backward[step][3][i * rows : (i + 1) * rows] * block.astype(wide), axis=0)
+        for step in range(chips)
+        for i, block in enumerate(x_steps[step])
+    )
+    own_low = hidden_grad.astype(narrow)
+    if n_tensor == 4:
+        cut = split_at(rows)
+        one, two = flip(own_low, 1), flip(own_low, 2)
+        one, two, down_both, *up_full = lax.optimization_barrier((one, two, down_both, *up_full))
+        low, high = flip(two[:cut], 1), flip(one[cut:], 2)
+        shared_down_own = shared_part(down_both)
+        grad_blocks = [own_low, one, two, low, high]
+    else:
+        shared_down_own = shared_part(down_both)
+        grad_blocks = plane_gather(own_low)
+    hidden_grad_low = jnp.concatenate(grad_blocks, axis=0)
+    gate_both = core_sum(*gate_full)
+    hidden_grad_low, shared_down_own, gate_both = lax.optimization_barrier(
+        (hidden_grad_low, shared_down_own, gate_both)
+    )
+    shared_down_all = lax.all_gather(shared_down_own, "dp", axis=0, tiled=True)
+    shared_gate_own = shared_part(gate_both)
+    up_both = core_sum(*up_full)
+
+    o_grad = dot_tn(mixed_low, hidden_grad_low)
+    o_grad, shared_gate_own, up_both = lax.optimization_barrier((o_grad, shared_gate_own, up_both))
+    shared_gate_all = lax.all_gather(shared_gate_own, "dp", axis=0, tiled=True)
+    shared_up_own = shared_part(up_both)
     mixed_grad = dot_nt(hidden_grad_low, o_weight).astype(narrow).reshape(GROUP, heads, HD)
     scores_again = attention_scores(query_low, key_low, visible, scale)
     probs = jnp.exp(scores_again - log_total)
@@ -407,6 +878,16 @@
     query_lin_grad = rotate_back(query_grad, cosine, sine).reshape(GROUP, heads * HD).astype(narrow)
     key_lin_grad = rotate_back(key_grad, cosine, sine).reshape(GROUP, heads * HD).astype(narrow)
     value_lin_grad = value_grad.reshape(GROUP, heads * HD).astype(narrow)
+    expert_gate_own, expert_up_own, expert_down_own = (
+        expert_part(both) for both in (gate_both, up_both, down_both)
+    )
+    expert_down_grad = expert_down_own[None]
+    expert_gate_grad = expert_gate_own.T[None]
+    expert_up_grad = expert_up_own.T[None]
+    query_lin_grad, shared_up_own, _ = lax.optimization_barrier(
+        (query_lin_grad, shared_up_own, expert_down_own)
+    )
+    shared_up_all = lax.all_gather(shared_up_own, "dp", axis=0, tiled=True)
     norm_one_part = (
         dot_nt(query_lin_grad, q_weight)
         + dot_nt(key_lin_grad, k_weight)
@@ -422,71 +903,85 @@
     )
 
     width = heads * HD
-    attn_grads = jnp.concatenate(
-        [
-            dot_tn(normed_one, query_lin_grad).astype(narrow),
-            dot_tn(normed_one, key_lin_grad).astype(narrow),
-            dot_tn(normed_one, value_lin_grad).astype(narrow),
-            o_grad.astype(narrow),
-        ],
-        axis=1,
-    )
-    piece = D // n_dp
-    attn_sum = ring_scatter(
-        [
-            tuple(lax.dynamic_slice_in_dim(attn_grads, s * piece, piece, 0) for s in pair)
-            for pair in sources
-        ]
+
+    sources = ring_sources()
+    ring_places = ring_chips()
+
+    def dp_sum(full, scatter_ties=(), gather_ties=()):
+        piece = full.shape[0] // n_dp
+        core = data_index % 2
+        by_core = full.reshape(chips, 2, piece, full.shape[1])
+        mine = lax.dynamic_index_in_dim(by_core, core, 1, keepdims=False)
+        other = lax.dynamic_index_in_dim(by_core, 1 - core, 1, keepdims=False)
+        both = (mine.astype(wide) + swap_core(other).astype(wide)).astype(narrow)
+        parts = [lax.dynamic_index_in_dim(both, at, 0, keepdims=False) for at in ring_places]
+
+        def tie(value, ties, step):
+            return after(value, *ties[step]) if step < len(ties) else value
+
+        total = tie(ring_next(parts[1]), scatter_ties, 0)
+        for step in range(2, chips):
+            total = ring_next((parts[step].astype(wide) + total.astype(wide)).astype(narrow))
+            total = tie(total, scatter_ties, step - 1)
+        held = [(parts[0].astype(wide) + total.astype(wide)).astype(narrow)]
+        for step in range(chips - 1):
+            held.append(tie(ring_next(held[-1]), gather_ties, step))
+        blocks, places = [], []
+        for block, at in zip(held, sources):
+            blocks += [block, swap_core(block)]
+            places += [source * piece for source in at]
+        return blocks, jnp.stack(places)
+
+    o_blocks, o_places = dp_sum(o_grad.astype(narrow))
+    (o_sum,) = assemble(o_blocks, o_places, 1)
+    qkv_grad = dot_tn(
+        normed_one, jnp.concatenate([query_lin_grad, key_lin_grad, value_lin_grad], axis=1)
     ).astype(narrow)
-    attn_whole = jnp.zeros((D, 4 * width), narrow)
-    for pair, at in zip(ring_gather(attn_sum), sources):
-        for block, source in zip(pair, at):
-            attn_whole = lax.dynamic_update_slice_in_dim(attn_whole, block, source * piece, 0)
-    attn_whole = attn_whole.astype(wide)
-
-    expert_down_grad = expert_sum(down_full)[None]
-    expert_gate_grad = expert_sum(gate_full).T[None]
-    expert_up_grad = expert_sum(up_full).T[None]
-
-    bias_part = jnp.concatenate(
-        [
-            jnp.sum(query_lin_grad.astype(wide), axis=0),
-            jnp.sum(key_lin_grad.astype(wide), axis=0),
-            jnp.sum(value_lin_grad.astype(wide), axis=0),
-        ]
-    )
-    bias_spread = lax.dynamic_update_slice_in_dim(
-        jnp.zeros((n_tensor, 3 * width), wide), bias_part[None], slice_index, 0
-    )
-    small = lax.psum(
+    shared_down_grad = shared_down_all.astype(wide)
+    shared_gate_grad = turn(shared_gate_all)
+    shared_up_grad = turn(shared_up_all)
+    qkv_blocks, qkv_places = dp_sum(
+        qkv_grad,
+        ((shared_down_grad, expert_gate_grad), (shared_gate_grad,), (expert_up_grad, input_grad)),
+        ((shared_up_grad,), (o_sum,)),
+    )
+    q_sum, k_sum, v_sum = assemble(qkv_blocks, qkv_places, 3)
+
+    gains = sum_over_plane(
         jnp.concatenate(
             [
                 attn_gain_part,
                 mlp_gain_part,
                 router_grad_part,
                 jnp.broadcast_to(squared_own, (128,)),
-                bias_spread.reshape(-1),
             ]
-        ),
-        ("dp", "tensor"),
+        )
+    )
+    small = sum_over_dp(
+        jnp.concatenate(
+            [
+                gains,
+                jnp.sum(query_lin_grad.astype(wide), axis=0),
+                jnp.sum(key_lin_grad.astype(wide), axis=0),
+                jnp.sum(value_lin_grad.astype(wide), axis=0),
+            ]
+        )
     )
     attn_gain_grad, mlp_gain_grad, shared_router_grad = (small[i * D : (i + 1) * D] for i in range(3))
     teacher_loss = small[3 * D] / (valid_count * D)
-    biases = lax.dynamic_index_in_dim(
-        small[3 * D + 128 :].reshape(n_tensor, 3 * width), slice_index, 0, keepdims=False
-    )
+    biases = small[3 * D + 128 :]
     return (
         result.astype(narrow),
         teacher_loss,
         input_grad,
         attn_gain_grad,
-        attn_whole[:, :width],
+        q_sum,
         biases[:width],
-        attn_whole[:, width : 2 * width],
+        k_sum,
         biases[width : 2 * width],
-        attn_whole[:, 2 * width : 3 * width],
+        v_sum,
         biases[2 * width :],
-        attn_whole[:, 3 * width :].T,
+        o_sum,
         mlp_gain_grad,
         expert_gate_grad,
         expert_up_grad,

time: 1310 us -> 1040 us (0.79)
  Pallas kernels: 0 us -> 277 us
  matrix products: 278 us -> 52.6 us
  waiting for transfers between devices: 535 us -> 395 us
  local copies, waits for them, and re-layouts: 174 us -> 57.3 us
  blocking collectives: 55.9 us -> 0 us
  between operations: 8.22 us -> 26.3 us
    pallas_call x0 -> x15, Pallas kernels: none -> 277 us  [the longest x4 96.3 us: backward_step(): pl.pallas_call(functools.partial(backward_body, rows, count, places, bloc...]
    ppermute x27 -> x30, waiting for transfers between devices: 304 us -> 151 us  [ring_next(): return lax.ppermute(value, 'dp', pairs)]
    dot_general x16 -> x4, matrix products: 127 us -> 12.6 us  [dot_nt(): lax.dot_general(left, right, (((1,), (1,)), ((), ())), preferred_element_...]
    unnamed x358 -> x218, local copies, waits for them, and re-layouts: 86.6 us -> 22.3 us
    dot_general x16 -> x4, matrix products: 66.6 us -> 7.71 us  [dot_nn(): lax.dot_general(left, right, (((1,), (0,)), ((), ())), preferred_element_...]
    dot_general x7 -> x2, matrix products: 67.9 us -> 12.7 us  [dot_tn(): lax.dot_general(left, right, (((0,), (0,)), ((), ())), preferred_element_...]
    psum x1 -> x0, blocking collectives: 40.2 us -> none  [shards(): lax.psum(jnp.concatenate([attn_gain_part, mlp_gain_part, router_grad_part...]
    dynamic_update_slice x29 -> x0, local copies, waits for them, and re-layouts: 22.9 us -> none  [the longest x7 13.9 us: shards(): lax.dynamic_update_slice_in_dim(attn_whole, block, source * piece, 0)]
  transfers between devices with their start and end apart: 115 -> 96, of which waited for: 52 -> 39; matrix products, arithmetic and copies ran while one was open for 29% -> 20% of each run, Pallas kernels for 0% -> 26%
where the time goes in v2:
time: 1040 us
  waiting for transfers between devices  395 us (38%)
  Pallas kernels  277 us (27%)
  other arithmetic  141 us (14%)
  starting transfers between devices  88.3 us (8%)
  local copies, waits for them, and re-layouts  57.3 us (6%)
  matrix products  52.6 us (5%)
  between operations  26.3 us (3%)
    ppermute x43, waiting for transfers between devices, flip(): return lax.ppermute(value, 'tensor', [(i, i ^ bit) for i in range(size)])  241 us
    ppermute x30, waiting for transfers between devices, ring_next(): return lax.ppermute(value, 'dp', pairs)  151 us
    pallas_call x4, Pallas kernels, backward_step(): pl.pallas_call(functools.partial(backward_body, rows, count, places, bloc...  96.3 us
    pallas_call x4, Pallas kernels, forward_step(): pl.pallas_call(functools.partial(forward_body, rows, count, places, block...  89.7 us
    pallas_call x3, Pallas kernels, weight_grads(): pl.pallas_call(functools.partial(weight_body, rows, steps, blocks, places...  60.1 us
    ppermute x43, starting transfers between devices, flip(): return lax.ppermute(value, 'tensor', [(i, i ^ bit) for i in range(size)])  51.8 us
    ppermute x30, starting transfers between devices, ring_next(): return lax.ppermute(value, 'dp', pairs)  31.8 us
    convert_element_type x3, other arithmetic, core_sum(): return (mine.astype(wide) + swap_core(other).astype(wide)).astype(narrow)  24.8 us
  transfers between devices with their start and end apart: 96, of which 39 were waited for; matrix products, arithmetic and copies ran while one was open for 20% of the time, Pallas kernels for 26%

profile of v2, /device:TPU:0, one launch (start us, length us, event | category | flops | bytes accessed | tf_op | source)
XLA Modules:
  0.0 1037.7 jit_solution(2713281682551566009)
XLA Ops:
  64.3 37.9 %collective-permute-done.4.refs_3_ = bf16[528,2048]{1,0:T(8,128)(2,1)} collective-permute-done((bf16[528,2048]{1,0:T(8,128)(2,1)S(1)}, bf16[528,2048]{1,0:T(8,128)(2,1)}, u32[]{:S(2)}, u32[]{:S(2)}) %collective-permute-start.4) | collective-permute-done | bytes 2162720 | tf_op jit(solution)/shard_map/ppermute | solution.py:88
  102.2 43.1 %collective-permute-done.5.refs_7_ = bf16[528,2048]{1,0:T(8,128)(2,1)} collective-permute-done((bf16[528,2048]{1,0:T(8,128)(2,1)S(1)}, bf16[528,2048]{1,0:T(8,128)(2,1)}, u32[]{:S(2)}, u32[]{:S(2)}) %collective-permute-start.5) | collective-permute-done | bytes 2162720 | tf_op jit(solution)/shard_map/ppermute | solution.py:88
  204.1 16.5 %collective-permute-done.10.refs_1_ = bf16[192,2048]{1,0:T(8,128)(2,1)S(1)} collective-permute-done((bf16[192,2048]{1,0:T(8,128)(2,1)S(1)}, bf16[192,2048]{1,0:T(8,128)(2,1)S(1)}, u32[]{:S(2)}, u32[]{:S(2)}) %collective-permute-start.10) | collective-permute-done | bytes 786464 | tf_op jit(solution)/shard_map/ppermute | solution.py:88
  231.9 16.2 %collective-permute-done.12.refs_0_.refs_4_ = bf16[192,2048]{1,0:T(8,128)(2,1)} collective-permute-done((bf16[192,2048]{1,0:T(8,128)(2,1)S(1)}, bf16[192,2048]{1,0:T(8,128)(2,1)}, u32[]{:S(2)}, u32[]{:S(2)}) %collective-permute-start.12) | collective-permute-done | bytes 786464 | tf_op jit(solution)/shard_map/ppermute | solution.py:142
  263.1 22.5 %ffn_forward.4 = (bf16[192,2048]{1,0:T(8,128)(2,1)}, bf16[192,2048]{1,0:T(8,128)(2,1)}, bf16[384,2112]{1,0:T(8,128)(2,1)}, bf16[384,2112]{1,0:T(8,128)(2,1)}, bf...) custom-call(bf16[192,2048]{1,0:T(8,128)(2,1)} %copy-done.47, bf16[192,2048]{1,0:T(8,128)(2,1)} %copy-done.49, ...), custom_call_target="tpu_custom_call" | custom-call | flops 9965666304 | bytes 33964032 | tf_op jit(solution)/shard_map/ffn_forward/pallas_call | solution.py:343
  286.0 22.5 %ffn_forward.5 = (bf16[192,2048]{1,0:T(8,128)(2,1)}, bf16[192,2048]{1,0:T(8,128)(2,1)}, bf16[384,2112]{1,0:T(8,128)(2,1)}, bf16[384,2112]{1,0:T(8,128)(2,1)}, bf...) custom-call(bf16[192,2048]{1,0:T(8,128)(2,1)} %collective-permute-done.12.refs_0_.refs_4_, ...), custom_call_target="tpu_custom_call" | custom-call | flops 9965666304 | bytes 33964032 | tf_op jit(solution)/shard_map/ffn_forward/pallas_call | solution.py:343
  313.8 22.3 %ffn_forward.6 = (bf16[192,2048]{1,0:T(8,128)(2,1)}, bf16[192,2048]{1,0:T(8,128)(2,1)}, bf16[384,2112]{1,0:T(8,128)(2,1)}, bf16[384,2112]{1,0:T(8,128)(2,1)}, bf...) custom-call(bf16[192,2048]{1,0:T(8,128)(2,1)} %collective-permute-done.13.refs_0_.refs_6_, ...), custom_call_target="tpu_custom_call" | custom-call | flops 9965666304 | bytes 33964032 | tf_op jit(solution)/shard_map/ffn_forward/pallas_call | solution.py:343
  342.4 22.3 %ffn_forward.7 = (bf16[192,2048]{1,0:T(8,128)(2,1)}, bf16[192,2048]{1,0:T(8,128)(2,1)}, bf16[384,2112]{1,0:T(8,128)(2,1)}, bf16[384,2112]{1,0:T(8,128)(2,1)}, bf...) custom-call(bf16[192,2048]{1,0:T(8,128)(2,1)} %copy-done.52, bf16[192,2048]{1,0:T(8,128)(2,1)} %copy-done.51, ...), custom_call_target="tpu_custom_call" | custom-call | flops 9965666304 | bytes 33964032 | tf_op jit(solution)/shard_map/ffn_forward/pallas_call | solution.py:343
  391.9 18.5 %collective-permute-done.39.refs_1_ = bf16[192,2048]{1,0:T(8,128)(2,1)S(1)} collective-permute-done((bf16[192,2048]{1,0:T(8,128)(2,1)S(1)}, bf16[192,2048]{1,0:T(8,128)(2,1)S(1)}, u32[]{:S(2)}, u32[]{:S(2)}) %collective-permute-start.39) | collective-permute-done | bytes 786464 | tf_op jit(solution)/shard_map/ppermute | solution.py:88
  413.9 23.9 %ffn_backward.4 = (bf16[192,2048]{1,0:T(8,128)(2,1)}, bf16[192,2048]{1,0:T(8,128)(2,1)}, bf16[384,2112]{1,0:T(8,128)(2,1)}, bf16[384,2112]{1,0:T(8,128)(2,1)}, f32[384,1]{1,0:T(8,128)}) custom-call(bf16[192,2048]{1,0:T(8,128)(2,1)} %copy-done.18, bf16[192,2048]{1,0:T(8,128)(2,1)} %copy-done.84, bf16[528,2048]{1,0:T(8,128)(2,1)} %copy-done.28, ...), custom_call_target="tpu_custom_call" | custom-call | flops 9965666304 | bytes 35586048 | tf_op jit(solution)/shard_map/ffn_backward/pallas_call | solution.py:430
  440.7 24.2 %ffn_backward.5 = (bf16[192,2048]{1,0:T(8,128)(2,1)}, bf16[192,2048]{1,0:T(8,128)(2,1)}, bf16[384,2112]{1,0:T(8,128)(2,1)}, bf16[384,2112]{1,0:T(8,128)(2,1)}, f32[384,1]{1,0:T(8,128)}) custom-call(bf16[192,2048]{1,0:T(8,128)(2,1)} %collective-permute-done.34.refs_0_.refs_2_, bf16[192,2048]{1,0:T(8,128)(2,1)} %collective-permute-done.38.refs_1_.refs_3_, ...), custom_call_target="tpu_custom_call" | custom-call | flops 9965666304 | bytes 35586048 | tf_op jit(solution)/shard_map/ffn_backward/pallas_call | solution.py:430
  473.3 24.0 %ffn_backward.6 = (bf16[192,2048]{1,0:T(8,128)(2,1)}, bf16[192,2048]{1,0:T(8,128)(2,1)}, bf16[384,2112]{1,0:T(8,128)(2,1)}, bf16[384,2112]{1,0:T(8,128)(2,1)}, f32[384,1]{1,0:T(8,128)}) custom-call(bf16[192,2048]{1,0:T(8,128)(2,1)} %collective-permute-done.35.refs_0_.refs_4_, bf16[192,2048]{1,0:T(8,128)(2,1)} %collective-permute-done.36.refs_1_.refs_5_, ...), custom_call_target="tpu_custom_call" | custom-call | flops 9965666304 | bytes 35586048 | tf_op jit(solution)/shard_map/ffn_backward/pallas_call | solution.py:430
  502.3 24.2 %ffn_backward.7 = (bf16[192,2048]{1,0:T(8,128)(2,1)}, bf16[192,2048]{1,0:T(8,128)(2,1)}, bf16[384,2112]{1,0:T(8,128)(2,1)}, bf16[384,2112]{1,0:T(8,128)(2,1)}, f32[384,1]{1,0:T(8,128)}) custom-call(bf16[192,2048]{1,0:T(8,128)(2,1)} %collective-permute-done.37.refs_0_.refs_6_, bf16[192,2048]{1,0:T(8,128)(2,1)} %collective-permute-done.41.refs_1_.refs_7_, ...), custom_call_target="tpu_custom_call" | custom-call | flops 9965666304 | bytes 35586048 | tf_op jit(solution)/shard_map/ffn_backward/pallas_call | solution.py:430
  530.6 20.0 %weight_grads.3 = (bf16[1056,2048]{1,0:T(8,128)(2,1)}, bf16[1056,2048]{1,0:T(8,128)(2,1)}) custom-call(bf16[192,2048]{1,0:T(8,128)(2,1)} %copy-done.18, bf16[192,2048]{1,0:T(8,128)(2,1)} %copy-done.84, bf16[192,2048]{1,0:T(8,128)(2,1)} %collective-permute-done.34.refs_0_.refs_2_, bf16[192,2048]{1,0:T(8,128)(2,1)} %collective-permute-done.38.refs_1_.refs_3_, ...), custom_call_target="tpu_custom_call" | custom-call | flops 13287555072 | bytes 21430272 | tf_op jit(solution)/shard_map/weight_grads/pallas_call | solution.py:502
  559.4 20.0 %weight_grads.4 = (bf16[1056,2048]{1,0:T(8,128)(2,1)}, bf16[1056,2048]{1,0:T(8,128)(2,1)}) custom-call(bf16[192,2048]{1,0:T(8,128)(2,1)} %copy-done.52, bf16[192,2048]{1,0:T(8,128)(2,1)} %copy-done.51, bf16[192,2048]{1,0:T(8,128)(2,1)} %copy-done.47, bf16[192,2048]{1,0:T(8,128)(2,1)} %copy-done.49, ...), custom_call_target="tpu_custom_call" | custom-call | flops 13287555072 | bytes 21430272 | tf_op jit(solution)/shard_map/weight_grads/pallas_call | solution.py:502
  594.4 20.1 %weight_grads.5 = (bf16[1056,2048]{1,0:T(8,128)(2,1)}, bf16[1056,2048]{1,0:T(8,128)(2,1)}) custom-call(bf16[192,2048]{1,0:T(8,128)(2,1)} %copy-done.52, bf16[192,2048]{1,0:T(8,128)(2,1)} %copy-done.51, bf16[192,2048]{1,0:T(8,128)(2,1)} %copy-done.47, bf16[192,2048]{1,0:T(8,128)(2,1)} %copy-done.49, ...), custom_call_target="tpu_custom_call" | custom-call | flops 13287555072 | bytes 21430272 | tf_op jit(solution)/shard_map/weight_grads/pallas_call | solution.py:502
  660.0 11.5 %collective-permute-done.55 = bf16[176,2048]{1,0:T(8,128)(2,1)S(1)} collective-permute-done((bf16[176,2048]{1,0:T(8,128)(2,1)S(1)}, bf16[176,2048]{1,0:T(8,128)(2,1)S(1)}, u32[]{:S(2)}, u32[]{:S(2)}) %collective-permute-start.55) | collective-permute-done | bytes 720928 | tf_op jit(solution)/shard_map/ppermute | solution.py:88
  750.5 33.6 %collective-permute-done.57 = bf16[176,2048]{1,0:T(8,128)(2,1)S(1)} collective-permute-done((bf16[176,2048]{1,0:T(8,128)(2,1)S(1)}, bf16[176,2048]{1,0:T(8,128)(2,1)S(1)}, u32[]{:S(2)}, u32[]{:S(2)}) %collective-permute-start.57) | collective-permute-done | bytes 720928 | tf_op jit(solution)/shard_map/ppermute | solution.py:88
  829.8 12.0 %collective-permute-done.80 = bf16[64,2048]{1,0:T(8,128)(2,1)S(1)} collective-permute-done((bf16[64,2048]{1,0:T(8,128)(2,1)S(1)}, bf16[64,2048]{1,0:T(8,128)(2,1)S(1)}, u32[]{:S(2)}, u32[]{:S(2)}) %collective-permute-start.80) | collective-permute-done | bytes 262176 | tf_op jit(solution)/shard_map/ppermute | solution.py:142
  852.2 23.0 %collective-permute-done.70 = bf16[256,1536]{1,0:T(8,128)(2,1)} collective-permute-done((bf16[256,1536]{1,0:T(8,128)(2,1)}, bf16[256,1536]{1,0:T(8,128)(2,1)}, u32[]{:S(2)}, u32[]{:S(2)}) %collective-permute-start.70) | collective-permute-done | bytes 786464 | tf_op jit(solution)/shard_map/ppermute | solution.py:142
  908.1 15.1 %collective-permute-done.73 = bf16[256,1536]{1,0:T(8,128)(2,1)S(1)} collective-permute-done((bf16[256,1536]{1,0:T(8,128)(2,1)S(1)}, bf16[256,1536]{1,0:T(8,128)(2,1)S(1)}, u32[]{:S(2)}, u32[]{:S(2)}) %collective-permute-start.73) | collective-permute-done | bytes 786464 | tf_op jit(solution)/shard_map/ppermute | solution.py:142
  934.6 15.0 %collective-permute-done.84.refs_3_ = bf16[64,2048]{1,0:T(8,128)(2,1)S(1)} collective-permute-done((bf16[64,2048]{1,0:T(8,128)(2,1)S(1)}, bf16[64,2048]{1,0:T(8,128)(2,1)S(1)}, u32[]{:S(2)}, u32[]{:S(2)}) %collective-permute-start.84) | collective-permute-done | bytes 262176 | tf_op jit(solution)/shard_map/ppermute | solution.py:142
  964.5 18.3 %collective-permute-done.66 = f32[7808]{0:T(1024)S(1)} collective-permute-done((f32[7808]{0:T(1024)S(1)}, f32[7808]{0:T(1024)S(1)}, u32[]{:S(2)}, u32[]{:S(2)}) %collective-permute-start.66) | collective-permute-done | bytes 31264 | tf_op jit(solution)/shard_map/ppermute | solution.py:142
  1001.8 13.4 %collective-permute-done.68 = f32[7808]{0:T(1024)S(1)} collective-permute-done((f32[7808]{0:T(1024)S(1)}, f32[7808]{0:T(1024)S(1)}, u32[]{:S(2)}, u32[]{:S(2)}) %collective-permute-start.68) | collective-permute-done | bytes 31264 | tf_op jit(solution)/shard_map/ppermute | solution.py:142
  (581 shorter events, 491.2 us)
Async XLA Ops:
  7.2 836.3 %all-gather.4.cloned.1.call-start = ((), (), s32[]{:S(2)}) async-start(), calls=%async_computation | async-start | bytes 6488064 | tf_op jit(solution)/shard_map/all_gather | solution.py:855
  52.0 50.1 %collective-permute-start.4 = (bf16[528,2048]{1,0:T(8,128)(2,1)S(1)}, bf16[528,2048]{1,0:T(8,128)(2,1)}, u32[]{:S(2)}, u32[]{:S(2)}) collective-permute-start(bf16[528,2048]{1,0:T(8,128)(2,1)S(1)} %pad_maximum_fusion.refs_2_), channel_id=1, source_target_pairs={{0,1},{1,0},{2,3},{3,2},{4,5},{5,4},{6,7},{7,6},{8,9},{9,8},{10,11... | collective-permute-start | bytes 6488072 | tf_op jit(solution)/shard_map/ppermute | solution.py:88
  52.7 92.5 %collective-permute-start.5 = (bf16[528,2048]{1,0:T(8,128)(2,1)S(1)}, bf16[528,2048]{1,0:T(8,128)(2,1)}, u32[]{:S(2)}, u32[]{:S(2)}) collective-permute-start(bf16[528,2048]{1,0:T(8,128)(2,1)S(1)} %pad_maximum_fusion.1.refs_6_), channel_id=1, source_target_pairs={{0,1},{1,0},{2,3},{3,2},{4,5},{5,4},{6,7},{7,6},{8,9},{9,8},{10,11... | collective-permute-start | bytes 6488072 | tf_op jit(solution)/shard_map/ppermute | solution.py:88
  163.2 40.4 %collective-permute-start.17 = (bf16[528,2048]{1,0:T(8,128)(2,1)S(1)}, bf16[528,2048]{1,0:T(8,128)(2,1)S(1)}, u32[]{:S(2)}, u32[]{:S(2)}) collective-permute-start(bf16[528,2048]{1,0:T(8,128)(2,1)S(1)} %pad_maximum_fusion.refs_2_), channel_id=1, source_target_pairs={{0,4},{4,0},{8,12},{12,8},{16,20},{20,16},{24,28},{28,24},{1,5},{5... | collective-permute-start | bytes 6488072 | tf_op jit(solution)/shard_map/ppermute | solution.py:147
  163.2 40.4 %collective-permute-start.19 = (bf16[528,2048]{1,0:T(8,128)(2,1)S(1)}, bf16[528,2048]{1,0:T(8,128)(2,1)S(1)}, u32[]{:S(2)}, u32[]{:S(2)}) collective-permute-start(bf16[528,2048]{1,0:T(8,128)(2,1)S(1)} %pad_maximum_fusion.1.refs_6_), channel_id=1, source_target_pairs={{0,4},{4,0},{8,12},{12,8},{16,20},{20,16},{24,28},{28,24},{1,5},{5... | collective-permute-start | bytes 6488072 | tf_op jit(solution)/shard_map/ppermute | solution.py:147
  174.0 46.6 %collective-permute-start.21 = (bf16[528,2048]{1,0:T(8,128)(2,1)}, bf16[528,2048]{1,0:T(8,128)(2,1)}, u32[]{:S(2)}, u32[]{:S(2)}) collective-permute-start(bf16[528,2048]{1,0:T(8,128)(2,1)} %pad_maximum_fusion.2.refs_10_), channel_id=1, source_target_pairs={{0,1},{1,0},{2,3},{3,2},{4,5},{5,4},{6,7},{7,6},{8,9},{9,8},{10,11... | collective-permute-start | bytes 6488072 | tf_op jit(solution)/shard_map/ppermute | solution.py:88
  203.6 52.9 %collective-permute-start.18 = (bf16[528,2048]{1,0:T(8,128)(2,1)}, bf16[528,2048]{1,0:T(8,128)(2,1)}, u32[]{:S(2)}, u32[]{:S(2)}) collective-permute-start(bf16[528,2048]{1,0:T(8,128)(2,1)} %collective-permute-done.4.refs_3_), channel_id=1, source_target_pairs={{0,4},{4,0},{8,12},{12,8},{16,20},{20,16},{24,28},{28,24},{1,5},{5... | collective-permute-start | bytes 6488072 | tf_op jit(solution)/shard_map/ppermute | solution.py:147
  203.6 59.4 %collective-permute-start.20 = (bf16[528,2048]{1,0:T(8,128)(2,1)}, bf16[528,2048]{1,0:T(8,128)(2,1)}, u32[]{:S(2)}, u32[]{:S(2)}) collective-permute-start(bf16[528,2048]{1,0:T(8,128)(2,1)} %collective-permute-done.5.refs_7_), channel_id=1, source_target_pairs={{0,4},{4,0},{8,12},{12,8},{16,20},{20,16},{24,28},{28,24},{1,5},{5... | collective-permute-start | bytes 6488072 | tf_op jit(solution)/shard_map/ppermute | solution.py:147
  220.6 42.4 %collective-permute-start.22 = (bf16[528,2048]{1,0:T(8,128)(2,1)}, bf16[528,2048]{1,0:T(8,128)(2,1)}, u32[]{:S(2)}, u32[]{:S(2)}) collective-permute-start(bf16[528,2048]{1,0:T(8,128)(2,1)} %pad_maximum_fusion.2.refs_10_), channel_id=1, source_target_pairs={{0,4},{4,0},{8,12},{12,8},{16,20},{20,16},{24,28},{28,24},{1,5},{5... | collective-permute-start | bytes 6488072 | tf_op jit(solution)/shard_map/ppermute | solution.py:147
  220.6 42.4 %collective-permute-start.23 = (bf16[528,2048]{1,0:T(8,128)(2,1)}, bf16[528,2048]{1,0:T(8,128)(2,1)}, u32[]{:S(2)}, u32[]{:S(2)}) collective-permute-start(bf16[528,2048]{1,0:T(8,128)(2,1)} %collective-permute-done.21.refs_11_), channel_id=1, source_target_pairs={{0,4},{4,0},{8,12},{12,8},{16,20},{20,16},{24,28},{28,24},{1,5},{5... | collective-permute-start | bytes 6488072 | tf_op jit(solution)/shard_map/ppermute | solution.py:147
  464.9 34.5 %collective-permute-start.42 = (bf16[192,2048]{1,0:T(8,128)(2,1)}, bf16[192,2048]{1,0:T(8,128)(2,1)}, u32[]{:S(2)}, u32[]{:S(2)}) collective-permute-start(bf16[192,2048]{1,0:T(8,128)(2,1)} %get-tuple-element.189), channel_id=1, source_target_pairs={{0,2},{1,3},{2,0},{3,1},{4,6},{5,7},{6,4},{7,5},{8,10},{9,11},{10,... | collective-permute-start | bytes 2359304 | tf_op jit(solution)/shard_map/ppermute | solution.py:88
  589.4 53.8 %collective-permute-start.54 = (bf16[1056,2048]{1,0:T(8,128)(2,1)}, bf16[1056,2048]{1,0:T(8,128)(2,1)}, u32[]{:S(2)}, u32[]{:S(2)}) collective-permute-start(bf16[1056,2048]{1,0:T(8,128)(2,1)} %get-tuple-element.260), channel_id=1, source_target_pairs={{0,4},{4,0},{8,12},{12,8},{16,20},{20,16},{24,28},{28,24},{1,5},{5... | collective-permute-start | bytes 12976136 | tf_op jit(solution)/shard_map/ppermute | solution.py:147
  651.2 237.4 %all-gather.6.cloned.1.call-start = ((), (), s32[]{:S(2)}) async-start(), calls=%async_computation.1 | async-start | bytes 6488064 | tf_op jit(solution)/shard_map/all_gather | solution.py:861
  682.0 267.6 %all-gather.8.cloned.1.call-start = ((), (), s32[]{:S(2)}) async-start(), calls=%async_computation.2 | async-start | bytes 6488064 | tf_op jit(solution)/shard_map/all_gather | solution.py:890
  703.1 294.8 %collective-permute-start.58 = (bf16[352,2048]{1,0:T(8,128)(2,1)}, bf16[352,2048]{1,0:T(8,128)(2,1)}, u32[]{:S(2)}, u32[]{:S(2)}) collective-permute-start(bf16[352,2048]{1,0:T(8,128)(2,1)} %slice.257), channel_id=1, source_target_pairs={{0,1},{1,0},{2,3},{3,2},{4,5},{5,4},{6,7},{7,6},{8,9},{9,8},{10,11... | collective-permute-start | bytes 4325384 | tf_op jit(solution)/shard_map/ppermute | solution.py:88
  707.5 88.9 %collective-permute-start.71 = (bf16[352,2048]{1,0:T(8,128)(2,1)}, bf16[352,2048]{1,0:T(8,128)(2,1)}, u32[]{:S(2)}, u32[]{:S(2)}) collective-permute-start(bf16[352,2048]{1,0:T(8,128)(2,1)} %slice.278), channel_id=1, source_target_pairs={{0,1},{1,0},{2,3},{3,2},{4,5},{5,4},{6,7},{7,6},{8,9},{9,8},{10,11... | collective-permute-start | bytes 4325384 | tf_op jit(solution)/shard_map/ppermute | solution.py:88
  737.9 46.2 %collective-permute-start.57 = (bf16[176,2048]{1,0:T(8,128)(2,1)S(1)}, bf16[176,2048]{1,0:T(8,128)(2,1)S(1)}, u32[]{:S(2)}, u32[]{:S(2)}) collective-permute-start(bf16[176,2048]{1,0:T(8,128)(2,1)S(1)} %slice.255), channel_id=1, source_target_pairs={{0,1},{1,0},{2,3},{3,2},{4,5},{5,4},{6,7},{7,6},{8,9},{9,8},{10,11... | collective-permute-start | bytes 2162696 | tf_op jit(solution)/shard_map/ppermute | solution.py:88
  749.6 59.2 %collective-permute-start.79 = (bf16[4,64,2048]{2,1,0:T(8,128)(2,1)}, bf16[4,64,2048]{2,1,0:T(8,128)(2,1)}, u32[]{:S(2)}, u32[]{:S(2)}) collective-permute-start(bf16[4,64,2048]{2,1,0:T(8,128)(2,1)} %dynamic-slice_bitcast_fusion.1), channel_id=1, source_target_pairs={{0,4},{4,0},{8,12},{12,8},{16,20},{20,16},{24,28},{28,24},{1,5},{5... | collective-permute-start | bytes 3145736 | tf_op jit(solution)/shard_map/ppermute | solution.py:147
  749.6 128.2 %collective-permute-start.74 = (bf16[352,2048]{1,0:T(8,128)(2,1)}, bf16[352,2048]{1,0:T(8,128)(2,1)}, u32[]{:S(2)}, u32[]{:S(2)}) collective-permute-start(bf16[352,2048]{1,0:T(8,128)(2,1)} %slice.280), channel_id=1, source_target_pairs={{0,1},{1,0},{2,3},{3,2},{4,5},{5,4},{6,7},{7,6},{8,9},{9,8},{10,11... | collective-permute-start | bytes 4325384 | tf_op jit(solution)/shard_map/ppermute | solution.py:88
  826.9 48.4 %collective-permute-start.70 = (bf16[256,1536]{1,0:T(8,128)(2,1)}, bf16[256,1536]{1,0:T(8,128)(2,1)}, u32[]{:S(2)}, u32[]{:S(2)}) collective-permute-start(bf16[256,1536]{1,0:T(8,128)(2,1)} %dynamic-slice_bitcast_fusion.2), channel_id=1, source_target_pairs={{0,8},{4,12},{8,24},{12,28},{24,16},{28,20},{16,0},{20,4},{1,9},{5... | collective-permute-start | bytes 2359304 | tf_op jit(solution)/shard_map/ppermute | solution.py:142
  828.5 57.7 %collective-permute-start.62 = (bf16[192,2048]{1,0:T(8,128)(2,1)}, bf16[192,2048]{1,0:T(8,128)(2,1)}, u32[]{:S(2)}, u32[]{:S(2)}) collective-permute-start(bf16[192,2048]{1,0:T(8,128)(2,1)} %pad_maximum_fusion.6), channel_id=1, source_target_pairs={{0,2},{1,3},{2,0},{3,1},{4,6},{5,7},{6,4},{7,5},{8,10},{9,11},{10,... | collective-permute-start | bytes 2359304 | tf_op jit(solution)/shard_map/ppermute | solution.py:88
  841.8 44.4 %collective-permute-start.60 = (bf16[192,2048]{1,0:T(8,128)(2,1)}, bf16[192,2048]{1,0:T(8,128)(2,1)}, u32[]{:S(2)}, u32[]{:S(2)}) collective-permute-start(bf16[192,2048]{1,0:T(8,128)(2,1)} %pad_maximum_fusion.5), channel_id=1, source_target_pairs={{0,1},{1,0},{2,3},{3,2},{4,5},{5,4},{6,7},{7,6},{8,9},{9,8},{10,11... | collective-permute-start | bytes 2359304 | tf_op jit(solution)/shard_map/ppermute | solution.py:88
  886.2 39.3 %collective-permute-start.82 = (bf16[64,2048]{1,0:T(8,128)(2,1)}, bf16[64,2048]{1,0:T(8,128)(2,1)S(1)}, u32[]{:S(2)}, u32[]{:S(2)}) collective-permute-start(bf16[64,2048]{1,0:T(8,128)(2,1)} %fusion.38), channel_id=1, source_target_pairs={{0,8},{4,12},{8,24},{12,28},{24,16},{28,20},{16,0},{20,4},{1,9},{5... | collective-permute-start | bytes 786440 | tf_op jit(solution)/shard_map/ppermute | solution.py:142
  958.8 35.0 %collective-permute-start.78 = (bf16[256,1536]{1,0:T(8,128)(2,1)}, bf16[256,1536]{1,0:T(8,128)(2,1)}, u32[]{:S(2)}, u32[]{:S(2)}) collective-permute-start(bf16[256,1536]{1,0:T(8,128)(2,1)} %collective-permute-done.76.refs_3_), channel_id=1, source_target_pairs={{0,8},{4,12},{8,24},{12,28},{24,16},{28,20},{16,0},{20,4},{1,9},{5... | collective-permute-start | bytes 2359304 | tf_op jit(solution)/shard_map/ppermute | solution.py:142
  (177 other events, 2900.3 us)
Sparse Core Ops, SparseCore 0:
  651.4 57.9 all-gather.3
  711.0 59.0 all-gather.5
  796.5 77.3 all-gather.7

commit v3 on v2

--- a/solution.py
+++ b/solution.py
@@ -79,8 +79,12 @@
     return lax.dot_general(left, right, (((0,), (0,)), ((), ())), preferred_element_type=WIDE)
 
 
+def pin(values):
+    return lax.optimization_barrier(values)
+
+
 def after(value, *others):
-    return lax.optimization_barrier((value,) + others)[0]
+    return pin((value,) + others)[0]
 
 
 def flip(value, bit):
@@ -127,6 +131,13 @@
     return parts[0]
 
 
+def plane_gather_spare(value):
+    if lax.axis_size("tensor") != 4:
+        return plane_gather(value)
+    one, two = flip(value, 1), flip(value, 2)
+    return [value, one, two, flip(one, 2)]
+
+
 def ring_order(chips):
     odd = list(range(1, chips, 2))
     even = list(range(2, chips, 2))
@@ -232,20 +243,6 @@
         if step == 0:
             return here
         total = ring_next(here.astype(NARROW))
-
-
-def sum_over_dp(vector):
-    both = vector + swap_core(vector)
-    chips = lax.axis_size("dp") // 2
-    held = [both]
-    for _ in range(chips - 1):
-        held.append(ring_next(held[-1]))
-    stacked = jnp.stack(held)
-    places = jnp.stack(ring_chips())
-    ordered = [
-        jnp.sum(jnp.where((places == chip)[:, None], stacked, 0.0), axis=0) for chip in range(chips)
-    ]
-    return sum(ordered[1:], ordered[0])
 
 
 def sum_over_plane(vector):
@@ -283,34 +280,64 @@
     ]
 
 
-def forward_body(rows, count, places, blocks, *refs):
+def piece_moves(moves, piece_rows):
+    found = []
+    for block, at, size, place in moves:
+        first = 0
+        for piece, (owner, rows) in enumerate(piece_rows):
+            if owner != block:
+                continue
+            low, high = max(at, first), min(at + size, first + rows)
+            if low < high:
+                found.append((piece, low - first, high - low, place + low - at))
+            first += rows
+    return found
+
+
+def flat_pieces(weights):
+    pieces = [piece for blocks in weights for block in blocks for piece in block]
+    rows = [
+        [(b, piece.shape[0]) for b, block in enumerate(blocks) for piece in block]
+        for blocks in weights
+    ]
+    return pieces, rows
+
+
+def column(mix):
+    return mix[...].T[:, :1]
+
+
+def forward_body(rows, count, places, piece_rows, *refs):
     x_refs, refs = refs[:count], refs[count:]
-    weights, refs = [refs[n * blocks : (n + 1) * blocks] for n in range(3)], refs[3 * blocks :]
+    weights = []
+    for held in piece_rows:
+        weights.append(refs[: len(held)])
+        refs = refs[len(held) :]
     mix_one, mix_two, router = refs[:3]
     out_refs, refs = refs[3 : 3 + count], refs[3 + count :]
-    gate_ref, up_ref, hidden_ref, factor_ref = refs[:4]
-    xs, gate_s, up_s, down_s, ys, gs, us, hs, sems = refs[4:]
+    kept_refs, factor_ref, refs = refs[:9], refs[9], refs[10:]
+    xs, gate_s, up_s, down_s, ys = refs[:5]
+    kept, sems = refs[5:14], refs[14]
     copies = Copies(sems)
     x_in = [copies.start(x_refs[i], xs.at[pl.ds(i * rows, rows)]) for i in range(count)]
     w_in = [
         [
             [
                 copies.start(weights[n][b].at[pl.ds(at, size)], held.at[pl.ds(place, size)])
-                for b, at, size, place in pieces
+                for b, at, size, place in piece_moves(moves, piece_rows[n])
             ]
             for n, held in enumerate((gate_s, up_s, down_s))
         ]
-        for _, _, pieces in places
+        for _, _, moves in places
     ]
     for copy in x_in:
         copy.wait()
     x = xs[...]
     router_gate = jax.nn.sigmoid(jnp.sum(x.astype(WIDE) * router[...], axis=1, keepdims=True))
     factor_ref[...] = router_gate
+    factors = (column(mix_one), column(mix_two), router_gate)
     total, away = None, []
-    for (start, size, _), arriving, factor in zip(
-        places, w_in, (mix_one[...], mix_two[...], router_gate)
-    ):
+    for at, ((start, size, _), arriving) in enumerate(zip(places, w_in)):
         span = pl.ds(start, size)
         for copy in arriving[0]:
             copy.wait()
@@ -318,40 +345,40 @@
         for copy in arriving[1]:
             copy.wait()
         up_in = dot_nt(x, up_s[span])
-        hidden = (gate_in * jax.nn.sigmoid(gate_in) * up_in * factor).astype(NARROW)
-        gs[:, start : start + size] = gate_in.astype(NARROW)
-        us[:, start : start + size] = up_in.astype(NARROW)
-        hs[:, start : start + size] = hidden
+        hidden = (gate_in * jax.nn.sigmoid(gate_in) * up_in * factors[at]).astype(NARROW)
+        for n, value in enumerate((gate_in, up_in, hidden)):
+            kept[3 * n + at][...] = value.astype(NARROW)
+            away.append(copies.start(kept[3 * n + at], kept_refs[3 * n + at]))
         for copy in arriving[2]:
             copy.wait()
         part = dot_nn(hidden, down_s[span])
         total = part if total is None else total + part
     ys[...] = total.astype(NARROW)
-    away = [copies.start(ys.at[pl.ds(i * rows, rows)], out_refs[i]) for i in range(count)]
-    away += [copies.start(gs, gate_ref), copies.start(us, up_ref), copies.start(hs, hidden_ref)]
+    away += [copies.start(ys.at[pl.ds(i * rows, rows)], out_refs[i]) for i in range(count)]
     for copy in away:
         copy.wait()
 
 
 def forward_step(x_blocks, weights, mix_one, mix_two, router, cut):
     count, (rows, width) = len(x_blocks), x_blocks[0].shape
-    blocks, parts = len(weights[0]), weights[0][0].shape[0]
+    pieces, piece_rows = flat_pieces(weights)
+    blocks, parts = len(weights[0]), sum(piece.shape[0] for piece in weights[0][0])
     places = weight_places(parts, blocks, cut)
     total, hidden = count * rows, blocks * parts
     anywhere, local = pl.BlockSpec(memory_space=pl.ANY), pl.BlockSpec(memory_space=pltpu.VMEM)
     shape = jax.ShapeDtypeStruct
     outs = pl.pallas_call(
-        functools.partial(forward_body, rows, count, places, blocks),
+        functools.partial(forward_body, rows, count, places, piece_rows),
         out_shape=[shape((rows, width), NARROW)] * count
-        + [shape((total, hidden), NARROW)] * 3
+        + [shape((total, size), NARROW) for _ in range(3) for _, size, _ in places]
         + [shape((total, 1), WIDE)],
-        in_specs=[anywhere] * (count + 3 * blocks) + [local] * 3,
-        out_specs=[anywhere] * (count + 3) + [local],
+        in_specs=[anywhere] * (count + len(pieces)) + [local] * 3,
+        out_specs=[anywhere] * (count + 9) + [local],
         scratch_shapes=[pltpu.VMEM((total, width), NARROW)]
         + [pltpu.VMEM((hidden, width), NARROW)] * 3
         + [pltpu.VMEM((total, width), NARROW)]
-        + [pltpu.VMEM((total, hidden), NARROW)] * 3
-        + [pltpu.SemaphoreType.DMA((2 * count + 6 * blocks + 3,))],
+        + [pltpu.VMEM((total, size), NARROW) for _ in range(3) for _, size, _ in places]
+        + [pltpu.SemaphoreType.DMA((2 * count + 3 * len(pieces) + 9,))],
         compiler_params=pltpu.CompilerParams(vmem_limit_bytes=VMEM_BYTES),
         cost_estimate=pl.CostEstimate(
             flops=6 * total * hidden * width,
@@ -359,54 +386,59 @@
             transcendentals=total * hidden,
         ),
         name="ffn_forward",
-    )(*x_blocks, *[w for held in weights for w in held], mix_one, mix_two, router)
-    return outs[:count], outs[count], outs[count + 1], outs[count + 2], outs[count + 3]
-
-
-def backward_body(rows, count, places, blocks, *refs):
+    )(*x_blocks, *pieces, mix_one, mix_two, router)
+    outs, kept = outs[:count], outs[count:]
+    return outs, kept[:3], kept[3:6], kept[6:9], kept[9]
+
+
+def backward_body(rows, count, places, piece_rows, *refs):
     g_refs, refs = refs[:count], refs[count:]
-    weights, refs = [refs[n * blocks : (n + 1) * blocks] for n in range(3)], refs[3 * blocks :]
-    (gate_ref, up_ref, mix_one, mix_two, rg, router), refs = refs[:6], refs[6:]
-    out_refs, refs = refs[:count], refs[count:]
-    gate_out, up_out, logit_ref = refs[:3]
-    xs, gate_s, up_s, down_s, ys, gs, us, sems = refs[3:]
+    weights = []
+    for held in piece_rows:
+        weights.append(refs[: len(held)])
+        refs = refs[len(held) :]
+    kept_refs, refs = refs[:6], refs[6:]
+    mix_one, mix_two, rg, router = refs[:4]
+    out_refs, refs = refs[4 : 4 + count], refs[4 + count :]
+    grad_refs, logit_ref, refs = refs[:6], refs[6], refs[7:]
+    xs, gate_s, up_s, down_s, ys = refs[:5]
+    kept, sems = refs[5:11], refs[11]
     copies = Copies(sems)
     g_in = [copies.start(g_refs[i], xs.at[pl.ds(i * rows, rows)]) for i in range(count)]
-    w_in, kept = [], []
-    for start, size, pieces in places:
-        arriving = [
-            [
-                copies.start(weights[n][b].at[pl.ds(at, n_rows)], held.at[pl.ds(place, n_rows)])
-                for b, at, n_rows, place in pieces
-            ]
-            for n, held in ((2, down_s), (0, gate_s), (1, up_s))
-        ]
+    w_in, kept_in = [], []
+    for at, (start, size, moves) in enumerate(places):
+        arriving = []
+        for n, held in ((2, down_s), (0, gate_s), (1, up_s)):
+            arriving.append(
+                [
+                    copies.start(weights[n][b].at[pl.ds(first, n_rows)], held.at[pl.ds(place, n_rows)])
+                    for b, first, n_rows, place in piece_moves(moves, piece_rows[n])
+                ]
+            )
+            if n == 2:
+                kept_in.append([copies.start(kept_refs[3 * i + at], kept[3 * i + at]) for i in range(2)])
         w_in.append(arriving)
-        if not kept:
-            kept = [copies.start(gate_ref, gs), copies.start(up_ref, us)]
     for copy in g_in:
         copy.wait()
     grad = xs[...]
-    total = None
-    for (start, size, _), arriving, factor in zip(
-        places, w_in, (mix_one[...], mix_two[...], rg[...])
-    ):
+    factors = (column(mix_one), column(mix_two), rg[...])
+    total, away = None, []
+    for at, ((start, size, _), arriving) in enumerate(zip(places, w_in)):
         span = pl.ds(start, size)
         for copy in arriving[0]:
             copy.wait()
-        grad_hidden = dot_nt(grad, down_s[span]) * factor
-        if total is None:
-            for copy in kept:
-                copy.wait()
-        gate_in = gs[:, start : start + size].astype(WIDE)
-        up_in = us[:, start : start + size].astype(WIDE)
+        grad_hidden = dot_nt(grad, down_s[span]) * factors[at]
+        for copy in kept_in[at]:
+            copy.wait()
+        gate_in, up_in = kept[at][...].astype(WIDE), kept[3 + at][...].astype(WIDE)
         squash = jax.nn.sigmoid(gate_in)
         up_grad = grad_hidden * gate_in * squash
         gate_grad = grad_hidden * up_in * squash * (1.0 + gate_in * (1.0 - squash))
         logit = jnp.sum(up_grad * up_in, axis=1, keepdims=True)
         gate_grad, up_grad = gate_grad.astype(NARROW), up_grad.astype(NARROW)
-        gs[:, start : start + size] = gate_grad
-        us[:, start : start + size] = up_grad
+        for n, value in enumerate((gate_grad, up_grad)):
+            kept[3 * n + at][...] = value
+            away.append(copies.start(kept[3 * n + at], grad_refs[3 * n + at]))
         for copy in arriving[1] + arriving[2]:
             copy.wait()
         part = dot_nn(gate_grad, gate_s[span]) + dot_nn(up_grad, up_s[span])
@@ -414,31 +446,31 @@
     logit = logit * (1.0 - rg[...])
     logit_ref[...] = logit
     ys[...] = (total + logit * router[...]).astype(NARROW)
-    away = [copies.start(ys.at[pl.ds(i * rows, rows)], out_refs[i]) for i in range(count)]
-    away += [copies.start(gs, gate_out), copies.start(us, up_out)]
+    away += [copies.start(ys.at[pl.ds(i * rows, rows)], out_refs[i]) for i in range(count)]
     for copy in away:
         copy.wait()
 
 
 def backward_step(g_blocks, weights, gate_in, up_in, mix_one, mix_two, rg, router, cut):
     count, (rows, width) = len(g_blocks), g_blocks[0].shape
-    blocks, parts = len(weights[0]), weights[0][0].shape[0]
+    pieces, piece_rows = flat_pieces(weights)
+    blocks, parts = len(weights[0]), sum(piece.shape[0] for piece in weights[0][0])
     places = weight_places(parts, blocks, cut)
     total, hidden = count * rows, blocks * parts
     anywhere, local = pl.BlockSpec(memory_space=pl.ANY), pl.BlockSpec(memory_space=pltpu.VMEM)
     shape = jax.ShapeDtypeStruct
     outs = pl.pallas_call(
-        functools.partial(backward_body, rows, count, places, blocks),
+        functools.partial(backward_body, rows, count, places, piece_rows),
         out_shape=[shape((rows, width), NARROW)] * count
-        + [shape((total, hidden), NARROW)] * 2
+        + [shape((total, size), NARROW) for _ in range(2) for _, size, _ in places]
         + [shape((total, 1), WIDE)],
-        in_specs=[anywhere] * (count + 3 * blocks + 2) + [local] * 4,
-        out_specs=[anywhere] * (count + 2) + [local],
+        in_specs=[anywhere] * (count + len(pieces) + 6) + [local] * 4,
+        out_specs=[anywhere] * (count + 6) + [local],
         scratch_shapes=[pltpu.VMEM((total, width), NARROW)]
         + [pltpu.VMEM((hidden, width), NARROW)] * 3
         + [pltpu.VMEM((total, width), NARROW)]
-        + [pltpu.VMEM((total, hidden), NARROW)] * 2
-        + [pltpu.SemaphoreType.DMA((2 * count + 6 * blocks + 4,))],
+        + [pltpu.VMEM((total, size), NARROW) for _ in range(2) for _, size, _ in places]
+        + [pltpu.SemaphoreType.DMA((2 * count + 3 * len(pieces) + 12,))],
         compiler_params=pltpu.CompilerParams(vmem_limit_bytes=VMEM_BYTES),
         cost_estimate=pl.CostEstimate(
             flops=6 * total * hidden * width,
@@ -448,111 +480,167 @@
         name="ffn_backward",
     )(
         *g_blocks,
-        *[w for held in weights for w in held],
-        gate_in,
-        up_in,
+        *pieces,
+        *gate_in,
+        *up_in,
         mix_one,
         mix_two,
         rg,
         router,
     )
-    return outs[:count], outs[count], outs[count + 1], outs[count + 2]
-
-
-def weight_body(rows, steps, blocks, places, tiles, parts, *refs):
-    x_refs, refs = refs[: steps * blocks], refs[steps * blocks :]
-    left_refs, refs = refs[:steps], refs[steps:]
-    mine_ref, other_ref, xs, ls, os, sems = refs
+    outs, kept = outs[:count], outs[count:]
+    return outs, kept[:3], kept[3:6], kept[6]
+
+
+def weight_body(rows, steps, blocks, shape, splits, apart, *refs):
+    groups, names = len(shape), sum(shape)
+    x_refs, refs = refs[: groups * steps * blocks], refs[groups * steps * blocks :]
+    left_refs, refs = refs[: names * steps], refs[names * steps :]
+    out_refs, refs = refs[:splits], refs[splits:]
+    xs, ls, os, sems = refs
     copies = Copies(sems)
-    part = blocks * rows
-    arrived = []
-    for s in range(steps):
-        for i in range(blocks):
-            place = pl.ds((s * blocks + i) * rows, rows)
-            arrived.append(copies.start(x_refs[s * blocks + i], xs.at[place]))
-        arrived.append(copies.start(left_refs[s], ls.at[pl.ds(s * part, part)]))
-    for copy in arrived:
-        copy.wait()
-    moves = [
-        (place, n_rows, b, at)
-        for _, _, chunk in places
-        for b, at, n_rows, place in chunk
-    ]
-    half = (1 + max(b for _, _, b, _ in moves)) // 2
-    away, ready = [], 0
-    for start, size in tiles:
-        os[pl.ds(start, size)] = dot_tn(ls[:, start : start + size], xs[...]).astype(NARROW)
-        for at, n_rows, b, offset in moves:
-            if ready < at + n_rows <= start + size:
-                target = mine_ref if b < half else other_ref
-                goal = target.at[pl.ds((b % half) * parts + offset, n_rows)]
-                away.append(copies.start(os.at[pl.ds(at, n_rows)], goal))
-        ready = start + size
+    part, hidden = blocks * rows, os.shape[1]
+    x_in, left_in, n = [], [], 0
+    for group, amount in enumerate(shape):
+        arriving = []
+        for i in range(steps * blocks):
+            source = x_refs[group * steps * blocks + i]
+            arriving.append(copies.start(source, xs.at[group, pl.ds(i * rows, rows)]))
+        x_in.append(arriving)
+        for _ in range(amount):
+            left_in.append(
+                [
+                    copies.start(left_refs[n * steps + s], ls.at[n, pl.ds(s * part, part)])
+                    for s in range(steps)
+                ]
+            )
+            n += 1
+    away, n = [], 0
+    size = hidden // splits
+    for group, amount in enumerate(shape):
+        for copy in x_in[group]:
+            copy.wait()
+        for _ in range(amount):
+            for copy in left_in[n]:
+                copy.wait()
+            os[n] = dot_tn(ls[n], xs[group]).astype(NARROW)
+            if apart:
+                away.append(copies.start(os.at[n], out_refs[n]))
+            else:
+                for j in range(splits):
+                    target = out_refs[j].at[pl.ds(n * size, size)]
+                    away.append(copies.start(os.at[n, pl.ds(j * size, size)], target))
+            n += 1
     for copy in away:
         copy.wait()
 
 
-def weight_grads(x_blocks, lefts, parts, cut, blocks_of):
-    steps, blocks = len(x_blocks), len(x_blocks[0])
-    rows, width = x_blocks[0][0].shape
-    total, hidden = steps * blocks * rows, lefts[0].shape[1]
-    places = weight_places(parts, blocks_of, cut)
-    tiles = [(at, min(512, hidden - at)) for at in range(0, hidden, 512)]
+def weight_grads(groups, splits, apart=False, light=False):
+    steps, blocks = len(groups[0][0]), len(groups[0][0][0])
+    shape = [len(lefts) for _, lefts in groups]
+    names = sum(shape)
+    rows, width = groups[0][0][0][0].shape
+    total, hidden = steps * blocks * rows, groups[0][1][0][0].shape[1]
     anywhere = pl.BlockSpec(memory_space=pl.ANY)
-    return pl.pallas_call(
-        functools.partial(weight_body, rows, steps, blocks, places, tiles, parts),
-        out_shape=[jax.ShapeDtypeStruct((hidden // 2, width), NARROW)] * 2,
-        in_specs=[anywhere] * (steps * (blocks + 1)),
-        out_specs=[anywhere] * 2,
+    outs = pl.pallas_call(
+        functools.partial(weight_body, rows, steps, blocks, shape, splits, apart),
+        out_shape=[jax.ShapeDtypeStruct((names * hidden // splits, width), NARROW)] * splits,
+        in_specs=[anywhere] * (steps * (len(groups) * blocks + names)),
+        out_specs=[anywhere] * splits,
         scratch_shapes=[
-            pltpu.VMEM((total, width), NARROW),
-            pltpu.VMEM((total, hidden), NARROW),
-            pltpu.VMEM((hidden, width), NARROW),
-            pltpu.SemaphoreType.DMA((steps * (blocks + 1) + 2 * blocks_of,)),
+            pltpu.VMEM((len(groups), total, width), NARROW),
+            pltpu.VMEM((names, total, hidden), NARROW),
+            pltpu.VMEM((names, hidden, width), NARROW),
+            pltpu.SemaphoreType.DMA((steps * (len(groups) * blocks + names) + names * splits,)),
         ],
         compiler_params=pltpu.CompilerParams(vmem_limit_bytes=VMEM_BYTES),
         cost_estimate=pl.CostEstimate(
-            flops=2 * total * hidden * width,
-            bytes_accessed=2 * total * width + 2 * (total + width) * hidden,
+            flops=0 if light else 2 * names * total * hidden * width,
+            bytes_accessed=0 if light else 2 * total * width + 2 * names * (total + width) * hidden,
             transcendentals=0,
         ),
         name="weight_grads",
-    )(*[b for step in x_blocks for b in step], *lefts)
-
-
-def assemble_body(count, splits, *refs):
-    places, blocks, outs = refs[0], refs[1 : 1 + count], refs[1 + count : 1 + count + splits]
-    held, sems = refs[1 + count + splits :]
-    rows = blocks[0].shape[0]
+    )(
+        *[b for x_blocks, _ in groups for step in x_blocks for b in step],
+        *[a for _, lefts in groups for left in lefts for a in left],
+    )
+    return list(outs)
+
+
+def attention_body(piece, order, normed, grads, hidden, mixed, mine_ref, other_ref):
+    width = mixed.shape[1]
+    half = mine_ref.shape[0]
+    for i in range(2 * half):
+        target = mine_ref if i < half else other_ref
+        span = pl.ds(pl.multiple_of(order[i] * piece, 128), piece)
+        target[i % half, :, : 3 * width] = dot_tn(normed[:, span], grads[...]).astype(NARROW)
+        target[i % half, :, 3 * width :] = dot_tn(hidden[:, span], mixed[...]).astype(NARROW)
+
+
+def attention_grads(order, normed, grads, hidden, mixed):
+    count = order.shape[0]
+    group, depth = normed.shape
+    width = mixed.shape[1]
+    piece = depth // count
+    local = pl.BlockSpec(memory_space=pltpu.VMEM)
+    return pl.pallas_call(
+        functools.partial(attention_body, piece),
+        out_shape=[jax.ShapeDtypeStruct((count // 2, piece, 4 * width), NARROW)] * 2,
+        in_specs=[pl.BlockSpec(memory_space=pltpu.SMEM)] + [local] * 4,
+        out_specs=[local] * 2,
+        compiler_params=pltpu.CompilerParams(vmem_limit_bytes=VMEM_BYTES),
+        cost_estimate=pl.CostEstimate(
+            flops=8 * group * depth * width,
+            bytes_accessed=4 * group * depth + 8 * group * width + 8 * depth * width,
+            transcendentals=0,
+        ),
+        name="attention_grads",
+    )(order, normed, grads, hidden, mixed)
+
+
+def assemble_body(count, rows, *refs):
+    places, blocks, refs = refs[0], refs[1 : 1 + count], refs[1 + count :]
+    outs, (held, straight, turned, sems) = refs[-8:-4], refs[-4:]
     copies = Copies(sems)
+    width = straight.shape[3]
     moved = []
     for i in range(count):
-        place = pl.multiple_of(places[i], rows)
-        moved.append(copies.start(blocks[i], held.at[pl.ds(place, rows)]))
-    for copy in moved:
+        moved.append(copies.start(blocks[i].at[pl.ds(0, rows)], held.at[i]))
+    away = []
+    for i in range(count):
+        moved[i].wait()
+        place = pl.multiple_of(places[i], 128)
+        for j in range(3):
+            straight[i, j] = held[i, :, j * width : (j + 1) * width].astype(WIDE)
+            away.append(copies.start(straight.at[i, j], outs[j].at[pl.ds(place, rows)]))
+        turned[i] = held[i, :, 3 * width :].astype(WIDE).T
+        away.append(copies.start(turned.at[i], outs[3].at[:, pl.ds(place, rows)]))
+    for copy in away:
         copy.wait()
-    width = held.shape[1] // splits
-    for j in range(splits):
-        outs[j][...] = held[:, j * width : (j + 1) * width].astype(WIDE)
-
-
-def assemble(blocks, places, splits):
-    count, (rows, width) = len(blocks), blocks[0].shape
-    shape = jax.ShapeDtypeStruct((count * rows, width // splits), WIDE)
-    local = pl.BlockSpec(memory_space=pltpu.VMEM)
+
+
+def assemble(blocks, places, rows, before):
+    count, wide = len(blocks), blocks[0].shape[1]
+    width = wide // 4
+    depth = D
+    shapes = [jax.ShapeDtypeStruct((depth, width), WIDE)] * 3
+    anywhere = pl.BlockSpec(memory_space=pl.ANY)
+    before = [] if before is None else list(before)
     return pl.pallas_call(
-        functools.partial(assemble_body, count, splits),
-        out_shape=[shape] * splits,
-        in_specs=[pl.BlockSpec(memory_space=pltpu.SMEM)]
-        + [pl.BlockSpec(memory_space=pl.ANY)] * count,
-        out_specs=[local] * splits,
+        functools.partial(assemble_body, count, rows),
+        out_shape=shapes + [jax.ShapeDtypeStruct((width, depth), WIDE)],
+        in_specs=[pl.BlockSpec(memory_space=pltpu.SMEM)] + [anywhere] * (count + len(before)),
+        out_specs=[anywhere] * 4,
         scratch_shapes=[
-            pltpu.VMEM((count * rows, width), NARROW),
-            pltpu.SemaphoreType.DMA((count,)),
+            pltpu.VMEM((count, rows, wide), NARROW),
+            pltpu.VMEM((count, 3, rows, width), WIDE),
+            pltpu.VMEM((count, width, rows), WIDE),
+            pltpu.SemaphoreType.DMA((5 * count,)),
         ],
+        input_output_aliases={1 + count + i: i for i in range(len(before))},
         compiler_params=pltpu.CompilerParams(vmem_limit_bytes=VMEM_BYTES),
         name="assemble",
-    )(places, *blocks)
+    )(places, *blocks, *before)
 
 
 def turn_body(x_ref, out_ref):
@@ -628,8 +716,7 @@
     own_input = hidden_in.astype(wide)
     inverse_one = lax.rsqrt(jnp.mean(own_input * own_input, axis=1, keepdims=True) + EPSILON)
     hat_one = own_input * inverse_one
-    normed_one_blocks = plane_gather((hat_one * attn_gain).astype(narrow))
-    normed_one = jnp.concatenate(normed_one_blocks, axis=0)
+    normed_own = (hat_one * attn_gain).astype(narrow)
 
     def pack(expert_rows, shared_rows):
         if f_pad != f_shared:
@@ -648,9 +735,19 @@
     def both_cores(blocks):
         return blocks + [swap_core(block) for block in blocks]
 
-    own_gate, own_up, normed_one = lax.optimization_barrier((own_gate, own_up, normed_one))
+    staged = n_tensor == 4 and n_dp == 8
+    if staged:
+        cut = split_at(own_down.shape[0])
+        low = flip((expert_down[0] if cut <= f_expert else own_down)[:cut], w_bits[0])
+        one, two = flip(normed_own, 1), flip(normed_own, 2)
+        one, two, low, own_gate, own_down = pin((one, two, low, own_gate, own_down))
+        normed_one_blocks = [normed_own, one, two, flip(one, 2)]
+        high = flip(own_down[cut:], w_bits[0])
+    else:
+        normed_one_blocks = plane_gather(normed_own)
+        high = own_down
     gate_blocks = bits_gather(own_gate, w_bits)
-    up_blocks = bits_gather(own_up, w_bits)
+    normed_one = jnp.concatenate(normed_one_blocks, axis=0)
 
     row_slices = [slice_index ^ offset for offset in bits_offsets(r_bits)]
     mixing = jnp.sum(
@@ -674,7 +771,8 @@
             [jnp.sum(jnp.where((slices == at)[None, :, None], chosen, 0.0), axis=1) for at in row_slices],
             axis=1,
         )
-        return chosen.reshape(-1, len(row_slices) * rows, 1)
+        chosen = chosen.reshape(-1, 1, len(row_slices) * rows)
+        return jnp.broadcast_to(chosen, (chosen.shape[0], 8, chosen.shape[2]))
 
     mix_one, mix_two = mixing_of(data_index), mixing_of(data_index ^ 1)
 
@@ -691,25 +789,54 @@
     probs_low = (expo / total_expo).astype(narrow)
     mixed = jnp.einsum("hts,shd->thd", probs_low, value_low, preferred_element_type=wide)
     mixed_low = mixed.reshape(GROUP, heads * HD).astype(narrow)
-    mixed_low = after(mixed_low, *gate_blocks, *up_blocks)
+    own_swaps = [swap_core(own) for own in (own_gate, own_up, own_down)]
+    mix_one, mix_two = ([mix[i] for i in range(n_dp // 2)] for mix in (mix_one, mix_two))
+    mixed_low, mix_one, mix_two, own_swaps = pin((mixed_low, mix_one, mix_two, own_swaps))
     head_part = dot_nn(mixed_low, o_weight).astype(narrow)
-    attn_own = plane_scatter([head_part[j * rows : (j + 1) * rows] for j in range(n_tensor)])
-
-    attn_own, own_down = lax.optimization_barrier((attn_own, own_down))
-    down_blocks = bits_gather(own_down, w_bits)
+    parts = [head_part[j * rows : (j + 1) * rows] for j in range(n_tensor)]
+    if n_tensor == 4:
+        far = [flip(part, 2) for part in parts[2:]]
+        near = (parts[1].astype(wide) + far[1].astype(wide)).astype(narrow)
+        near, gate_blocks, own_up, high = pin((near, gate_blocks, own_up, high))
+        attn_own = parts[0].astype(wide) + far[0].astype(wide) + flip(near, 1).astype(wide)
+    else:
+        attn_own = plane_scatter(parts)
+
     hidden_mid = own_input + attn_own
     inverse_two = lax.rsqrt(jnp.mean(hidden_mid * hidden_mid, axis=1, keepdims=True) + EPSILON)
     hat_two = hidden_mid * inverse_two
     normed_two = (hat_two * mlp_gain).astype(narrow)
-
-    weights = [both_cores(blocks) for blocks in (gate_blocks, up_blocks, down_blocks)]
+    chips = n_dp // 2
+    x_chain = [normed_two, ring_next(normed_two)]
+    x_steps = [bits_gather(normed_two, r_bits)]
+    if staged:
+        up_low = flip(own_up[:cut], w_bits[0])
+        x_chain[1], x_steps, own_up = pin((x_chain[1], x_steps, own_up))
+        x_chain.append(ring_next(x_chain[1]))
+        x_steps.append(bits_gather(x_chain[1], r_bits))
+        up_high = flip(own_up[cut:], w_bits[0])
+        x_chain[2], x_steps = pin((x_chain[2], x_steps))
+        x_chain.append(ring_next(x_chain[2]))
+        x_steps.append(bits_gather(x_chain[2], r_bits))
+        x_steps.append(bits_gather(x_chain[3], r_bits))
+        arrived = ([gate_blocks[1]], [up_low, up_high], [low, high])
+        weights = [
+            [[own], pieces, [swapped], [swap_core(piece) for piece in pieces]]
+            for own, pieces, swapped in zip((own_gate, own_up, own_down), arrived, own_swaps)
+        ]
+    else:
+        while len(x_chain) < chips:
+            x_chain.append(ring_next(x_chain[-1]))
+        x_steps += [bits_gather(block, r_bits) for block in x_chain[1:]]
+        up_blocks, down_blocks = bits_gather(own_up, w_bits), bits_gather(own_down, w_bits)
+        weights = [
+            [[block] for block in blocks + [swapped] + [swap_core(block) for block in blocks[1:]]]
+            for blocks, swapped in zip((gate_blocks, up_blocks, down_blocks), own_swaps)
+        ]
     n_blocks, n_hidden = len(weights[0]), len(weights[0]) // 2
     places = weight_places(f_expert + f_shared, n_blocks, f_expert)
 
     router_row = shared_router.astype(wide)[None]
-    x_chain = chain_gather(normed_two)
-    chips = len(x_chain)
-    x_steps = [bits_gather(block, r_bits) for block in x_chain]
     forward, out_sums, total = {}, {}, None
     order = list(range(1, chips)) + [0]
     for place, step in enumerate(order):
@@ -749,24 +876,42 @@
     )
     grad_own = result_grad.astype(narrow)
 
+    def core_parts(mine, other, first, size):
+        return [
+            mine[first + j * size : first + (j + 1) * size].astype(wide)
+            + other[first + j * size : first + (j + 1) * size].astype(wide)
+            for j in range(n_hidden)
+        ]
+
+    def shared_parts(mine, other, which):
+        both = core_parts(mine, other, which * n_hidden * f_pad, f_pad)
+        return [both[0]] + [part.astype(narrow) for part in both[1:]]
+
+    def shared_sum(parts):
+        return bits_scatter(parts, w_bits)[:f_shared].astype(narrow)
+
+    def expert_sum(mine, other):
+        return bits_scatter(core_parts(mine, other, 0, f_expert), w_bits)
+
+    hidden_of = [[forward[step][3][part] for step in range(chips)] for part in range(3)]
     g_chain = chain_gather(grad_own)
     g_steps = [bits_gather(block, r_bits) for block in g_chain]
     backward, dx_sums, total = [], {}, None
     for step in range(chips):
-        g, ready = g_steps[step], []
+        ready = []
         if step + 1 < chips:
             ready.append(g_chain[step + 1])
         if step >= 1:
-            ready += list(backward[step - 1][0])
+            ready.append(backward[step - 1][0])
         if step >= 2:
             dx_sums[step - 2] = bits_scatter(backward[step - 2][0], r_bits)
             ready.append(dx_sums[step - 2])
-        flat = list(lax.optimization_barrier((*g, *ready)))
+        g, ready = pin((g_steps[step], ready))
         if step >= 2:
-            dx_sums[step - 2] = flat[-1]
+            dx_sums[step - 2] = ready[2 if step + 1 < chips else 1]
         backward.append(
             backward_step(
-                flat[: len(g)],
+                g,
                 weights,
                 forward[step][1],
                 forward[step][2],
@@ -777,53 +922,36 @@
                 f_expert,
             )
         )
-    gate_grads = [item[1] for item in backward]
-    up_grads = [item[2] for item in backward]
-    hidden_steps = [forward[step][3] for step in range(chips)]
-
-    def core_sum(mine, other):
-        return (mine.astype(wide) + swap_core(other).astype(wide)).astype(narrow)
-
-    def shared_part(both):
-        size = f_expert + f_pad
-        own = bits_scatter(
-            [both[j * size + f_expert : (j + 1) * size] for j in range(n_hidden)], w_bits
-        )
-        return own[:f_shared].astype(narrow)
-
-    def expert_part(both):
-        size = f_expert + f_pad
-        return bits_scatter([both[j * size : j * size + f_expert] for j in range(n_hidden)], w_bits)
-
-    def held_until(steps, *others):
-        count = len(steps[0])
-        flat = lax.optimization_barrier((*[b for blocks in steps for b in blocks], *others))
-        blocks = flat[: count * len(steps)]
-        held = [list(blocks[i * count : (i + 1) * count]) for i in range(len(steps))]
-        return held, flat[count * len(steps) :]
-
-    total = None
+    gate_of, up_of = (
+        [[backward[step][n][part] for step in range(chips)] for part in range(3)] for n in (1, 2)
+    )
     for step in range(1, chips - 2):
         here = dx_sums[step].astype(wide)
         total = ring_next((here if total is None else here + total.astype(wide)).astype(narrow))
     dx_sums[chips - 2] = bits_scatter(backward[chips - 2][0], r_bits)
-    held, (dx_sums[chips - 2], total, *_) = held_until(
-        g_steps, dx_sums[chips - 2], total, *backward[-1][0]
-    )
-    down_full = weight_grads(held, hidden_steps, f_expert + f_pad, f_expert, n_blocks)
+    x_steps, g_steps, dx_sums[chips - 2], total, _ = pin(
+        (x_steps, g_steps, dx_sums[chips - 2], total, backward[-1][0])
+    )
+    shared_mine, shared_other = weight_grads(
+        [(g_steps, [hidden_of[2]]), (x_steps, [gate_of[2], up_of[2]])], 2
+    )
     total = ring_next((dx_sums[chips - 2].astype(wide) + total.astype(wide)).astype(narrow))
     dx_sums[chips - 1] = bits_scatter(backward[chips - 1][0], r_bits)
-    held, (dx_sums[chips - 1], total, *down_full) = held_until(
-        x_steps, dx_sums[chips - 1], total, *down_full
-    )
-    gate_full = weight_grads(held, gate_grads, f_expert + f_pad, f_expert, n_blocks)
-    total = ring_next((dx_sums[chips - 1].astype(wide) + total.astype(wide)).astype(narrow))
+    g_steps, dx_sums[chips - 1], total, shared_mine, shared_other = pin(
+        (g_steps, dx_sums[chips - 1], total, shared_mine, shared_other)
+    )
+    here = (dx_sums[chips - 1].astype(wide) + total.astype(wide)).astype(narrow)
+    here, g_steps = pin((here, g_steps))
+    total = ring_next(here)
+    (down_other,) = weight_grads([(g_steps, hidden_of[1:2])], 1, light=True)
+    g_steps, down_other, shared_other = pin((g_steps, down_other, shared_other))
+    shared_other = swap_core(shared_other)
+    (down_mine,) = weight_grads([(g_steps, hidden_of[:1])], 1, light=True)
+    shared_mine, shared_other, down_mine, down_other = pin(
+        (shared_mine, shared_other, down_mine, down_other)
+    )
+    shared_down_own = shared_sum(shared_parts(shared_mine, shared_other, 0))
     normed_two_grad = dx_sums[0].astype(wide) + total.astype(wide)
-    down_both = core_sum(*down_full)
-    held, (normed_two_grad, down_both, *gate_full) = held_until(
-        x_steps, normed_two_grad, down_both, *gate_full
-    )
-    up_full = weight_grads(held, up_grads, f_expert + f_pad, f_expert, n_blocks)
 
     grad_wide = grad_own.astype(wide)
     mlp_gain_part = jnp.sum(normed_two_grad * hat_two, axis=0)
@@ -838,28 +966,26 @@
     )
     own_low = hidden_grad.astype(narrow)
     if n_tensor == 4:
-        cut = split_at(rows)
+        own_low, x_steps, shared_down_own = pin((own_low, x_steps, shared_down_own))
         one, two = flip(own_low, 1), flip(own_low, 2)
-        one, two, down_both, *up_full = lax.optimization_barrier((one, two, down_both, *up_full))
-        low, high = flip(two[:cut], 1), flip(one[cut:], 2)
-        shared_down_own = shared_part(down_both)
-        grad_blocks = [own_low, one, two, low, high]
+        gate_experts = weight_grads([(x_steps, gate_of[:2])], 2, True)
+        one, two, gate_experts, shared_mine, shared_other = pin(
+            (one, two, gate_experts, shared_mine, shared_other)
+        )
+        grad_blocks = [own_low, one, two, flip(one, 2)]
     else:
-        shared_down_own = shared_part(down_both)
+        gate_experts = weight_grads([(x_steps, gate_of[:2])], 2, True)
         grad_blocks = plane_gather(own_low)
+    down_experts = [down_mine, down_other]
+    shared_down_all = lax.all_gather(shared_down_own, "dp", axis=0, tiled=True)
+    shared_gate_own = shared_sum(shared_parts(shared_mine, shared_other, 1))
+    grad_blocks, gate_experts, shared_gate_own, shared_mine, shared_other = pin(
+        (grad_blocks, gate_experts, shared_gate_own, shared_mine, shared_other)
+    )
+    shared_gate_all = lax.all_gather(shared_gate_own, "dp", axis=0, tiled=True)
+    shared_up_own = shared_sum(shared_parts(shared_mine, shared_other, 2))
     hidden_grad_low = jnp.concatenate(grad_blocks, axis=0)
-    gate_both = core_sum(*gate_full)
-    hidden_grad_low, shared_down_own, gate_both = lax.optimization_barrier(
-        (hidden_grad_low, shared_down_own, gate_both)
-    )
-    shared_down_all = lax.all_gather(shared_down_own, "dp", axis=0, tiled=True)
-    shared_gate_own = shared_part(gate_both)
-    up_both = core_sum(*up_full)
-
-    o_grad = dot_tn(mixed_low, hidden_grad_low)
-    o_grad, shared_gate_own, up_both = lax.optimization_barrier((o_grad, shared_gate_own, up_both))
-    shared_gate_all = lax.all_gather(shared_gate_own, "dp", axis=0, tiled=True)
-    shared_up_own = shared_part(up_both)
+
     mixed_grad = dot_nt(hidden_grad_low, o_weight).astype(narrow).reshape(GROUP, heads, HD)
     scores_again = attention_scores(query_low, key_low, visible, scale)
     probs = jnp.exp(scores_again - log_total)
@@ -875,23 +1001,43 @@
     key_grad = (
         jnp.einsum("hts,thd->shd", scores_grad, query_low, preferred_element_type=wide) * scale
     )
+    query_grad, shared_up_own, down_experts, gate_experts = pin(
+        (query_grad, shared_up_own, down_experts, gate_experts)
+    )
+    shared_up_all = lax.all_gather(shared_up_own, "dp", axis=0, tiled=True)
+    for experts_of in (down_experts, gate_experts):
+        experts_of[1] = swap_core(experts_of[1])
     query_lin_grad = rotate_back(query_grad, cosine, sine).reshape(GROUP, heads * HD).astype(narrow)
     key_lin_grad = rotate_back(key_grad, cosine, sine).reshape(GROUP, heads * HD).astype(narrow)
     value_lin_grad = value_grad.reshape(GROUP, heads * HD).astype(narrow)
-    expert_gate_own, expert_up_own, expert_down_own = (
-        expert_part(both) for both in (gate_both, up_both, down_both)
-    )
-    expert_down_grad = expert_down_own[None]
-    expert_gate_grad = expert_gate_own.T[None]
-    expert_up_grad = expert_up_own.T[None]
-    query_lin_grad, shared_up_own, _ = lax.optimization_barrier(
-        (query_lin_grad, shared_up_own, expert_down_own)
-    )
-    shared_up_all = lax.all_gather(shared_up_own, "dp", axis=0, tiled=True)
-    norm_one_part = (
-        dot_nt(query_lin_grad, q_weight)
-        + dot_nt(key_lin_grad, k_weight)
-        + dot_nt(value_lin_grad, v_weight)
+    width = heads * HD
+    piece = D // n_dp
+    sources = ring_sources()
+    ring_places = ring_chips()
+    lin_grads = jnp.concatenate([query_lin_grad, key_lin_grad, value_lin_grad], axis=1)
+    attn_mine, attn_other = attention_grads(
+        jnp.stack([at[0] for at in sources] + [at[1] for at in sources]).astype(jnp.int32),
+        normed_one,
+        lin_grads,
+        hidden_grad_low,
+        mixed_low,
+    )
+    attn_other = swap_core(attn_other)
+    attn_other, lin_grads, x_steps = pin((attn_other, lin_grads, x_steps))
+
+    def attn_part(step):
+        return attn_mine[step].astype(wide) + attn_other[step].astype(wide)
+
+    here, x_steps = pin((attn_part(1).astype(narrow), x_steps))
+    total = ring_next(here)
+    up_experts = weight_grads([(x_steps, up_of[:2])], 2, True)
+    up_experts[1] = swap_core(up_experts[1])
+    total, up_experts, down_experts, gate_experts = pin(
+        (total, up_experts, down_experts, gate_experts)
+    )
+    norm_one_part = sum(
+        dot_nt(lin_grads[:, i * width : (i + 1) * width], weight)
+        for i, weight in enumerate((q_weight, k_weight, v_weight))
     ).astype(narrow)
     normed_one_grad = plane_scatter(
         [norm_one_part[j * rows : (j + 1) * rows] for j in range(n_tensor)]
@@ -902,53 +1048,8 @@
         scaled_one - hat_one * jnp.mean(scaled_one * hat_one, axis=1, keepdims=True)
     )
 
-    width = heads * HD
-
-    sources = ring_sources()
-    ring_places = ring_chips()
-
-    def dp_sum(full, scatter_ties=(), gather_ties=()):
-        piece = full.shape[0] // n_dp
-        core = data_index % 2
-        by_core = full.reshape(chips, 2, piece, full.shape[1])
-        mine = lax.dynamic_index_in_dim(by_core, core, 1, keepdims=False)
-        other = lax.dynamic_index_in_dim(by_core, 1 - core, 1, keepdims=False)
-        both = (mine.astype(wide) + swap_core(other).astype(wide)).astype(narrow)
-        parts = [lax.dynamic_index_in_dim(both, at, 0, keepdims=False) for at in ring_places]
-
-        def tie(value, ties, step):
-            return after(value, *ties[step]) if step < len(ties) else value
-
-        total = tie(ring_next(parts[1]), scatter_ties, 0)
-        for step in range(2, chips):
-            total = ring_next((parts[step].astype(wide) + total.astype(wide)).astype(narrow))
-            total = tie(total, scatter_ties, step - 1)
-        held = [(parts[0].astype(wide) + total.astype(wide)).astype(narrow)]
-        for step in range(chips - 1):
-            held.append(tie(ring_next(held[-1]), gather_ties, step))
-        blocks, places = [], []
-        for block, at in zip(held, sources):
-            blocks += [block, swap_core(block)]
-            places += [source * piece for source in at]
-        return blocks, jnp.stack(places)
-
-    o_blocks, o_places = dp_sum(o_grad.astype(narrow))
-    (o_sum,) = assemble(o_blocks, o_places, 1)
-    qkv_grad = dot_tn(
-        normed_one, jnp.concatenate([query_lin_grad, key_lin_grad, value_lin_grad], axis=1)
-    ).astype(narrow)
-    shared_down_grad = shared_down_all.astype(wide)
-    shared_gate_grad = turn(shared_gate_all)
-    shared_up_grad = turn(shared_up_all)
-    qkv_blocks, qkv_places = dp_sum(
-        qkv_grad,
-        ((shared_down_grad, expert_gate_grad), (shared_gate_grad,), (expert_up_grad, input_grad)),
-        ((shared_up_grad,), (o_sum,)),
-    )
-    q_sum, k_sum, v_sum = assemble(qkv_blocks, qkv_places, 3)
-
-    gains = sum_over_plane(
-        jnp.concatenate(
+    def small_rows():
+        gains = jnp.concatenate(
             [
                 attn_gain_part,
                 mlp_gain_part,
@@ -956,17 +1057,55 @@
                 jnp.broadcast_to(squared_own, (128,)),
             ]
         )
-    )
-    small = sum_over_dp(
-        jnp.concatenate(
-            [
-                gains,
-                jnp.sum(query_lin_grad.astype(wide), axis=0),
-                jnp.sum(key_lin_grad.astype(wide), axis=0),
-                jnp.sum(value_lin_grad.astype(wide), axis=0),
-            ]
+        biases = [
+            jnp.sum(grad.astype(wide), axis=0)
+            for grad in (query_lin_grad, key_lin_grad, value_lin_grad)
+        ]
+        small = jnp.concatenate([sum_over_plane(gains), *biases])
+        small = small + swap_core(small)
+        lanes = 4 * width
+        count = -(-small.shape[0] // (8 * lanes)) * 8
+        small = jnp.pad(small, (0, count * lanes - small.shape[0])).reshape(count, lanes)
+        high = small.astype(narrow)
+        return jnp.concatenate([high, (small - high.astype(wide)).astype(narrow)], axis=0)
+
+    expert_down_grad = expert_sum(*down_experts)[None]
+    expert_gate_grad = expert_sum(*gate_experts).T[None]
+    expert_up_grad = expert_sum(*up_experts).T[None]
+    shared_down_grad = shared_down_all.astype(wide)
+    shared_gate_grad = turn(shared_gate_all)
+    shared_up_grad = turn(shared_up_all)
+    ties = [(), (shared_down_grad, shared_gate_grad)]
+    for step in range(2, chips):
+        if step - 2 < len(ties):
+            total = after(total, *ties[step - 2])
+        total = ring_next((attn_part(step) + total.astype(wide)).astype(narrow))
+    total = after(total, input_grad, expert_down_grad)
+    attn_own = (attn_part(0) + total.astype(wide)).astype(narrow)
+    attn_held = [jnp.concatenate([attn_own, small_rows()], axis=0)]
+    ties = [(shared_up_grad, expert_gate_grad), (expert_up_grad,)]
+    for step in range(chips - 1):
+        block = ring_next(attn_held[-1])
+        attn_held.append(after(block, *ties[step]) if step < len(ties) else block)
+    attn_blocks, attn_places, sums = [], [], None
+    for step, (block, at) in enumerate(zip(attn_held, sources)):
+        if step == chips - 1:
+            sums = assemble(attn_blocks, jnp.stack(attn_places), piece, None)
+            block, sums = pin((block, sums))
+            attn_blocks, attn_places = [], []
+        attn_blocks += [block, swap_core(block)]
+        attn_places += [source * piece for source in at]
+    q_sum, k_sum, v_sum, o_sum = assemble(attn_blocks, jnp.stack(attn_places), piece, sums)
+    small = 0.0
+    for chip in range(chips):
+        rows_of = sum(
+            jnp.where(at == chip, block[piece:].astype(wide), 0.0)
+            for block, at in zip(attn_held, ring_places)
         )
-    )
+        small = small + rows_of
+    half = small.shape[0] // 2
+    small = (small[:half] + small[half:]).reshape(-1)
+
     attn_gain_grad, mlp_gain_grad, shared_router_grad = (small[i * D : (i + 1) * D] for i in range(3))
     teacher_loss = small[3 * D] / (valid_count * D)
     biases = small[3 * D + 128 :]
@@ -980,7 +1119,7 @@
         k_sum,
         biases[width : 2 * width],
         v_sum,
-        biases[2 * width :],
+        biases[2 * width : 3 * width],
         o_sum,
         mlp_gain_grad,
         expert_gate_grad,

time: 1040 us -> 940 us (0.904)
  waiting for transfers between devices: 395 us -> 299 us
  starting transfers between devices: 88.3 us -> 76.1 us
    ppermute x30 -> x21, waiting for transfers between devices: 151 us -> 81.2 us  [ring_next(): return lax.ppermute(value, 'dp', pairs)]
    ppermute x43 -> x42, waiting for transfers between devices: 241 us -> 211 us  [flip(): return lax.ppermute(value, 'tensor', [(i, i ^ bit) for i in range(size)])]
    dot_general x2 -> x0, matrix products: 12.7 us -> none  [dot_tn(): lax.dot_general(left, right, (((0,), (0,)), ((), ())), preferred_element_...]
    squeeze x12 -> x0, local copies, waits for them, and re-layouts: 11.2 us -> none  [the longest x4 3.55 us: shards(): mix_two[step]]
    pallas_call x13 -> x16, Pallas kernels: 259 us -> 269 us  [the longest x4 94.1 us: backward_step(): pl.pallas_call(functools.partial(backward_body, rows, count, places, piec...]
    ppermute x30 -> x21, starting transfers between devices: 31.8 us -> 23.8 us  [ring_next(): return lax.ppermute(value, 'dp', pairs)]
    convert_element_type x15 -> x18, other arithmetic: 45.1 us -> 41.2 us  [the longest x3 8.21 us: shared_sum(): return bits_scatter(parts, w_bits)[:f_shared].astype(narrow)]
    unnamed x218 -> x206, local copies, waits for them, and re-layouts: 22.3 us -> 18.9 us
  transfers between devices with their start and end apart: 96 -> 84, of which waited for: 39 -> 39; matrix products, arithmetic and copies ran while one was open for 20% -> 23% of each run, Pallas kernels for 26% -> 29%
where the time goes in v3:
time: 940 us; the launch traced here: 933 us
  waiting for transfers between devices  299 us (32%)
  Pallas kernels  287 us (31%)
  other arithmetic  141 us (15%)
  starting transfers between devices  76.1 us (8%)
  local copies, waits for them, and re-layouts  52.3 us (6%)
  matrix products  49.7 us (5%)
  between operations  27.8 us (3%)
    ppermute x42, waiting for transfers between devices, flip(): return lax.ppermute(value, 'tensor', [(i, i ^ bit) for i in range(size)])  211 us
    pallas_call x4, Pallas kernels, backward_step(): pl.pallas_call(functools.partial(backward_body, rows, count, places, piec...  94.1 us
    pallas_call x4, Pallas kernels, forward_step(): pl.pallas_call(functools.partial(forward_body, rows, count, places, piece...  82.6 us
    ppermute x21, waiting for transfers between devices, ring_next(): return lax.ppermute(value, 'dp', pairs)  81.2 us
    pallas_call x5, Pallas kernels, weight_grads(): pl.pallas_call(functools.partial(weight_body, rows, steps, blocks, shape,...  68.1 us
    ppermute x42, starting transfers between devices, flip(): return lax.ppermute(value, 'tensor', [(i, i ^ bit) for i in range(size)])  49.4 us
    ppermute x21, starting transfers between devices, ring_next(): return lax.ppermute(value, 'dp', pairs)  23.8 us
    unnamed x206, local copies, waits for them, and re-layouts  18.9 us
  transfers between devices with their start and end apart: 84, of which 39 were waited for; matrix products, arithmetic and copies ran while one was open for 23% of the time, Pallas kernels for 29%

profile of v3, /device:TPU:0, one launch (start us, length us, event | category | flops | bytes accessed | tf_op | source)
XLA Modules:
  0.0 933.0 jit_solution(17582713222553567715)
XLA Ops:
  40.1 16.4 %collective-permute-done.2.refs_13_ = bf16[256,2048]{1,0:T(8,128)(2,1)} collective-permute-done((bf16[256,2048]{1,0:T(8,128)(2,1)}, bf16[256,2048]{1,0:T(8,128)(2,1)}, u32[]{:S(2)}, u32[]{:S(2)}) %collective-permute-start.2) | collective-permute-done | bytes 1048608 | tf_op jit(solution)/shard_map/ppermute | solution.py:92
  62.4 12.3 %collective-permute-done.3 = bf16[192,2048]{1,0:T(8,128)(2,1)S(1)} collective-permute-done((bf16[192,2048]{1,0:T(8,128)(2,1)}, bf16[192,2048]{1,0:T(8,128)(2,1)S(1)}, u32[]{:S(2)}, u32[]{:S(2)}) %collective-permute-start.3) | collective-permute-done | bytes 786464 | tf_op jit(solution)/shard_map/ppermute | solution.py:92
  117.1 15.5 %collective-permute-done.11 = bf16[192,2048]{1,0:T(8,128)(2,1)S(1)} collective-permute-done((bf16[192,2048]{1,0:T(8,128)(2,1)S(1)}, bf16[192,2048]{1,0:T(8,128)(2,1)S(1)}, u32[]{:S(2)}, u32[]{:S(2)}) %collective-permute-start.11) | collective-permute-done | bytes 786464 | tf_op jit(solution)/shard_map/ppermute | solution.py:92
  204.8 18.3 %collective-permute-done.19.refs_0_.refs_14_.refs_6_ = bf16[192,2048]{1,0:T(8,128)(2,1)} collective-permute-done((bf16[192,2048]{1,0:T(8,128)(2,1)S(1)}, bf16[192,2048]{1,0:T(8,128)(2,1)}, u32[]{:S(2)}, u32[]{:S(2)}) %collective-permute-start.19) | collective-permute-done | bytes 786464 | tf_op jit(solution)/shard_map/ppermute | solution.py:153
  223.8 20.6 %ffn_forward.4 = (bf16[192,2048]{1,0:T(8,128)(2,1)}, bf16[192,2048]{1,0:T(8,128)(2,1)}, bf16[384,704]{1,0:T(8,128)(2,1)}, bf16[384,704]{1,0:T(8,128)(2,1)}, bf16...) custom-call(bf16[192,2048]{1,0:T(8,128)(2,1)} %copy-done.57, ...), custom_call_target="tpu_custom_call" | custom-call | flops 9965666304 | bytes 33964032 | tf_op jit(solution)/shard_map/ffn_forward/pallas_call | solution.py:370
  245.9 20.9 %ffn_forward.5 = (bf16[192,2048]{1,0:T(8,128)(2,1)}, bf16[192,2048]{1,0:T(8,128)(2,1)}, bf16[384,704]{1,0:T(8,128)(2,1)}, bf16[384,704]{1,0:T(8,128)(2,1)}, bf16...) custom-call(bf16[192,2048]{1,0:T(8,128)(2,1)} %copy-done.53, ...), custom_call_target="tpu_custom_call" | custom-call | flops 9965666304 | bytes 33964032 | tf_op jit(solution)/shard_map/ffn_forward/pallas_call | solution.py:370
  270.0 20.6 %ffn_forward.6 = (bf16[192,2048]{1,0:T(8,128)(2,1)}, bf16[192,2048]{1,0:T(8,128)(2,1)}, bf16[384,704]{1,0:T(8,128)(2,1)}, bf16[384,704]{1,0:T(8,128)(2,1)}, bf16...) custom-call(bf16[192,2048]{1,0:T(8,128)(2,1)} %collective-permute-do, ...), custom_call_target="tpu_custom_call" | custom-call | flops 9965666304 | bytes 33964032 | tf_op jit(solution)/shard_map/ffn_forward/pallas_call | solution.py:370
  296.9 20.6 %ffn_forward.7 = (bf16[192,2048]{1,0:T(8,128)(2,1)}, bf16[192,2048]{1,0:T(8,128)(2,1)}, bf16[384,704]{1,0:T(8,128)(2,1)}, bf16[384,704]{1,0:T(8,128)(2,1)}, bf16...) custom-call(bf16[192,2048]{1,0:T(8,128)(2,1)} %copy-done.32, ...), custom_call_target="tpu_custom_call" | custom-call | flops 9965666304 | bytes 33964032 | tf_op jit(solution)/shard_map/ffn_forward/pallas_call | solution.py:370
  323.7 11.3 %collective-permute-done.32 = bf16[192,2048]{1,0:T(8,128)(2,1)} collective-permute-done((bf16[192,2048]{1,0:T(8,128)(2,1)}, bf16[192,2048]{1,0:T(8,128)(2,1)}, u32[]{:S(2)}, u32[]{:S(2)}) %collective-permute-start.32) | collective-permute-done | bytes 786464 | tf_op jit(solution)/shard_map/ppermute | solution.py:92
  345.6 13.9 %collective-permute-done.41.refs_1_ = bf16[192,2048]{1,0:T(8,128)(2,1)S(1)} collective-permute-done((bf16[192,2048]{1,0:T(8,128)(2,1)S(1)}, bf16[192,2048]{1,0:T(8,128)(2,1)S(1)}, u32[]{:S(2)}, u32[]{:S(2)}) %collective-permute-start.41) | collective-permute-done | bytes 786464 | tf_op jit(solution)/shard_map/ppermute | solution.py:92
  363.1 23.5 %ffn_backward.4 = (bf16[192,2048]{1,0:T(8,128)(2,1)}, bf16[192,2048]{1,0:T(8,128)(2,1)}, bf16[384,704]{1,0:T(8,128)(2,1)}, bf16[384,704]{1,0:T(8,128)(2,1)}, bf1...) custom-call(bf16[192,2048]{1,0:T(8,128)(2,1)} %copy-done.10, ...), custom_call_target="tpu_custom_call" | custom-call | flops 9965666304 | bytes 35586048 | tf_op jit(solution)/shard_map/ffn_backward/pallas_call | solution.py:462
  391.0 23.4 %ffn_backward.5 = (bf16[192,2048]{1,0:T(8,128)(2,1)}, bf16[192,2048]{1,0:T(8,128)(2,1)}, bf16[384,704]{1,0:T(8,128)(2,1)}, bf16[384,704]{1,0:T(8,128)(2,1)}, bf1...) custom-call(bf16[192,2048]{1,0:T(8,128)(2,1)} %collective-permute-do, ...), custom_call_target="tpu_custom_call" | custom-call | flops 9965666304 | bytes 35586048 | tf_op jit(solution)/shard_map/ffn_backward/pallas_call | solution.py:462
  425.6 23.6 %ffn_backward.6 = (bf16[192,2048]{1,0:T(8,128)(2,1)}, bf16[192,2048]{1,0:T(8,128)(2,1)}, bf16[384,704]{1,0:T(8,128)(2,1)}, bf16[384,704]{1,0:T(8,128)(2,1)}, bf1...) custom-call(bf16[192,2048]{1,0:T(8,128)(2,1)} %collective-permute-do, ...), custom_call_target="tpu_custom_call" | custom-call | flops 9965666304 | bytes 35586048 | tf_op jit(solution)/shard_map/ffn_backward/pallas_call | solution.py:462
  460.3 23.5 %ffn_backward.7 = (bf16[192,2048]{1,0:T(8,128)(2,1)}, bf16[192,2048]{1,0:T(8,128)(2,1)}, bf16[384,704]{1,0:T(8,128)(2,1)}, bf16[384,704]{1,0:T(8,128)(2,1)}, bf1...) custom-call(bf16[192,2048]{1,0:T(8,128)(2,1)} %copy-done.28, ...), custom_call_target="tpu_custom_call" | custom-call | flops 9965666304 | bytes 35586048 | tf_op jit(solution)/shard_map/ffn_backward/pallas_call | solution.py:462
  487.4 19.4 %weight_grads.5 = (bf16[1056,2048]{1,0:T(8,128)(2,1)}, bf16[1056,2048]{1,0:T(8,128)(2,1)}) custom-call(bf16[192,2048]{1,0:T(8,128)(2,1)} %copy-done.10, bf16[192,2048]{1,0:T(8,128)(2,1)} %copy-done.27, bf16[192,2048]{1,0:T(8,128)(2,1)} %collective-permute-done.36.refs_0_.refs_2_, bf16[192,2048]{1,0:T(8,128)(2,1)} %collective-permute-done.40.refs_1_.refs_3_, ...), custom_call_target="tpu_custom_call" | custom-call | flops 13287555072 | bytes 21430272 | tf_op jit(solution)/shard_map/weight_grads/pallas_call | solution.py:545
  550.5 13.1 %collective-permute-done.51 = bf16[176,2048]{1,0:T(8,128)(2,1)S(1)} collective-permute-done((bf16[176,2048]{1,0:T(8,128)(2,1)S(1)}, bf16[176,2048]{1,0:T(8,128)(2,1)S(1)}, u32[]{:S(2)}, u32[]{:S(2)}) %collective-permute-start.51) | collective-permute-done | bytes 720928 | tf_op jit(solution)/shard_map/ppermute | solution.py:92
  568.1 14.6 %weight_grads.8 = (bf16[704,2048]{1,0:T(8,128)(2,1)}, bf16[704,2048]{1,0:T(8,128)(2,1)}) custom-call(bf16[192,2048]{1,0:T(8,128)(2,1)} %copy-done.32, bf16[192,2048]{1,0:T(8,128)(2,1)} %copy-done.55, bf16[192,2048]{1,0:T(8,128)(2,1)} %copy-done.57, bf16[192,2048]{1,0:T(8,128)(2,1)} %copy-done.59, bf16[192,2048]{1,0:T(8,128)(2,1)} %copy-done.53, ...), custom_call_target="tpu_custom_call" | custom-call | flops 8858370048 | bytes 16384000 | tf_op jit(solution)/shard_map/weight_grads/pallas_call | solution.py:545
  675.3 12.9 %attention_grads.1 = (bf16[4,256,2048]{2,1,0:T(8,128)(2,1)}, bf16[4,256,2048]{2,1,0:T(8,128)(2,1)}) custom-call(s32[8]{0:T(128)} %stack.109.order, bf16[768,2048]{1,0:T(8,128)(2,1)} %pad_maximum_fusion.normed, bf16[768,1536]{1,0:T(8,128)(2,1)} %pad_maximum_fusion.1.grads, bf16[768,2048]{1,0:T(8,128)(2,1)} %copy-done.69, bf16[768,512]{1,0:T(8,128)(2,1)} %copy-done.52), custom_call_target="tpu_custom_call" | custom-call | flops 6442450944 | bytes 17825792 | tf_op jit(solution)/shard_map/attention_grads/pallas_call | solution.py:586
  711.2 14.6 %weight_grads.9 = (bf16[704,2048]{1,0:T(8,128)(2,1)}, bf16[704,2048]{1,0:T(8,128)(2,1)}) custom-call(bf16[192,2048]{1,0:T(8,128)(2,1)} %copy-done.32, bf16[192,2048]{1,0:T(8,128)(2,1)} %copy-done.55, bf16[192,2048]{1,0:T(8,128)(2,1)} %copy-done.57, bf16[192,2048]{1,0:T(8,128)(2,1)} %copy-done.59, bf16[192,2048]{1,0:T(8,128)(2,1)} %copy-done.53, ...), custom_call_target="tpu_custom_call" | custom-call | flops 8858370048 | bytes 16384000 | tf_op jit(solution)/shard_map/weight_grads/pallas_call | solution.py:545
  734.1 13.8 %collective-permute-done.61 = bf16[192,2048]{1,0:T(8,128)(2,1)S(1)} collective-permute-done((bf16[192,2048]{1,0:T(8,128)(2,1)S(1)}, bf16[192,2048]{1,0:T(8,128)(2,1)S(1)}, u32[]{:S(2)}, u32[]{:S(2)}) %collective-permute-start.61) | collective-permute-done | bytes 786464 | tf_op jit(solution)/shard_map/ppermute | solution.py:92
  757.8 15.9 %collective-permute-done.65 = bf16[256,2048]{1,0:T(8,128)(2,1)S(1)} collective-permute-done((bf16[256,2048]{1,0:T(8,128)(2,1)S(1)}, bf16[256,2048]{1,0:T(8,128)(2,1)S(1)}, u32[]{:S(2)}, u32[]{:S(2)}) %collective-permute-start.65) | collective-permute-done | bytes 1048608 | tf_op jit(solution)/shard_map/ppermute | solution.py:153
  835.4 12.3 %collective-permute-done.73 = bf16[352,2048]{1,0:T(8,128)(2,1)S(1)} collective-permute-done((bf16[352,2048]{1,0:T(8,128)(2,1)S(1)}, bf16[352,2048]{1,0:T(8,128)(2,1)S(1)}, u32[]{:S(2)}, u32[]{:S(2)}) %collective-permute-start.73) | collective-permute-done | bytes 1441824 | tf_op jit(solution)/shard_map/ppermute | solution.py:92
  861.9 14.7 %collective-permute-done.75 = bf16[352,2048]{1,0:T(8,128)(2,1)} collective-permute-done((bf16[352,2048]{1,0:T(8,128)(2,1)}, bf16[352,2048]{1,0:T(8,128)(2,1)}, u32[]{:S(2)}, u32[]{:S(2)}) %collective-permute-start.75) | collective-permute-done | bytes 1441824 | tf_op jit(solution)/shard_map/ppermute | solution.py:92
  894.7 13.2 %collective-permute-done.76.refs_1_ = bf16[272,2048]{1,0:T(8,128)(2,1)} collective-permute-done((bf16[272,2048]{1,0:T(8,128)(2,1)}, bf16[272,2048]{1,0:T(8,128)(2,1)}, u32[]{:S(2)}, u32[]{:S(2)}) %collective-permute-start.76) | collective-permute-done | bytes 1114144 | tf_op jit(solution)/shard_map/ppermute | solution.py:153
  (541 shorter events, 496.5 us)
Async XLA Ops:
  7.2 776.0 %all-gather.4.cloned.1.call-start = ((), (), s32[]{:S(2)}) async-start(), calls=%async_computation | async-start | bytes 6488064 | tf_op jit(solution)/shard_map/all_gather | solution.py:980
  17.2 39.3 %collective-permute-start.2 = (bf16[256,2048]{1,0:T(8,128)(2,1)}, bf16[256,2048]{1,0:T(8,128)(2,1)}, u32[]{:S(2)}, u32[]{:S(2)}) collective-permute-start(bf16[256,2048]{1,0:T(8,128)(2,1)} %slice_bitcast_fusion), channel_id=1, source_target_pairs={{0,1},{1,0},{2,3},{3,2},{4,5},{5,4},{6,7},{7,6},{8,9},{9,8},{10,11... | collective-permute-start | bytes 3145736 | tf_op jit(solution)/shard_map/ppermute | solution.py:92
  27.3 78.1 %collective-permute-start.8 = (bf16[528,2048]{1,0:T(8,128)(2,1)}, bf16[528,2048]{1,0:T(8,128)(2,1)}, u32[]{:S(2)}, u32[]{:S(2)}) collective-permute-start(bf16[528,2048]{1,0:T(8,128)(2,1)} %pad_maximum_fusion.4.refs_6_), channel_id=1, source_target_pairs={{0,4},{4,0},{8,12},{12,8},{16,20},{20,16},{24,28},{28,24},{1,5},{5... | collective-permute-start | bytes 6488072 | tf_op jit(solution)/shard_map/ppermute | solution.py:158
  60.1 78.8 %collective-permute-start.12 = (bf16[528,2048]{1,0:T(8,128)(2,1)}, bf16[528,2048]{1,0:T(8,128)(2,1)}, u32[]{:S(2)}, u32[]{:S(2)}) collective-permute-start(bf16[528,2048]{1,0:T(8,128)(2,1)} %pad_maximum_fusion.2.refs_2_), channel_id=1, source_target_pairs={{0,1},{1,0},{2,3},{3,2},{4,5},{5,4},{6,7},{7,6},{8,9},{9,8},{10,11... | collective-permute-start | bytes 6488072 | tf_op jit(solution)/shard_map/ppermute | solution.py:92
  61.9 43.5 %collective-permute-start.7 = (bf16[528,2048]{1,0:T(8,128)(2,1)}, bf16[528,2048]{1,0:T(8,128)(2,1)}, u32[]{:S(2)}, u32[]{:S(2)}) collective-permute-start(bf16[528,2048]{1,0:T(8,128)(2,1)} %pad_maximum_fusion.2.refs_2_), channel_id=1, source_target_pairs={{0,4},{4,0},{8,12},{12,8},{16,20},{20,16},{24,28},{28,24},{1,5},{5... | collective-permute-start | bytes 6488072 | tf_op jit(solution)/shard_map/ppermute | solution.py:158
  61.9 43.5 %collective-permute-start.9 = (bf16[528,2048]{1,0:T(8,128)(2,1)}, bf16[528,2048]{1,0:T(8,128)(2,1)}, u32[]{:S(2)}, u32[]{:S(2)}) collective-permute-start(bf16[528,2048]{1,0:T(8,128)(2,1)} %pad_maximum_fusion.3.refs_12_), channel_id=1, source_target_pairs={{0,4},{4,0},{8,12},{12,8},{16,20},{20,16},{24,28},{28,24},{1,5},{5... | collective-permute-start | bytes 6488072 | tf_op jit(solution)/shard_map/ppermute | solution.py:158
  115.6 29.3 %collective-permute-start.10 = (bf16[192,2048]{1,0:T(8,128)(2,1)S(1)}, bf16[192,2048]{1,0:T(8,128)(2,1)S(1)}, u32[]{:S(2)}, u32[]{:S(2)}) collective-permute-start(bf16[192,2048]{1,0:T(8,128)(2,1)S(1)} %get-tuple-element.609), channel_id=1, source_target_pairs={{0,2},{1,3},{2,0},{3,1},{4,6},{5,7},{6,4},{7,5},{8,10},{9,11},{10,... | collective-permute-start | bytes 2359304 | tf_op jit(solution)/shard_map/ppermute | solution.py:92
  173.8 49.9 %collective-permute-start.22 = (bf16[528,2048]{1,0:T(8,128)(2,1)}, bf16[528,2048]{1,0:T(8,128)(2,1)}, u32[]{:S(2)}, u32[]{:S(2)}) collective-permute-start(bf16[528,2048]{1,0:T(8,128)(2,1)} %collective-permute-done.12.refs_3_), channel_id=1, source_target_pairs={{0,4},{4,0},{8,12},{12,8},{16,20},{20,16},{24,28},{28,24},{1,5},{5... | collective-permute-start | bytes 6488072 | tf_op jit(solution)/shard_map/ppermute | solution.py:158
  203.5 42.4 %collective-permute-start.21 = (bf16[192,2048]{1,0:T(8,128)(2,1)S(1)}, bf16[192,2048]{1,0:T(8,128)(2,1)}, u32[]{:S(2)}, u32[]{:S(2)}) collective-permute-start(bf16[192,2048]{1,0:T(8,128)(2,1)S(1)} %collective-permute-done.17.refs_0_.refs_12_.refs_4_), channel_id=1, source_target_pairs={{0,2},{1,3},{2,0},{3,1},{4,6},{5,7},{6,4},{7,5},{8,10},{9,11},{10,... | collective-permute-start | bytes 2359304 | tf_op jit(solution)/shard_map/ppermute | solution.py:92
  386.7 29.6 %collective-permute-start.42 = (bf16[192,2048]{1,0:T(8,128)(2,1)}, bf16[192,2048]{1,0:T(8,128)(2,1)}, u32[]{:S(2)}, u32[]{:S(2)}) collective-permute-start(bf16[192,2048]{1,0:T(8,128)(2,1)} %get-tuple-element.350), channel_id=1, source_target_pairs={{0,2},{1,3},{2,0},{3,1},{4,6},{5,7},{6,4},{7,5},{8,10},{9,11},{10,... | collective-permute-start | bytes 2359304 | tf_op jit(solution)/shard_map/ppermute | solution.py:92
  388.1 30.8 %collective-permute-start.39 = (bf16[192,2048]{1,0:T(8,128)(2,1)}, bf16[192,2048]{1,0:T(8,128)(2,1)S(1)}, u32[]{:S(2)}, u32[]{:S(2)}) collective-permute-start(bf16[192,2048]{1,0:T(8,128)(2,1)} %collective-permute-done.37.refs_0_.refs_4_), channel_id=1, source_target_pairs={{0,8},{4,12},{8,24},{12,28},{24,16},{28,20},{16,0},{20,4},{1,9},{5... | collective-permute-start | bytes 2359304 | tf_op jit(solution)/shard_map/ppermute | solution.py:153
  390.7 33.1 %collective-permute-start.38 = (bf16[192,2048]{1,0:T(8,128)(2,1)}, bf16[192,2048]{1,0:T(8,128)(2,1)S(1)}, u32[]{:S(2)}, u32[]{:S(2)}) collective-permute-start(bf16[192,2048]{1,0:T(8,128)(2,1)} %collective-permute-done.37.refs_0_.refs_4_), channel_id=1, source_target_pairs={{0,2},{1,3},{2,0},{3,1},{4,6},{5,7},{6,4},{7,5},{8,10},{9,11},{10,... | collective-permute-start | bytes 2359304 | tf_op jit(solution)/shard_map/ppermute | solution.py:92
  414.4 35.8 %collective-permute-start.45 = (bf16[192,2048]{1,0:T(8,128)(2,1)}, bf16[192,2048]{1,0:T(8,128)(2,1)}, u32[]{:S(2)}, u32[]{:S(2)}) collective-permute-start(bf16[192,2048]{1,0:T(8,128)(2,1)} %get-tuple-element.361), channel_id=1, source_target_pairs={{0,2},{1,3},{2,0},{3,1},{4,6},{5,7},{6,4},{7,5},{8,10},{9,11},{10,... | collective-permute-start | bytes 2359304 | tf_op jit(solution)/shard_map/ppermute | solution.py:92
  423.9 33.8 %collective-permute-start.43 = (bf16[192,2048]{1,0:T(8,128)(2,1)S(1)}, bf16[192,2048]{1,0:T(8,128)(2,1)}, u32[]{:S(2)}, u32[]{:S(2)}) collective-permute-start(bf16[192,2048]{1,0:T(8,128)(2,1)S(1)} %collective-permute-done.39.refs_0_.refs_6_), channel_id=1, source_target_pairs={{0,2},{1,3},{2,0},{3,1},{4,6},{5,7},{6,4},{7,5},{8,10},{9,11},{10,... | collective-permute-start | bytes 2359304 | tf_op jit(solution)/shard_map/ppermute | solution.py:92
  449.2 36.4 %collective-permute-start.44 = (bf16[192,2048]{1,0:T(8,128)(2,1)}, bf16[192,2048]{1,0:T(8,128)(2,1)S(1)}, u32[]{:S(2)}, u32[]{:S(2)}) collective-permute-start(bf16[192,2048]{1,0:T(8,128)(2,1)} %get-tuple-element.373), channel_id=1, source_target_pairs={{0,2},{1,3},{2,0},{3,1},{4,6},{5,7},{6,4},{7,5},{8,10},{9,11},{10,... | collective-permute-start | bytes 2359304 | tf_op jit(solution)/shard_map/ppermute | solution.py:92
  566.2 225.7 %all-gather.6.cloned.1.call-start = ((), (), s32[]{:S(2)}) async-start(), calls=%async_computation.1 | async-start | bytes 6488064 | tf_op jit(solution)/shard_map/all_gather | solution.py:985
  613.2 49.8 %collective-permute-start.56 = (bf16[176,2048]{1,0:T(8,128)(2,1)}, bf16[176,2048]{1,0:T(8,128)(2,1)}, u32[]{:S(2)}, u32[]{:S(2)}) collective-permute-start(bf16[176,2048]{1,0:T(8,128)(2,1)} %add_convert_fusion.13), channel_id=1, source_target_pairs={{0,1},{1,0},{2,3},{3,2},{4,5},{5,4},{6,7},{7,6},{8,9},{9,8},{10,11... | collective-permute-start | bytes 2162696 | tf_op jit(solution)/shard_map/ppermute | solution.py:92
  621.0 230.3 %all-gather.8.cloned.1.call-start = ((), (), s32[]{:S(2)}) async-start(), calls=%async_computation.2 | async-start | bytes 6488064 | tf_op jit(solution)/shard_map/all_gather | solution.py:1007
  690.0 67.8 %collective-permute-start.67 = (bf16[704,2048]{1,0:T(8,128)(2,1)}, bf16[704,2048]{1,0:T(8,128)(2,1)}, u32[]{:S(2)}, u32[]{:S(2)}) collective-permute-start(bf16[704,2048]{1,0:T(8,128)(2,1)} %weight_grads.6), channel_id=1, source_target_pairs={{0,4},{4,0},{8,12},{12,8},{16,20},{20,16},{24,28},{28,24},{1,5},{5... | collective-permute-start | bytes 8650760 | tf_op jit(solution)/shard_map/ppermute | solution.py:158
  690.4 67.4 %collective-permute-start.68 = (bf16[704,2048]{1,0:T(8,128)(2,1)}, bf16[704,2048]{1,0:T(8,128)(2,1)}, u32[]{:S(2)}, u32[]{:S(2)}) collective-permute-start(bf16[704,2048]{1,0:T(8,128)(2,1)} %get-tuple-element.533), channel_id=1, source_target_pairs={{0,4},{4,0},{8,12},{12,8},{16,20},{20,16},{24,28},{28,24},{1,5},{5... | collective-permute-start | bytes 8650760 | tf_op jit(solution)/shard_map/ppermute | solution.py:158
  725.7 48.0 %collective-permute-start.66 = (bf16[704,2048]{1,0:T(8,128)(2,1)}, bf16[704,2048]{1,0:T(8,128)(2,1)S(1)}, u32[]{:S(2)}, u32[]{:S(2)}) collective-permute-start(bf16[704,2048]{1,0:T(8,128)(2,1)} %get-tuple-element.529), channel_id=1, source_target_pairs={{0,4},{4,0},{8,12},{12,8},{16,20},{20,16},{24,28},{28,24},{1,5},{5... | collective-permute-start | bytes 8650760 | tf_op jit(solution)/shard_map/ppermute | solution.py:158
  782.0 34.7 %collective-permute-start.71 = (bf16[352,2048]{1,0:T(8,128)(2,1)}, bf16[352,2048]{1,0:T(8,128)(2,1)S(1)}, u32[]{:S(2)}, u32[]{:S(2)}) collective-permute-start(bf16[352,2048]{1,0:T(8,128)(2,1)} %add_convert_fusion.3), channel_id=1, source_target_pairs={{0,1},{1,0},{2,3},{3,2},{4,5},{5,4},{6,7},{7,6},{8,9},{9,8},{10,11... | collective-permute-start | bytes 4325384 | tf_op jit(solution)/shard_map/ppermute | solution.py:92
  807.6 40.1 %collective-permute-start.73 = (bf16[352,2048]{1,0:T(8,128)(2,1)S(1)}, bf16[352,2048]{1,0:T(8,128)(2,1)S(1)}, u32[]{:S(2)}, u32[]{:S(2)}) collective-permute-start(bf16[352,2048]{1,0:T(8,128)(2,1)S(1)} %add_convert_fusion.2), channel_id=1, source_target_pairs={{0,1},{1,0},{2,3},{3,2},{4,5},{5,4},{6,7},{7,6},{8,9},{9,8},{10,11... | collective-permute-start | bytes 4325384 | tf_op jit(solution)/shard_map/ppermute | solution.py:92
  834.4 42.1 %collective-permute-start.75 = (bf16[352,2048]{1,0:T(8,128)(2,1)}, bf16[352,2048]{1,0:T(8,128)(2,1)}, u32[]{:S(2)}, u32[]{:S(2)}) collective-permute-start(bf16[352,2048]{1,0:T(8,128)(2,1)} %add_convert_fusion.1), channel_id=1, source_target_pairs={{0,1},{1,0},{2,3},{3,2},{4,5},{5,4},{6,7},{7,6},{8,9},{9,8},{10,11... | collective-permute-start | bytes 4325384 | tf_op jit(solution)/shard_map/ppermute | solution.py:92
  (160 other events, 2530.0 us)
Sparse Core Ops, SparseCore 0:
  566.4 58.8 all-gather.3
  626.9 59.0 all-gather.5
  690.7 59.2 all-gather.7

commit v4 on v3

--- a/solution.py
+++ b/solution.py
@@ -156,6 +156,12 @@
 def swap_core(value):
     size = lax.axis_size("dp")
     return lax.ppermute(value, "dp", [(i, i ^ 1) for i in range(size)])
+
+
+def both_ways(value, bit):
+    n_dp, size = lax.axis_size("dp"), lax.axis_size("tensor")
+    pairs = [(d * size + t, (d ^ 1) * size + (t ^ bit)) for d in range(n_dp) for t in range(size)]
+    return lax.ppermute(value, ("dp", "tensor"), pairs)
 
 
 def ring_chips():
@@ -336,23 +342,29 @@
     router_gate = jax.nn.sigmoid(jnp.sum(x.astype(WIDE) * router[...], axis=1, keepdims=True))
     factor_ref[...] = router_gate
     factors = (column(mix_one), column(mix_two), router_gate)
-    total, away = None, []
-    for at, ((start, size, _), arriving) in enumerate(zip(places, w_in)):
-        span = pl.ds(start, size)
-        for copy in arriving[0]:
-            copy.wait()
-        gate_in = dot_nt(x, gate_s[span])
-        for copy in arriving[1]:
-            copy.wait()
-        up_in = dot_nt(x, up_s[span])
-        hidden = (gate_in * jax.nn.sigmoid(gate_in) * up_in * factors[at]).astype(NARROW)
-        for n, value in enumerate((gate_in, up_in, hidden)):
-            kept[3 * n + at][...] = value.astype(NARROW)
-            away.append(copies.start(kept[3 * n + at], kept_refs[3 * n + at]))
-        for copy in arriving[2]:
-            copy.wait()
-        part = dot_nn(hidden, down_s[span])
-        total = part if total is None else total + part
+    away, products, total = [], [], None
+    for at in range(len(places) + 1):
+        if at < len(places):
+            start, size, _ = places[at]
+            for copy in w_in[at][0] + w_in[at][1]:
+                copy.wait()
+        if at > 0:
+            for copy in w_in[at - 1][2]:
+                copy.wait()
+        if at < len(places):
+            products.append(
+                (dot_nt(x, gate_s[pl.ds(start, size)]), dot_nt(x, up_s[pl.ds(start, size)]))
+            )
+        if at > 0:
+            gate_in, up_in = products[at - 1]
+            hidden = (gate_in * jax.nn.sigmoid(gate_in) * up_in * factors[at - 1]).astype(NARROW)
+            for n, value in enumerate((gate_in, up_in, hidden)):
+                kept[3 * n + at - 1][...] = value.astype(NARROW)
+            start, size, _ = places[at - 1]
+            part = dot_nn(hidden, down_s[pl.ds(start, size)])
+            total = part if total is None else total + part
+            for n in range(3):
+                away.append(copies.start(kept[3 * n + at - 1], kept_refs[3 * n + at - 1]))
     ys[...] = total.astype(NARROW)
     away += [copies.start(ys.at[pl.ds(i * rows, rows)], out_refs[i]) for i in range(count)]
     for copy in away:
@@ -422,27 +434,33 @@
         copy.wait()
     grad = xs[...]
     factors = (column(mix_one), column(mix_two), rg[...])
-    total, away = None, []
-    for at, ((start, size, _), arriving) in enumerate(zip(places, w_in)):
-        span = pl.ds(start, size)
-        for copy in arriving[0]:
-            copy.wait()
-        grad_hidden = dot_nt(grad, down_s[span]) * factors[at]
-        for copy in kept_in[at]:
-            copy.wait()
-        gate_in, up_in = kept[at][...].astype(WIDE), kept[3 + at][...].astype(WIDE)
-        squash = jax.nn.sigmoid(gate_in)
-        up_grad = grad_hidden * gate_in * squash
-        gate_grad = grad_hidden * up_in * squash * (1.0 + gate_in * (1.0 - squash))
-        logit = jnp.sum(up_grad * up_in, axis=1, keepdims=True)
-        gate_grad, up_grad = gate_grad.astype(NARROW), up_grad.astype(NARROW)
-        for n, value in enumerate((gate_grad, up_grad)):
-            kept[3 * n + at][...] = value
-            away.append(copies.start(kept[3 * n + at], grad_refs[3 * n + at]))
-        for copy in arriving[1] + arriving[2]:
-            copy.wait()
-        part = dot_nn(gate_grad, gate_s[span]) + dot_nn(up_grad, up_s[span])
-        total = part if total is None else total + part
+    away, products, total = [], [], None
+    for at in range(len(places) + 1):
+        if at < len(places):
+            start, size, _ = places[at]
+            for copy in w_in[at][0] + kept_in[at]:
+                copy.wait()
+        if at > 0:
+            for copy in w_in[at - 1][1] + w_in[at - 1][2]:
+                copy.wait()
+        if at < len(places):
+            products.append(dot_nt(grad, down_s[pl.ds(start, size)]))
+        if at > 0:
+            grad_hidden = products[at - 1] * factors[at - 1]
+            gate_in, up_in = kept[at - 1][...].astype(WIDE), kept[2 + at][...].astype(WIDE)
+            squash = jax.nn.sigmoid(gate_in)
+            up_grad = grad_hidden * gate_in * squash
+            gate_grad = grad_hidden * up_in * squash * (1.0 + gate_in * (1.0 - squash))
+            logit = jnp.sum(up_grad * up_in, axis=1, keepdims=True)
+            gate_grad, up_grad = gate_grad.astype(NARROW), up_grad.astype(NARROW)
+            kept[at - 1][...] = gate_grad
+            kept[2 + at][...] = up_grad
+            start, size, _ = places[at - 1]
+            span = pl.ds(start, size)
+            part = dot_nn(gate_grad, gate_s[span]) + dot_nn(up_grad, up_s[span])
+            total = part if total is None else total + part
+            for n in range(2):
+                away.append(copies.start(kept[3 * n + at - 1], grad_refs[3 * n + at - 1]))
     logit = logit * (1.0 - rg[...])
     logit_ref[...] = logit
     ys[...] = (total + logit * router[...]).astype(NARROW)
@@ -492,14 +510,13 @@
     return outs, kept[:3], kept[3:6], kept[6]
 
 
-def weight_body(rows, steps, blocks, shape, splits, apart, *refs):
+def weight_body(rows, steps, blocks, shape, plan, *refs):
     groups, names = len(shape), sum(shape)
     x_refs, refs = refs[: groups * steps * blocks], refs[groups * steps * blocks :]
     left_refs, refs = refs[: names * steps], refs[names * steps :]
-    out_refs, refs = refs[:splits], refs[splits:]
-    xs, ls, os, sems = refs
+    out_refs, (xs, ls, os, sems) = refs[:-4], refs[-4:]
     copies = Copies(sems)
-    part, hidden = blocks * rows, os.shape[1]
+    part = blocks * rows
     x_in, left_in, n = [], [], 0
     for group, amount in enumerate(shape):
         arriving = []
@@ -516,7 +533,6 @@
             )
             n += 1
     away, n = [], 0
-    size = hidden // splits
     for group, amount in enumerate(shape):
         for copy in x_in[group]:
             copy.wait()
@@ -524,34 +540,38 @@
             for copy in left_in[n]:
                 copy.wait()
             os[n] = dot_tn(ls[n], xs[group]).astype(NARROW)
-            if apart:
-                away.append(copies.start(os.at[n], out_refs[n]))
-            else:
-                for j in range(splits):
-                    target = out_refs[j].at[pl.ds(n * size, size)]
-                    away.append(copies.start(os.at[n, pl.ds(j * size, size)], target))
+            for first, size, out, place in plan[n]:
+                target = out_refs[out].at[pl.ds(place, size)]
+                away.append(copies.start(os.at[n, pl.ds(first, size)], target))
             n += 1
     for copy in away:
         copy.wait()
 
 
-def weight_grads(groups, splits, apart=False, light=False):
+def weight_grads(groups, plan=None, light=False):
     steps, blocks = len(groups[0][0]), len(groups[0][0][0])
     shape = [len(lefts) for _, lefts in groups]
     names = sum(shape)
     rows, width = groups[0][0][0][0].shape
     total, hidden = steps * blocks * rows, groups[0][1][0][0].shape[1]
+    plan = plan or [[(0, hidden, n, 0)] for n in range(names)]
+    sizes = {}
+    for moves in plan:
+        for _, size, out, place in moves:
+            sizes[out] = max(sizes.get(out, 0), place + size)
     anywhere = pl.BlockSpec(memory_space=pl.ANY)
     outs = pl.pallas_call(
-        functools.partial(weight_body, rows, steps, blocks, shape, splits, apart),
-        out_shape=[jax.ShapeDtypeStruct((names * hidden // splits, width), NARROW)] * splits,
+        functools.partial(weight_body, rows, steps, blocks, shape, plan),
+        out_shape=[jax.ShapeDtypeStruct((sizes[out], width), NARROW) for out in range(len(sizes))],
         in_specs=[anywhere] * (steps * (len(groups) * blocks + names)),
-        out_specs=[anywhere] * splits,
+        out_specs=[anywhere] * len(sizes),
         scratch_shapes=[
             pltpu.VMEM((len(groups), total, width), NARROW),
             pltpu.VMEM((names, total, hidden), NARROW),
             pltpu.VMEM((names, hidden, width), NARROW),
-            pltpu.SemaphoreType.DMA((steps * (len(groups) * blocks + names) + names * splits,)),
+            pltpu.SemaphoreType.DMA(
+                (steps * (len(groups) * blocks + names) + sum(len(moves) for moves in plan),)
+            ),
         ],
         compiler_params=pltpu.CompilerParams(vmem_limit_bytes=VMEM_BYTES),
         cost_estimate=pl.CostEstimate(
@@ -644,19 +664,21 @@
 
 
 def turn_body(x_ref, out_ref):
-    out_ref[...] = x_ref[...].astype(WIDE).T
-
-
-def turn(value):
-    rows, width = value.shape
-    if rows % 128:
-        return value.T.astype(WIDE)
+    count, _, rows, width = x_ref.shape
+    out_ref[...] = x_ref[...].reshape(count * rows, width).astype(WIDE).T
+
+
+def turn(value, count, which, rows):
+    width = value.shape[1]
+    value = value.reshape(count, 2, -1, width)
+    if value.shape[2] != rows or (count * rows) % 128:
+        return value[:, which, :rows].reshape(count * rows, width).T.astype(WIDE)
     return pl.pallas_call(
         turn_body,
         grid=(width // 256,),
-        out_shape=jax.ShapeDtypeStruct((width, rows), WIDE),
-        in_specs=[pl.BlockSpec((rows, 256), lambda i: (0, i))],
-        out_specs=pl.BlockSpec((256, rows), lambda i: (i, 0)),
+        out_shape=jax.ShapeDtypeStruct((width, count * rows), WIDE),
+        in_specs=[pl.BlockSpec((count, 1, rows, 256), lambda i: (0, which, 0, i))],
+        out_specs=pl.BlockSpec((256, count * rows), lambda i: (i, 0)),
         compiler_params=pltpu.CompilerParams(vmem_limit_bytes=VMEM_BYTES),
         name="turn",
     )(value)
@@ -883,12 +905,8 @@
             for j in range(n_hidden)
         ]
 
-    def shared_parts(mine, other, which):
-        both = core_parts(mine, other, which * n_hidden * f_pad, f_pad)
-        return [both[0]] + [part.astype(narrow) for part in both[1:]]
-
     def shared_sum(parts):
-        return bits_scatter(parts, w_bits)[:f_shared].astype(narrow)
+        return bits_scatter(parts, w_bits).astype(narrow)
 
     def expert_sum(mine, other):
         return bits_scatter(core_parts(mine, other, 0, f_expert), w_bits)
@@ -932,25 +950,45 @@
     x_steps, g_steps, dx_sums[chips - 2], total, _ = pin(
         (x_steps, g_steps, dx_sums[chips - 2], total, backward[-1][0])
     )
-    shared_mine, shared_other = weight_grads(
-        [(g_steps, [hidden_of[2]]), (x_steps, [gate_of[2], up_of[2]])], 2
+    near, far = n_blocks, n_blocks + 1
+    plan = [[(b * f_pad, f_pad, b, 0) for b in range(n_blocks)]]
+    plan += [
+        [
+            (b * f_pad, f_pad, near if b < n_hidden else far, (b % n_hidden * 2 + n) * f_pad)
+            for b in range(n_blocks)
+        ]
+        for n in range(2)
+    ]
+    *down_pieces, shared_mine, shared_other = weight_grads(
+        [(g_steps, [hidden_of[2]]), (x_steps, [gate_of[2], up_of[2]])], plan
     )
     total = ring_next((dx_sums[chips - 2].astype(wide) + total.astype(wide)).astype(narrow))
     dx_sums[chips - 1] = bits_scatter(backward[chips - 1][0], r_bits)
-    g_steps, dx_sums[chips - 1], total, shared_mine, shared_other = pin(
-        (g_steps, dx_sums[chips - 1], total, shared_mine, shared_other)
+    g_steps, dx_sums[chips - 1], total, shared_mine, shared_other, down_pieces = pin(
+        (g_steps, dx_sums[chips - 1], total, shared_mine, shared_other, down_pieces)
     )
     here = (dx_sums[chips - 1].astype(wide) + total.astype(wide)).astype(narrow)
-    here, g_steps = pin((here, g_steps))
+    here, g_steps, down_pieces = pin((here, g_steps, down_pieces))
     total = ring_next(here)
-    (down_other,) = weight_grads([(g_steps, hidden_of[1:2])], 1, light=True)
-    g_steps, down_other, shared_other = pin((g_steps, down_other, shared_other))
-    shared_other = swap_core(shared_other)
-    (down_mine,) = weight_grads([(g_steps, hidden_of[:1])], 1, light=True)
-    shared_mine, shared_other, down_mine, down_other = pin(
-        (shared_mine, shared_other, down_mine, down_other)
-    )
-    shared_down_own = shared_sum(shared_parts(shared_mine, shared_other, 0))
+    if n_hidden == 2:
+        bit = w_bits[0]
+        parts = [
+            down_pieces[0],
+            flip(down_pieces[1], bit),
+            swap_core(down_pieces[2]),
+            both_ways(down_pieces[3], bit),
+        ]
+        down_experts = weight_grads([(g_steps, hidden_of[:2])])
+        total, parts, down_experts = pin((total, parts, down_experts))
+        shared_down_own = sum(part.astype(wide) for part in parts)[:f_shared].astype(narrow)
+    else:
+        parts = [
+            mine.astype(wide) + swap_core(other).astype(wide)
+            for mine, other in zip(down_pieces[:n_hidden], down_pieces[n_hidden:])
+        ]
+        down_experts = weight_grads([(g_steps, hidden_of[:2])])
+        shared_down_own = shared_sum(parts)[:f_shared]
+    shared_down_all = lax.all_gather(shared_down_own, "dp", axis=0, tiled=True)
     normed_two_grad = dx_sums[0].astype(wide) + total.astype(wide)
 
     grad_wide = grad_own.astype(wide)
@@ -966,24 +1004,21 @@
     )
     own_low = hidden_grad.astype(narrow)
     if n_tensor == 4:
-        own_low, x_steps, shared_down_own = pin((own_low, x_steps, shared_down_own))
+        own_low, x_steps = pin((own_low, x_steps))
+        shared_other = swap_core(shared_other)
         one, two = flip(own_low, 1), flip(own_low, 2)
-        gate_experts = weight_grads([(x_steps, gate_of[:2])], 2, True)
+        gate_experts = weight_grads([(x_steps, gate_of[:2])])
         one, two, gate_experts, shared_mine, shared_other = pin(
             (one, two, gate_experts, shared_mine, shared_other)
         )
         grad_blocks = [own_low, one, two, flip(one, 2)]
     else:
-        gate_experts = weight_grads([(x_steps, gate_of[:2])], 2, True)
+        gate_experts = weight_grads([(x_steps, gate_of[:2])])
+        shared_other = swap_core(shared_other)
         grad_blocks = plane_gather(own_low)
-    down_experts = [down_mine, down_other]
-    shared_down_all = lax.all_gather(shared_down_own, "dp", axis=0, tiled=True)
-    shared_gate_own = shared_sum(shared_parts(shared_mine, shared_other, 1))
-    grad_blocks, gate_experts, shared_gate_own, shared_mine, shared_other = pin(
-        (grad_blocks, gate_experts, shared_gate_own, shared_mine, shared_other)
-    )
-    shared_gate_all = lax.all_gather(shared_gate_own, "dp", axis=0, tiled=True)
-    shared_up_own = shared_sum(shared_parts(shared_mine, shared_other, 2))
+    both = core_parts(shared_mine, shared_other, 0, 2 * f_pad)
+    shared_two_own = shared_sum([both[0]] + [part.astype(narrow) for part in both[1:]])
+    grad_blocks, gate_experts = pin((grad_blocks, gate_experts))
     hidden_grad_low = jnp.concatenate(grad_blocks, axis=0)
 
     mixed_grad = dot_nt(hidden_grad_low, o_weight).astype(narrow).reshape(GROUP, heads, HD)
@@ -994,6 +1029,8 @@
         "hts,thd->shd", probs.astype(narrow), mixed_grad, preferred_element_type=wide
     )
     inner = jnp.sum(probs * probs_grad, axis=2, keepdims=True)
+    inner, shared_two_own = pin((inner, shared_two_own))
+    shared_two_all = lax.all_gather(shared_two_own, "dp", axis=0, tiled=True)
     scores_grad = (probs * (probs_grad - inner)).astype(narrow)
     query_grad = (
         jnp.einsum("hts,shd->thd", scores_grad, key_low, preferred_element_type=wide) * scale
@@ -1001,10 +1038,7 @@
     key_grad = (
         jnp.einsum("hts,thd->shd", scores_grad, query_low, preferred_element_type=wide) * scale
     )
-    query_grad, shared_up_own, down_experts, gate_experts = pin(
-        (query_grad, shared_up_own, down_experts, gate_experts)
-    )
-    shared_up_all = lax.all_gather(shared_up_own, "dp", axis=0, tiled=True)
+    query_grad, down_experts, gate_experts = pin((query_grad, down_experts, gate_experts))
     for experts_of in (down_experts, gate_experts):
         experts_of[1] = swap_core(experts_of[1])
     query_lin_grad = rotate_back(query_grad, cosine, sine).reshape(GROUP, heads * HD).astype(narrow)
@@ -1028,13 +1062,9 @@
     def attn_part(step):
         return attn_mine[step].astype(wide) + attn_other[step].astype(wide)
 
-    here, x_steps = pin((attn_part(1).astype(narrow), x_steps))
-    total = ring_next(here)
-    up_experts = weight_grads([(x_steps, up_of[:2])], 2, True)
+    total = ring_next(attn_part(1).astype(narrow))
+    up_experts = weight_grads([(x_steps, up_of[:2])])
     up_experts[1] = swap_core(up_experts[1])
-    total, up_experts, down_experts, gate_experts = pin(
-        (total, up_experts, down_experts, gate_experts)
-    )
     norm_one_part = sum(
         dot_nt(lin_grads[:, i * width : (i + 1) * width], weight)
         for i, weight in enumerate((q_weight, k_weight, v_weight))
@@ -1048,8 +1078,8 @@
         scaled_one - hat_one * jnp.mean(scaled_one * hat_one, axis=1, keepdims=True)
     )
 
-    def small_rows():
-        gains = jnp.concatenate(
+    gains = sum_over_plane(
+        jnp.concatenate(
             [
                 attn_gain_part,
                 mlp_gain_part,
@@ -1057,11 +1087,17 @@
                 jnp.broadcast_to(squared_own, (128,)),
             ]
         )
+    )
+    gains, down_experts, gate_experts, up_experts = pin(
+        (gains, down_experts, gate_experts, up_experts)
+    )
+
+    def small_rows():
         biases = [
             jnp.sum(grad.astype(wide), axis=0)
             for grad in (query_lin_grad, key_lin_grad, value_lin_grad)
         ]
-        small = jnp.concatenate([sum_over_plane(gains), *biases])
+        small = jnp.concatenate([gains, *biases])
         small = small + swap_core(small)
         lanes = 4 * width
         count = -(-small.shape[0] // (8 * lanes)) * 8
@@ -1073,29 +1109,36 @@
     expert_gate_grad = expert_sum(*gate_experts).T[None]
     expert_up_grad = expert_sum(*up_experts).T[None]
     shared_down_grad = shared_down_all.astype(wide)
-    shared_gate_grad = turn(shared_gate_all)
-    shared_up_grad = turn(shared_up_all)
-    ties = [(), (shared_down_grad, shared_gate_grad)]
+    shared_gate_grad = turn(shared_two_all, n_dp, 0, f_shared)
+    shared_up_grad = turn(shared_two_all, n_dp, 1, f_shared)
+    ties = [(), (shared_down_grad,)]
     for step in range(2, chips):
         if step - 2 < len(ties):
             total = after(total, *ties[step - 2])
         total = ring_next((attn_part(step) + total.astype(wide)).astype(narrow))
-    total = after(total, input_grad, expert_down_grad)
+    total = after(total, input_grad, shared_gate_grad)
     attn_own = (attn_part(0) + total.astype(wide)).astype(narrow)
     attn_held = [jnp.concatenate([attn_own, small_rows()], axis=0)]
-    ties = [(shared_up_grad, expert_gate_grad), (expert_up_grad,)]
+    ties = [(shared_up_grad, expert_down_grad), (expert_gate_grad,)]
+    swapped, sums = [], None
+
+    def placed(first, last, before):
+        blocks, places_at = [], []
+        for step in range(first, last):
+            blocks += [attn_held[step], swapped[step]]
+            places_at += [source * piece for source in sources[step]]
+        return assemble(blocks, jnp.stack(places_at), piece, before)
+
     for step in range(chips - 1):
+        swapped.append(swap_core(attn_held[-1]))
         block = ring_next(attn_held[-1])
-        attn_held.append(after(block, *ties[step]) if step < len(ties) else block)
-    attn_blocks, attn_places, sums = [], [], None
-    for step, (block, at) in enumerate(zip(attn_held, sources)):
-        if step == chips - 1:
-            sums = assemble(attn_blocks, jnp.stack(attn_places), piece, None)
-            block, sums = pin((block, sums))
-            attn_blocks, attn_places = [], []
-        attn_blocks += [block, swap_core(block)]
-        attn_places += [source * piece for source in at]
-    q_sum, k_sum, v_sum, o_sum = assemble(attn_blocks, jnp.stack(attn_places), piece, sums)
+        if step == 1:
+            sums = placed(0, 1, None)
+        if step < len(ties):
+            block, swapped, sums = pin((block, swapped, sums, ties[step]))[:3]
+        attn_held.append(block)
+    swapped.append(swap_core(attn_held[-1]))
+    q_sum, k_sum, v_sum, o_sum = placed(1, chips, sums)
     small = 0.0
     for chip in range(chips):
         rows_of = sum(

time: 940 us -> 902 us (0.960)
  Pallas kernels: 287 us -> 268 us
    ppermute x42 -> x41, waiting for transfers between devices: 211 us -> 203 us  [flip(): return lax.ppermute(value, 'tensor', [(i, i ^ bit) for i in range(size)])]
    unnamed x206 -> x200, local copies, waits for them, and re-layouts: 18.9 us -> 13.3 us
    pallas_call x5 -> x4, Pallas kernels: 68.1 us -> 63 us  [weight_grads(): pl.pallas_call(functools.partial(weight_body, rows, steps, blocks, shape,...]
    ppermute x42 -> x41, starting transfers between devices: 49.4 us -> 51.3 us  [flip(): return lax.ppermute(value, 'tensor', [(i, i ^ bit) for i in range(size)])]
  transfers between devices with their start and end apart: 84 -> 84, of which waited for: 39 -> 36; matrix products, arithmetic and copies ran while one was open for 23% -> 23% of each run, Pallas kernels for 29% -> 29%
where the time goes in v4:
time: 902 us; the launch traced here: 895 us
  waiting for transfers between devices  295 us (33%)
  Pallas kernels  268 us (30%)
  other arithmetic  132 us (15%)
  starting transfers between devices  78.8 us (9%)
  matrix products  46.7 us (5%)
  local copies, waits for them, and re-layouts  46.3 us (5%)
  between operations  28.2 us (3%)
    ppermute x41, waiting for transfers between devices, flip(): return lax.ppermute(value, 'tensor', [(i, i ^ bit) for i in range(size)])  203 us
    pallas_call x4, Pallas kernels, backward_step(): pl.pallas_call(functools.partial(backward_body, rows, count, places, piec...  86.5 us
    ppermute x21, waiting for transfers between devices, ring_next(): return lax.ppermute(value, 'dp', pairs)  82.1 us
    pallas_call x4, Pallas kernels, forward_step(): pl.pallas_call(functools.partial(forward_body, rows, count, places, piece...  76.9 us
    pallas_call x4, Pallas kernels, weight_grads(): pl.pallas_call(functools.partial(weight_body, rows, steps, blocks, shape,...  63 us
    ppermute x41, starting transfers between devices, flip(): return lax.ppermute(value, 'tensor', [(i, i ^ bit) for i in range(size)])  51.3 us
    ppermute x21, starting transfers between devices, ring_next(): return lax.ppermute(value, 'dp', pairs)  23.3 us
    pallas_call x2, Pallas kernels, turn(): pl.pallas_call(turn_body, grid=(width // 256,), out_shape=jax.ShapeDtypeS...  18.5 us
  transfers between devices with their start and end apart: 84, of which 36 were waited for; matrix products, arithmetic and copies ran while one was open for 23% of the time, Pallas kernels for 29%

profile of v4, /device:TPU:0, one launch (start us, length us, event | category | flops | bytes accessed | tf_op | source)
XLA Modules:
  0.0 895.4 jit_solution(3617885017947072609)
XLA Ops:
  40.1 16.4 %collective-permute-done.2.refs_13_ = bf16[256,2048]{1,0:T(8,128)(2,1)} collective-permute-done((bf16[256,2048]{1,0:T(8,128)(2,1)}, bf16[256,2048]{1,0:T(8,128)(2,1)}, u32[]{:S(2)}, u32[]{:S(2)}) %collective-permute-start.2) | collective-permute-done | bytes 1048608 | tf_op jit(solution)/shard_map/ppermute | solution.py:92
  62.4 12.3 %collective-permute-done.3 = bf16[192,2048]{1,0:T(8,128)(2,1)S(1)} collective-permute-done((bf16[192,2048]{1,0:T(8,128)(2,1)}, bf16[192,2048]{1,0:T(8,128)(2,1)S(1)}, u32[]{:S(2)}, u32[]{:S(2)}) %collective-permute-start.3) | collective-permute-done | bytes 786464 | tf_op jit(solution)/shard_map/ppermute | solution.py:92
  117.0 15.5 %collective-permute-done.11 = bf16[192,2048]{1,0:T(8,128)(2,1)S(1)} collective-permute-done((bf16[192,2048]{1,0:T(8,128)(2,1)S(1)}, bf16[192,2048]{1,0:T(8,128)(2,1)S(1)}, u32[]{:S(2)}, u32[]{:S(2)}) %collective-permute-start.11) | collective-permute-done | bytes 786464 | tf_op jit(solution)/shard_map/ppermute | solution.py:92
  174.1 10.7 %collective-permute-done.23.refs_7_ = bf16[256,2048]{1,0:T(8,128)(2,1)} collective-permute-done((bf16[256,2048]{1,0:T(8,128)(2,1)S(1)}, bf16[256,2048]{1,0:T(8,128)(2,1)}, u32[]{:S(2)}, u32[]{:S(2)}) %collective-permute-start.23) | collective-permute-done | bytes 1048608 | tf_op jit(solution)/shard_map/ppermute | solution.py:92
  203.5 18.5 %collective-permute-done.19.refs_0_.refs_14_.refs_6_ = bf16[192,2048]{1,0:T(8,128)(2,1)} collective-permute-done((bf16[192,2048]{1,0:T(8,128)(2,1)}, bf16[192,2048]{1,0:T(8,128)(2,1)}, u32[]{:S(2)}, u32[]{:S(2)}) %collective-permute-start.19) | collective-permute-done | bytes 786464 | tf_op jit(solution)/shard_map/ppermute | solution.py:153
  222.6 19.2 %ffn_forward.4 = (bf16[192,2048]{1,0:T(8,128)(2,1)}, bf16[192,2048]{1,0:T(8,128)(2,1)}, bf16[384,704]{1,0:T(8,128)(2,1)}, bf16[384,704]{1,0:T(8,128)(2,1)}, bf16...) custom-call(bf16[192,2048]{1,0:T(8,128)(2,1)} %copy-done.51, ...), custom_call_target="tpu_custom_call" | custom-call | flops 9965666304 | bytes 33964032 | tf_op jit(solution)/shard_map/ffn_forward/pallas_call | solution.py:382
  243.3 19.4 %ffn_forward.5 = (bf16[192,2048]{1,0:T(8,128)(2,1)}, bf16[192,2048]{1,0:T(8,128)(2,1)}, bf16[384,704]{1,0:T(8,128)(2,1)}, bf16[384,704]{1,0:T(8,128)(2,1)}, bf16...) custom-call(bf16[192,2048]{1,0:T(8,128)(2,1)} %collective-permute-do, ...), custom_call_target="tpu_custom_call" | custom-call | flops 9965666304 | bytes 33964032 | tf_op jit(solution)/shard_map/ffn_forward/pallas_call | solution.py:382
  266.0 19.1 %ffn_forward.6 = (bf16[192,2048]{1,0:T(8,128)(2,1)}, bf16[192,2048]{1,0:T(8,128)(2,1)}, bf16[384,704]{1,0:T(8,128)(2,1)}, bf16[384,704]{1,0:T(8,128)(2,1)}, bf16...) custom-call(bf16[192,2048]{1,0:T(8,128)(2,1)} %collective-permute-do, ...), custom_call_target="tpu_custom_call" | custom-call | flops 9965666304 | bytes 33964032 | tf_op jit(solution)/shard_map/ffn_forward/pallas_call | solution.py:382
  291.4 19.1 %ffn_forward.7 = (bf16[192,2048]{1,0:T(8,128)(2,1)}, bf16[192,2048]{1,0:T(8,128)(2,1)}, bf16[384,704]{1,0:T(8,128)(2,1)}, bf16[384,704]{1,0:T(8,128)(2,1)}, bf16...) custom-call(bf16[192,2048]{1,0:T(8,128)(2,1)} %copy-done.25, ...), custom_call_target="tpu_custom_call" | custom-call | flops 9965666304 | bytes 33964032 | tf_op jit(solution)/shard_map/ffn_forward/pallas_call | solution.py:382
  317.0 11.0 %collective-permute-done.32 = bf16[192,2048]{1,0:T(8,128)(2,1)} collective-permute-done((bf16[192,2048]{1,0:T(8,128)(2,1)}, bf16[192,2048]{1,0:T(8,128)(2,1)}, u32[]{:S(2)}, u32[]{:S(2)}) %collective-permute-start.32) | collective-permute-done | bytes 786464 | tf_op jit(solution)/shard_map/ppermute | solution.py:92
  338.8 14.0 %collective-permute-done.41.refs_1_ = bf16[192,2048]{1,0:T(8,128)(2,1)S(1)} collective-permute-done((bf16[192,2048]{1,0:T(8,128)(2,1)S(1)}, bf16[192,2048]{1,0:T(8,128)(2,1)S(1)}, u32[]{:S(2)}, u32[]{:S(2)}) %collective-permute-start.41) | collective-permute-done | bytes 786464 | tf_op jit(solution)/shard_map/ppermute | solution.py:92
  356.2 21.5 %ffn_backward.4 = (bf16[192,2048]{1,0:T(8,128)(2,1)}, bf16[192,2048]{1,0:T(8,128)(2,1)}, bf16[384,704]{1,0:T(8,128)(2,1)}, bf16[384,704]{1,0:T(8,128)(2,1)}, bf1...) custom-call(bf16[192,2048]{1,0:T(8,128)(2,1)} %copy-done.22, ...), custom_call_target="tpu_custom_call" | custom-call | flops 9965666304 | bytes 35586048 | tf_op jit(solution)/shard_map/ffn_backward/pallas_call | solution.py:480
  382.6 21.7 %ffn_backward.5 = (bf16[192,2048]{1,0:T(8,128)(2,1)}, bf16[192,2048]{1,0:T(8,128)(2,1)}, bf16[384,704]{1,0:T(8,128)(2,1)}, bf16[384,704]{1,0:T(8,128)(2,1)}, bf1...) custom-call(bf16[192,2048]{1,0:T(8,128)(2,1)} %collective-permute-do, ...), custom_call_target="tpu_custom_call" | custom-call | flops 9965666304 | bytes 35586048 | tf_op jit(solution)/shard_map/ffn_backward/pallas_call | solution.py:480
  417.0 21.7 %ffn_backward.6 = (bf16[192,2048]{1,0:T(8,128)(2,1)}, bf16[192,2048]{1,0:T(8,128)(2,1)}, bf16[384,704]{1,0:T(8,128)(2,1)}, bf16[384,704]{1,0:T(8,128)(2,1)}, bf1...) custom-call(bf16[192,2048]{1,0:T(8,128)(2,1)} %collective-permute-do, ...), custom_call_target="tpu_custom_call" | custom-call | flops 9965666304 | bytes 35586048 | tf_op jit(solution)/shard_map/ffn_backward/pallas_call | solution.py:480
  451.8 21.6 %ffn_backward.7 = (bf16[192,2048]{1,0:T(8,128)(2,1)}, bf16[192,2048]{1,0:T(8,128)(2,1)}, bf16[384,704]{1,0:T(8,128)(2,1)}, bf16[384,704]{1,0:T(8,128)(2,1)}, bf1...) custom-call(bf16[192,2048]{1,0:T(8,128)(2,1)} %collective-permute-do, ...), custom_call_target="tpu_custom_call" | custom-call | flops 9965666304 | bytes 35586048 | tf_op jit(solution)/shard_map/ffn_backward/pallas_call | solution.py:480
  477.5 19.4 %weight_grads.4 = (bf16[176,2048]{1,0:T(8,128)(2,1)}, bf16[176,2048]{1,0:T(8,128)(2,1)}, bf16[176,2048]{1,0:T(8,128)(2,1)}, bf16[176,2048]{1,0:T(8,128)(2,1)}, b...) custom-call(bf16[192,2048]{1,0:T(8,128)(2,1)} %copy-done.22, bf16[192,2048]{1,0:T(8,128)(2,1)} %copy-done.90, ...), custom_call_target="tpu_custom_call" | custom-call | flops 13287555072 | bytes 21430272 | tf_op jit(solution)/shard_map/weight_grads/pallas_call | solution.py:563
  503.9 14.5 %weight_grads.5 = (bf16[704,2048]{1,0:T(8,128)(2,1)}, bf16[704,2048]{1,0:T(8,128)(2,1)}) custom-call(bf16[192,2048]{1,0:T(8,128)(2,1)} %copy-done.22, bf16[192,2048]{1,0:T(8,128)(2,1)} %copy-done.90, bf16[192,2048]{1,0:T(8,128)(2,1)} %collective-permute-done.36.refs_0_.refs_2_, bf16[192,2048]{1,0:T(8,128)(2,1)} %collective-permute-done.40.refs_1_.refs_3_, ...), custom_call_target="tpu_custom_call" | custom-call | flops 8858370048 | bytes 16384000 | tf_op jit(solution)/shard_map/weight_grads/pallas_call | solution.py:563
  537.3 14.6 %weight_grads.6 = (bf16[704,2048]{1,0:T(8,128)(2,1)}, bf16[704,2048]{1,0:T(8,128)(2,1)}) custom-call(bf16[192,2048]{1,0:T(8,128)(2,1)} %copy-done.25, bf16[192,2048]{1,0:T(8,128)(2,1)} %copy-done.49, bf16[192,2048]{1,0:T(8,128)(2,1)} %copy-done.51, bf16[192,2048]{1,0:T(8,128)(2,1)} %copy-done.53, ...), custom_call_target="tpu_custom_call" | custom-call | flops 8858370048 | bytes 16384000 | tf_op jit(solution)/shard_map/weight_grads/pallas_call | solution.py:563
  561.3 13.4 %collective-permute-done.56 = bf16[192,2048]{1,0:T(8,128)(2,1)S(1)} collective-permute-done((bf16[192,2048]{1,0:T(8,128)(2,1)S(1)}, bf16[192,2048]{1,0:T(8,128)(2,1)S(1)}, u32[]{:S(2)}, u32[]{:S(2)}) %collective-permute-start.56) | collective-permute-done | bytes 786464 | tf_op jit(solution)/shard_map/ppermute | solution.py:92
  613.4 10.5 %multiply_convert_fusion = bf16[4,768,768]{1,2,0:T(8,128)(2,1)} fusion(f32[4,768,768]{1,2,0:T(8,128)} %get-tuple-element.632, f32[4,768,768]{1,2,0:T(8,128)} %copy-done.1, f32[4,768]{1,0:T(4,128)S(1)} %get-tuple-element.631, f32[4,768]{1,0:T(4,128)S(1)} %log_add_fusion), kind=kLoop, calls=%fused_computation | loop fusion | flops 9437184 | bytes 23617536 | tf_op jit(solution)/shard_map/convert_element_type | solution.py:1034
  643.2 12.6 %attention_grads.1 = (bf16[4,256,2048]{2,1,0:T(8,128)(2,1)}, bf16[4,256,2048]{2,1,0:T(8,128)(2,1)}) custom-call(s32[8]{0:T(128)} %stack.109.order, bf16[768,2048]{1,0:T(8,128)(2,1)} %pad_maximum_fusion.normed, bf16[768,1536]{1,0:T(8,128)(2,1)} %pad_maximum_fusion.1.grads, bf16[768,2048]{1,0:T(8,128)(2,1)} %copy-done.66, bf16[768,512]{1,0:T(8,128)(2,1)} %copy-done.48), custom_call_target="tpu_custom_call" | custom-call | flops 6442450944 | bytes 17825792 | tf_op jit(solution)/shard_map/attention_grads/pallas_call | solution.py:606
  678.2 14.5 %weight_grads.7 = (bf16[704,2048]{1,0:T(8,128)(2,1)}, bf16[704,2048]{1,0:T(8,128)(2,1)}) custom-call(bf16[192,2048]{1,0:T(8,128)(2,1)} %copy-done.25, bf16[192,2048]{1,0:T(8,128)(2,1)} %copy-done.49, bf16[192,2048]{1,0:T(8,128)(2,1)} %copy-done.51, bf16[192,2048]{1,0:T(8,128)(2,1)} %copy-done.53, ...), custom_call_target="tpu_custom_call" | custom-call | flops 8858370048 | bytes 16384000 | tf_op jit(solution)/shard_map/weight_grads/pallas_call | solution.py:563
  695.6 28.5 %collective-permute-done.69 = bf16[256,2048]{1,0:T(8,128)(2,1)} collective-permute-done((bf16[256,2048]{1,0:T(8,128)(2,1)S(1)}, bf16[256,2048]{1,0:T(8,128)(2,1)}, u32[]{:S(2)}, u32[]{:S(2)}) %collective-permute-start.69) | collective-permute-done | bytes 1048608 | tf_op jit(solution)/shard_map/ppermute | solution.py:153
  729.9 13.6 %collective-permute-done.60 = bf16[192,2048]{1,0:T(8,128)(2,1)S(1)} collective-permute-done((bf16[192,2048]{1,0:T(8,128)(2,1)S(1)}, bf16[192,2048]{1,0:T(8,128)(2,1)S(1)}, u32[]{:S(2)}, u32[]{:S(2)}) %collective-permute-start.60) | collective-permute-done | bytes 786464 | tf_op jit(solution)/shard_map/ppermute | solution.py:92
  (530 shorter events, 463.7 us)
Async XLA Ops:
  7.2 745.6 %all-gather.3.cloned.1.call-start = ((), (), s32[]{:S(2)}) async-start(), calls=%async_computation | async-start | bytes 6488064 | tf_op jit(solution)/shard_map/all_gather | solution.py:991
  17.2 39.3 %collective-permute-start.2 = (bf16[256,2048]{1,0:T(8,128)(2,1)}, bf16[256,2048]{1,0:T(8,128)(2,1)}, u32[]{:S(2)}, u32[]{:S(2)}) collective-permute-start(bf16[256,2048]{1,0:T(8,128)(2,1)} %slice_bitcast_fusion), channel_id=1, source_target_pairs={{0,1},{1,0},{2,3},{3,2},{4,5},{5,4},{6,7},{7,6},{8,9},{9,8},{10,11... | collective-permute-start | bytes 3145736 | tf_op jit(solution)/shard_map/ppermute | solution.py:92
  27.3 78.0 %collective-permute-start.8 = (bf16[528,2048]{1,0:T(8,128)(2,1)}, bf16[528,2048]{1,0:T(8,128)(2,1)}, u32[]{:S(2)}, u32[]{:S(2)}) collective-permute-start(bf16[528,2048]{1,0:T(8,128)(2,1)} %pad_maximum_fusion.4.refs_6_), channel_id=1, source_target_pairs={{0,4},{4,0},{8,12},{12,8},{16,20},{20,16},{24,28},{28,24},{1,5},{5... | collective-permute-start | bytes 6488072 | tf_op jit(solution)/shard_map/ppermute | solution.py:158
  60.1 78.7 %collective-permute-start.12 = (bf16[528,2048]{1,0:T(8,128)(2,1)}, bf16[528,2048]{1,0:T(8,128)(2,1)}, u32[]{:S(2)}, u32[]{:S(2)}) collective-permute-start(bf16[528,2048]{1,0:T(8,128)(2,1)} %pad_maximum_fusion.2.refs_2_), channel_id=1, source_target_pairs={{0,1},{1,0},{2,3},{3,2},{4,5},{5,4},{6,7},{7,6},{8,9},{9,8},{10,11... | collective-permute-start | bytes 6488072 | tf_op jit(solution)/shard_map/ppermute | solution.py:92
  61.9 43.4 %collective-permute-start.7 = (bf16[528,2048]{1,0:T(8,128)(2,1)}, bf16[528,2048]{1,0:T(8,128)(2,1)}, u32[]{:S(2)}, u32[]{:S(2)}) collective-permute-start(bf16[528,2048]{1,0:T(8,128)(2,1)} %pad_maximum_fusion.2.refs_2_), channel_id=1, source_target_pairs={{0,4},{4,0},{8,12},{12,8},{16,20},{20,16},{24,28},{28,24},{1,5},{5... | collective-permute-start | bytes 6488072 | tf_op jit(solution)/shard_map/ppermute | solution.py:158
  61.9 43.4 %collective-permute-start.9 = (bf16[528,2048]{1,0:T(8,128)(2,1)}, bf16[528,2048]{1,0:T(8,128)(2,1)}, u32[]{:S(2)}, u32[]{:S(2)}) collective-permute-start(bf16[528,2048]{1,0:T(8,128)(2,1)} %pad_maximum_fusion.3.refs_12_), channel_id=1, source_target_pairs={{0,4},{4,0},{8,12},{12,8},{16,20},{20,16},{24,28},{28,24},{1,5},{5... | collective-permute-start | bytes 6488072 | tf_op jit(solution)/shard_map/ppermute | solution.py:158
  115.5 29.2 %collective-permute-start.10 = (bf16[192,2048]{1,0:T(8,128)(2,1)S(1)}, bf16[192,2048]{1,0:T(8,128)(2,1)S(1)}, u32[]{:S(2)}, u32[]{:S(2)}) collective-permute-start(bf16[192,2048]{1,0:T(8,128)(2,1)S(1)} %get-tuple-element.601), channel_id=1, source_target_pairs={{0,2},{1,3},{2,0},{3,1},{4,6},{5,7},{6,4},{7,5},{8,10},{9,11},{10,... | collective-permute-start | bytes 2359304 | tf_op jit(solution)/shard_map/ppermute | solution.py:92
  173.4 49.2 %collective-permute-start.22 = (bf16[528,2048]{1,0:T(8,128)(2,1)}, bf16[528,2048]{1,0:T(8,128)(2,1)}, u32[]{:S(2)}, u32[]{:S(2)}) collective-permute-start(bf16[528,2048]{1,0:T(8,128)(2,1)} %collective-permute-done.12.refs_3_), channel_id=1, source_target_pairs={{0,4},{4,0},{8,12},{12,8},{16,20},{20,16},{24,28},{28,24},{1,5},{5... | collective-permute-start | bytes 6488072 | tf_op jit(solution)/shard_map/ppermute | solution.py:158
  202.2 41.1 %collective-permute-start.21 = (bf16[192,2048]{1,0:T(8,128)(2,1)}, bf16[192,2048]{1,0:T(8,128)(2,1)}, u32[]{:S(2)}, u32[]{:S(2)}) collective-permute-start(bf16[192,2048]{1,0:T(8,128)(2,1)} %collective-permute-done.17.refs_0_.refs_12_.refs_4_), channel_id=1, source_target_pairs={{0,2},{1,3},{2,0},{3,1},{4,6},{5,7},{6,4},{7,5},{8,10},{9,11},{10,... | collective-permute-start | bytes 2359304 | tf_op jit(solution)/shard_map/ppermute | solution.py:92
  382.4 33.0 %collective-permute-start.38 = (bf16[192,2048]{1,0:T(8,128)(2,1)}, bf16[192,2048]{1,0:T(8,128)(2,1)}, u32[]{:S(2)}, u32[]{:S(2)}) collective-permute-start(bf16[192,2048]{1,0:T(8,128)(2,1)} %collective-permute-done.37.refs_0_.refs_4_), channel_id=1, source_target_pairs={{0,2},{1,3},{2,0},{3,1},{4,6},{5,7},{6,4},{7,5},{8,10},{9,11},{10,... | collective-permute-start | bytes 2359304 | tf_op jit(solution)/shard_map/ppermute | solution.py:92
  404.3 34.9 %collective-permute-start.45 = (bf16[192,2048]{1,0:T(8,128)(2,1)}, bf16[192,2048]{1,0:T(8,128)(2,1)}, u32[]{:S(2)}, u32[]{:S(2)}) collective-permute-start(bf16[192,2048]{1,0:T(8,128)(2,1)} %get-tuple-element.357), channel_id=1, source_target_pairs={{0,2},{1,3},{2,0},{3,1},{4,6},{5,7},{6,4},{7,5},{8,10},{9,11},{10,... | collective-permute-start | bytes 2359304 | tf_op jit(solution)/shard_map/ppermute | solution.py:92
  415.4 33.7 %collective-permute-start.43 = (bf16[192,2048]{1,0:T(8,128)(2,1)}, bf16[192,2048]{1,0:T(8,128)(2,1)}, u32[]{:S(2)}, u32[]{:S(2)}) collective-permute-start(bf16[192,2048]{1,0:T(8,128)(2,1)} %collective-permute-done.39.refs_0_.refs_6_), channel_id=1, source_target_pairs={{0,2},{1,3},{2,0},{3,1},{4,6},{5,7},{6,4},{7,5},{8,10},{9,11},{10,... | collective-permute-start | bytes 2359304 | tf_op jit(solution)/shard_map/ppermute | solution.py:92
  438.7 36.7 %collective-permute-start.44 = (bf16[192,2048]{1,0:T(8,128)(2,1)}, bf16[192,2048]{1,0:T(8,128)(2,1)S(1)}, u32[]{:S(2)}, u32[]{:S(2)}) collective-permute-start(bf16[192,2048]{1,0:T(8,128)(2,1)} %get-tuple-element.369), channel_id=1, source_target_pairs={{0,2},{1,3},{2,0},{3,1},{4,6},{5,7},{6,4},{7,5},{8,10},{9,11},{10,... | collective-permute-start | bytes 2359304 | tf_op jit(solution)/shard_map/ppermute | solution.py:92
  528.7 241.0 %all-gather.5.cloned.1.call-start = ((), (), s32[]{:S(2)}) async-start(), calls=%async_computation.1 | async-start | bytes 12976128 | tf_op jit(solution)/shard_map/all_gather | solution.py:1033
  559.9 32.6 %collective-permute-start.57 = (bf16[352,2048]{1,0:T(8,128)(2,1)S(1)}, bf16[352,2048]{1,0:T(8,128)(2,1)S(1)}, u32[]{:S(2)}, u32[]{:S(2)}) collective-permute-start(bf16[352,2048]{1,0:T(8,128)(2,1)S(1)} %add_convert_fusion.5), channel_id=1, source_target_pairs={{0,1},{1,0},{2,3},{3,2},{4,5},{5,4},{6,7},{7,6},{8,9},{9,8},{10,11... | collective-permute-start | bytes 4325384 | tf_op jit(solution)/shard_map/ppermute | solution.py:92
  662.2 102.8 %collective-permute-start.65 = (bf16[704,2048]{1,0:T(8,128)(2,1)}, bf16[704,2048]{1,0:T(8,128)(2,1)}, u32[]{:S(2)}, u32[]{:S(2)}) collective-permute-start(bf16[704,2048]{1,0:T(8,128)(2,1)} %get-tuple-element.500), channel_id=1, source_target_pairs={{0,4},{4,0},{8,12},{12,8},{16,20},{20,16},{24,28},{28,24},{1,5},{5... | collective-permute-start | bytes 8650760 | tf_op jit(solution)/shard_map/ppermute | solution.py:158
  662.7 102.4 %collective-permute-start.66 = (bf16[704,2048]{1,0:T(8,128)(2,1)}, bf16[704,2048]{1,0:T(8,128)(2,1)}, u32[]{:S(2)}, u32[]{:S(2)}) collective-permute-start(bf16[704,2048]{1,0:T(8,128)(2,1)} %get-tuple-element.502), channel_id=1, source_target_pairs={{0,4},{4,0},{8,12},{12,8},{16,20},{20,16},{24,28},{28,24},{1,5},{5... | collective-permute-start | bytes 8650760 | tf_op jit(solution)/shard_map/ppermute | solution.py:158
  665.7 58.4 %collective-permute-start.69 = (bf16[256,2048]{1,0:T(8,128)(2,1)S(1)}, bf16[256,2048]{1,0:T(8,128)(2,1)}, u32[]{:S(2)}, u32[]{:S(2)}) collective-permute-start(bf16[256,2048]{1,0:T(8,128)(2,1)S(1)} %fusion.30), channel_id=1, source_target_pairs={{0,8},{4,12},{8,24},{12,28},{24,16},{28,20},{16,0},{20,4},{1,9},{5... | collective-permute-start | bytes 3145736 | tf_op jit(solution)/shard_map/ppermute | solution.py:153
  692.7 72.4 %collective-permute-start.67 = (bf16[704,2048]{1,0:T(8,128)(2,1)}, bf16[704,2048]{1,0:T(8,128)(2,1)}, u32[]{:S(2)}, u32[]{:S(2)}) collective-permute-start(bf16[704,2048]{1,0:T(8,128)(2,1)} %get-tuple-element.520), channel_id=1, source_target_pairs={{0,4},{4,0},{8,12},{12,8},{16,20},{20,16},{24,28},{28,24},{1,5},{5... | collective-permute-start | bytes 8650760 | tf_op jit(solution)/shard_map/ppermute | solution.py:158
  694.5 35.1 %collective-permute-start.62 = (bf16[192,2048]{1,0:T(8,128)(2,1)S(1)}, bf16[192,2048]{1,0:T(8,128)(2,1)S(1)}, u32[]{:S(2)}, u32[]{:S(2)}) collective-permute-start(bf16[192,2048]{1,0:T(8,128)(2,1)S(1)} %pad_maximum_fusion.7), channel_id=1, source_target_pairs={{0,2},{1,3},{2,0},{3,1},{4,6},{5,7},{6,4},{7,5},{8,10},{9,11},{10,... | collective-permute-start | bytes 2359304 | tf_op jit(solution)/shard_map/ppermute | solution.py:92
  729.6 31.9 %collective-permute-start.70 = (bf16[256,2048]{1,0:T(8,128)(2,1)S(1)}, bf16[256,2048]{1,0:T(8,128)(2,1)}, u32[]{:S(2)}, u32[]{:S(2)}) collective-permute-start(bf16[256,2048]{1,0:T(8,128)(2,1)S(1)} %fusion.10), channel_id=1, source_target_pairs={{0,8},{4,12},{8,24},{12,28},{24,16},{28,20},{16,0},{20,4},{1,9},{5... | collective-permute-start | bytes 3145736 | tf_op jit(solution)/shard_map/ppermute | solution.py:153
  768.2 34.7 %collective-permute-start.74 = (bf16[352,2048]{1,0:T(8,128)(2,1)}, bf16[352,2048]{1,0:T(8,128)(2,1)}, u32[]{:S(2)}, u32[]{:S(2)}) collective-permute-start(bf16[352,2048]{1,0:T(8,128)(2,1)} %add_convert_fusion.3), channel_id=1, source_target_pairs={{0,1},{1,0},{2,3},{3,2},{4,5},{5,4},{6,7},{7,6},{8,9},{9,8},{10,11... | collective-permute-start | bytes 4325384 | tf_op jit(solution)/shard_map/ppermute | solution.py:92
  794.9 38.9 %collective-permute-start.77 = (bf16[352,2048]{1,0:T(8,128)(2,1)}, bf16[352,2048]{1,0:T(8,128)(2,1)}, u32[]{:S(2)}, u32[]{:S(2)}) collective-permute-start(bf16[352,2048]{1,0:T(8,128)(2,1)} %add_convert_fusion.2), channel_id=1, source_target_pairs={{0,1},{1,0},{2,3},{3,2},{4,5},{5,4},{6,7},{7,6},{8,9},{9,8},{10,11... | collective-permute-start | bytes 4325384 | tf_op jit(solution)/shard_map/ppermute | solution.py:92
  822.9 41.3 %collective-permute-start.81 = (bf16[352,2048]{1,0:T(8,128)(2,1)}, bf16[352,2048]{1,0:T(8,128)(2,1)S(1)}, u32[]{:S(2)}, u32[]{:S(2)}) collective-permute-start(bf16[352,2048]{1,0:T(8,128)(2,1)} %add_convert_fusion.1), channel_id=1, source_target_pairs={{0,1},{1,0},{2,3},{3,2},{4,5},{5,4},{6,7},{7,6},{8,9},{9,8},{10,11... | collective-permute-start | bytes 4325384 | tf_op jit(solution)/shard_map/ppermute | solution.py:92
  (157 other events, 2433.1 us)
Sparse Core Ops, SparseCore 0:
  528.8 60.4 all-gather.2
  595.8 124.4 all-gather.4

commit v5 on v4

--- a/solution.py
+++ b/solution.py
@@ -837,7 +837,8 @@
         x_chain.append(ring_next(x_chain[1]))
         x_steps.append(bits_gather(x_chain[1], r_bits))
         up_high = flip(own_up[cut:], w_bits[0])
-        x_chain[2], x_steps = pin((x_chain[2], x_steps))
+        x_chain[2], x_steps, up_low = pin((x_chain[2], x_steps, up_low))
+        up_high = after(up_high, x_chain[2])
         x_chain.append(ring_next(x_chain[2]))
         x_steps.append(bits_gather(x_chain[2], r_bits))
         x_steps.append(bits_gather(x_chain[3], r_bits))

time: 902 us -> 902 us (level)
  transfers between devices with their start and end apart: 84 -> 84, of which waited for: 36 -> 37; matrix products, arithmetic and copies ran while one was open for 23% -> 23% of each run, Pallas kernels for 29% -> 29%
where the time goes in v5:
time: 902 us; the launch traced here: 895 us
  waiting for transfers between devices  295 us (33%)
  Pallas kernels  268 us (30%)
  other arithmetic  132 us (15%)
  starting transfers between devices  78.4 us (9%)
  matrix products  46.7 us (5%)
  local copies, waits for them, and re-layouts  46.3 us (5%)
  between operations  28.2 us (3%)
    ppermute x41, waiting for transfers between devices, flip(): return lax.ppermute(value, 'tensor', [(i, i ^ bit) for i in range(size)])  202 us
    pallas_call x4, Pallas kernels, backward_step(): pl.pallas_call(functools.partial(backward_body, rows, count, places, piec...  86.5 us
    ppermute x21, waiting for transfers between devices, ring_next(): return lax.ppermute(value, 'dp', pairs)  83.5 us
    pallas_call x4, Pallas kernels, forward_step(): pl.pallas_call(functools.partial(forward_body, rows, count, places, piece...  76.9 us
    pallas_call x4, Pallas kernels, weight_grads(): pl.pallas_call(functools.partial(weight_body, rows, steps, blocks, shape,...  63 us
    ppermute x41, starting transfers between devices, flip(): return lax.ppermute(value, 'tensor', [(i, i ^ bit) for i in range(size)])  51.2 us
    ppermute x21, starting transfers between devices, ring_next(): return lax.ppermute(value, 'dp', pairs)  23.3 us
    pallas_call x2, Pallas kernels, turn(): pl.pallas_call(turn_body, grid=(width // 256,), out_shape=jax.ShapeDtypeS...  18.5 us
  transfers between devices with their start and end apart: 84, of which 37 were waited for; matrix products, arithmetic and copies ran while one was open for 23% of the time, Pallas kernels for 29%

profile of v5, /device:TPU:0, one launch (start us, length us, event | category | flops | bytes accessed | tf_op | source)
XLA Modules:
  0.0 895.5 jit_solution(13648596506181029845)
XLA Ops:
  40.1 16.4 %collective-permute-done.2.refs_13_ = bf16[256,2048]{1,0:T(8,128)(2,1)} collective-permute-done((bf16[256,2048]{1,0:T(8,128)(2,1)}, bf16[256,2048]{1,0:T(8,128)(2,1)}, u32[]{:S(2)}, u32[]{:S(2)}) %collective-permute-start.2) | collective-permute-done | bytes 1048608 | tf_op jit(solution)/shard_map/ppermute | solution.py:92
  62.4 12.3 %collective-permute-done.3 = bf16[192,2048]{1,0:T(8,128)(2,1)S(1)} collective-permute-done((bf16[192,2048]{1,0:T(8,128)(2,1)}, bf16[192,2048]{1,0:T(8,128)(2,1)S(1)}, u32[]{:S(2)}, u32[]{:S(2)}) %collective-permute-start.3) | collective-permute-done | bytes 786464 | tf_op jit(solution)/shard_map/ppermute | solution.py:92
  117.0 15.5 %collective-permute-done.11 = bf16[192,2048]{1,0:T(8,128)(2,1)S(1)} collective-permute-done((bf16[192,2048]{1,0:T(8,128)(2,1)S(1)}, bf16[192,2048]{1,0:T(8,128)(2,1)S(1)}, u32[]{:S(2)}, u32[]{:S(2)}) %collective-permute-start.11) | collective-permute-done | bytes 786464 | tf_op jit(solution)/shard_map/ppermute | solution.py:92
  173.9 10.9 %collective-permute-done.19.refs_7_ = bf16[256,2048]{1,0:T(8,128)(2,1)} collective-permute-done((bf16[256,2048]{1,0:T(8,128)(2,1)S(1)}, bf16[256,2048]{1,0:T(8,128)(2,1)}, u32[]{:S(2)}, u32[]{:S(2)}) %collective-permute-start.19) | collective-permute-done | bytes 1048608 | tf_op jit(solution)/shard_map/ppermute | solution.py:92
  203.5 18.5 %collective-permute-done.20.refs_0_.refs_14_.refs_6_ = bf16[192,2048]{1,0:T(8,128)(2,1)} collective-permute-done((bf16[192,2048]{1,0:T(8,128)(2,1)}, bf16[192,2048]{1,0:T(8,128)(2,1)}, u32[]{:S(2)}, u32[]{:S(2)}) %collective-permute-start.20) | collective-permute-done | bytes 786464 | tf_op jit(solution)/shard_map/ppermute | solution.py:153
  222.6 19.2 %ffn_forward.4 = (bf16[192,2048]{1,0:T(8,128)(2,1)}, bf16[192,2048]{1,0:T(8,128)(2,1)}, bf16[384,704]{1,0:T(8,128)(2,1)}, bf16[384,704]{1,0:T(8,128)(2,1)}, bf16...) custom-call(bf16[192,2048]{1,0:T(8,128)(2,1)} %copy-done.51, ...), custom_call_target="tpu_custom_call" | custom-call | flops 9965666304 | bytes 33964032 | tf_op jit(solution)/shard_map/ffn_forward/pallas_call | solution.py:382
  243.3 19.4 %ffn_forward.5 = (bf16[192,2048]{1,0:T(8,128)(2,1)}, bf16[192,2048]{1,0:T(8,128)(2,1)}, bf16[384,704]{1,0:T(8,128)(2,1)}, bf16[384,704]{1,0:T(8,128)(2,1)}, bf16...) custom-call(bf16[192,2048]{1,0:T(8,128)(2,1)} %collective-permute-do, ...), custom_call_target="tpu_custom_call" | custom-call | flops 9965666304 | bytes 33964032 | tf_op jit(solution)/shard_map/ffn_forward/pallas_call | solution.py:382
  266.0 19.1 %ffn_forward.6 = (bf16[192,2048]{1,0:T(8,128)(2,1)}, bf16[192,2048]{1,0:T(8,128)(2,1)}, bf16[384,704]{1,0:T(8,128)(2,1)}, bf16[384,704]{1,0:T(8,128)(2,1)}, bf16...) custom-call(bf16[192,2048]{1,0:T(8,128)(2,1)} %collective-permute-do, ...), custom_call_target="tpu_custom_call" | custom-call | flops 9965666304 | bytes 33964032 | tf_op jit(solution)/shard_map/ffn_forward/pallas_call | solution.py:382
  291.4 19.1 %ffn_forward.7 = (bf16[192,2048]{1,0:T(8,128)(2,1)}, bf16[192,2048]{1,0:T(8,128)(2,1)}, bf16[384,704]{1,0:T(8,128)(2,1)}, bf16[384,704]{1,0:T(8,128)(2,1)}, bf16...) custom-call(bf16[192,2048]{1,0:T(8,128)(2,1)} %copy-done.25, ...), custom_call_target="tpu_custom_call" | custom-call | flops 9965666304 | bytes 33964032 | tf_op jit(solution)/shard_map/ffn_forward/pallas_call | solution.py:382
  317.0 11.0 %collective-permute-done.32 = bf16[192,2048]{1,0:T(8,128)(2,1)} collective-permute-done((bf16[192,2048]{1,0:T(8,128)(2,1)}, bf16[192,2048]{1,0:T(8,128)(2,1)}, u32[]{:S(2)}, u32[]{:S(2)}) %collective-permute-start.32) | collective-permute-done | bytes 786464 | tf_op jit(solution)/shard_map/ppermute | solution.py:92
  338.8 14.0 %collective-permute-done.41.refs_1_ = bf16[192,2048]{1,0:T(8,128)(2,1)S(1)} collective-permute-done((bf16[192,2048]{1,0:T(8,128)(2,1)S(1)}, bf16[192,2048]{1,0:T(8,128)(2,1)S(1)}, u32[]{:S(2)}, u32[]{:S(2)}) %collective-permute-start.41) | collective-permute-done | bytes 786464 | tf_op jit(solution)/shard_map/ppermute | solution.py:92
  356.2 21.5 %ffn_backward.4 = (bf16[192,2048]{1,0:T(8,128)(2,1)}, bf16[192,2048]{1,0:T(8,128)(2,1)}, bf16[384,704]{1,0:T(8,128)(2,1)}, bf16[384,704]{1,0:T(8,128)(2,1)}, bf1...) custom-call(bf16[192,2048]{1,0:T(8,128)(2,1)} %copy-done.22, ...), custom_call_target="tpu_custom_call" | custom-call | flops 9965666304 | bytes 35586048 | tf_op jit(solution)/shard_map/ffn_backward/pallas_call | solution.py:480
  382.6 21.7 %ffn_backward.5 = (bf16[192,2048]{1,0:T(8,128)(2,1)}, bf16[192,2048]{1,0:T(8,128)(2,1)}, bf16[384,704]{1,0:T(8,128)(2,1)}, bf16[384,704]{1,0:T(8,128)(2,1)}, bf1...) custom-call(bf16[192,2048]{1,0:T(8,128)(2,1)} %collective-permute-do, ...), custom_call_target="tpu_custom_call" | custom-call | flops 9965666304 | bytes 35586048 | tf_op jit(solution)/shard_map/ffn_backward/pallas_call | solution.py:480
  417.0 21.7 %ffn_backward.6 = (bf16[192,2048]{1,0:T(8,128)(2,1)}, bf16[192,2048]{1,0:T(8,128)(2,1)}, bf16[384,704]{1,0:T(8,128)(2,1)}, bf16[384,704]{1,0:T(8,128)(2,1)}, bf1...) custom-call(bf16[192,2048]{1,0:T(8,128)(2,1)} %collective-permute-do, ...), custom_call_target="tpu_custom_call" | custom-call | flops 9965666304 | bytes 35586048 | tf_op jit(solution)/shard_map/ffn_backward/pallas_call | solution.py:480
  451.8 21.6 %ffn_backward.7 = (bf16[192,2048]{1,0:T(8,128)(2,1)}, bf16[192,2048]{1,0:T(8,128)(2,1)}, bf16[384,704]{1,0:T(8,128)(2,1)}, bf16[384,704]{1,0:T(8,128)(2,1)}, bf1...) custom-call(bf16[192,2048]{1,0:T(8,128)(2,1)} %collective-permute-do, ...), custom_call_target="tpu_custom_call" | custom-call | flops 9965666304 | bytes 35586048 | tf_op jit(solution)/shard_map/ffn_backward/pallas_call | solution.py:480
  477.5 19.4 %weight_grads.4 = (bf16[176,2048]{1,0:T(8,128)(2,1)}, bf16[176,2048]{1,0:T(8,128)(2,1)}, bf16[176,2048]{1,0:T(8,128)(2,1)}, bf16[176,2048]{1,0:T(8,128)(2,1)}, b...) custom-call(bf16[192,2048]{1,0:T(8,128)(2,1)} %copy-done.22, bf16[192,2048]{1,0:T(8,128)(2,1)} %copy-done.90, ...), custom_call_target="tpu_custom_call" | custom-call | flops 13287555072 | bytes 21430272 | tf_op jit(solution)/shard_map/weight_grads/pallas_call | solution.py:563
  503.8 14.5 %weight_grads.5 = (bf16[704,2048]{1,0:T(8,128)(2,1)}, bf16[704,2048]{1,0:T(8,128)(2,1)}) custom-call(bf16[192,2048]{1,0:T(8,128)(2,1)} %copy-done.22, bf16[192,2048]{1,0:T(8,128)(2,1)} %copy-done.90, bf16[192,2048]{1,0:T(8,128)(2,1)} %collective-permute-done.36.refs_0_.refs_2_, bf16[192,2048]{1,0:T(8,128)(2,1)} %collective-permute-done.40.refs_1_.refs_3_, ...), custom_call_target="tpu_custom_call" | custom-call | flops 8858370048 | bytes 16384000 | tf_op jit(solution)/shard_map/weight_grads/pallas_call | solution.py:563
  537.3 14.6 %weight_grads.6 = (bf16[704,2048]{1,0:T(8,128)(2,1)}, bf16[704,2048]{1,0:T(8,128)(2,1)}) custom-call(bf16[192,2048]{1,0:T(8,128)(2,1)} %copy-done.25, bf16[192,2048]{1,0:T(8,128)(2,1)} %copy-done.49, bf16[192,2048]{1,0:T(8,128)(2,1)} %copy-done.51, bf16[192,2048]{1,0:T(8,128)(2,1)} %copy-done.53, ...), custom_call_target="tpu_custom_call" | custom-call | flops 8858370048 | bytes 16384000 | tf_op jit(solution)/shard_map/weight_grads/pallas_call | solution.py:563
  561.4 13.4 %collective-permute-done.56 = bf16[192,2048]{1,0:T(8,128)(2,1)S(1)} collective-permute-done((bf16[192,2048]{1,0:T(8,128)(2,1)S(1)}, bf16[192,2048]{1,0:T(8,128)(2,1)S(1)}, u32[]{:S(2)}, u32[]{:S(2)}) %collective-permute-start.56) | collective-permute-done | bytes 786464 | tf_op jit(solution)/shard_map/ppermute | solution.py:92
  613.4 10.5 %multiply_convert_fusion = bf16[4,768,768]{1,2,0:T(8,128)(2,1)} fusion(f32[4,768,768]{1,2,0:T(8,128)} %get-tuple-element.636, f32[4,768,768]{1,2,0:T(8,128)} %copy-done.1, f32[4,768]{1,0:T(4,128)S(1)} %get-tuple-element.635, f32[4,768]{1,0:T(4,128)S(1)} %log_add_fusion), kind=kLoop, calls=%fused_computation | loop fusion | flops 9437184 | bytes 23617536 | tf_op jit(solution)/shard_map/convert_element_type | solution.py:1035
  643.2 12.6 %attention_grads.1 = (bf16[4,256,2048]{2,1,0:T(8,128)(2,1)}, bf16[4,256,2048]{2,1,0:T(8,128)(2,1)}) custom-call(s32[8]{0:T(128)} %stack.109.order, bf16[768,2048]{1,0:T(8,128)(2,1)} %pad_maximum_fusion.normed, bf16[768,1536]{1,0:T(8,128)(2,1)} %pad_maximum_fusion.1.grads, bf16[768,2048]{1,0:T(8,128)(2,1)} %copy-done.66, bf16[768,512]{1,0:T(8,128)(2,1)} %copy-done.48), custom_call_target="tpu_custom_call" | custom-call | flops 6442450944 | bytes 17825792 | tf_op jit(solution)/shard_map/attention_grads/pallas_call | solution.py:606
  678.1 14.5 %weight_grads.7 = (bf16[704,2048]{1,0:T(8,128)(2,1)}, bf16[704,2048]{1,0:T(8,128)(2,1)}) custom-call(bf16[192,2048]{1,0:T(8,128)(2,1)} %copy-done.25, bf16[192,2048]{1,0:T(8,128)(2,1)} %copy-done.49, bf16[192,2048]{1,0:T(8,128)(2,1)} %copy-done.51, bf16[192,2048]{1,0:T(8,128)(2,1)} %copy-done.53, ...), custom_call_target="tpu_custom_call" | custom-call | flops 8858370048 | bytes 16384000 | tf_op jit(solution)/shard_map/weight_grads/pallas_call | solution.py:563
  695.6 28.6 %collective-permute-done.69 = bf16[256,2048]{1,0:T(8,128)(2,1)} collective-permute-done((bf16[256,2048]{1,0:T(8,128)(2,1)S(1)}, bf16[256,2048]{1,0:T(8,128)(2,1)}, u32[]{:S(2)}, u32[]{:S(2)}) %collective-permute-start.69) | collective-permute-done | bytes 1048608 | tf_op jit(solution)/shard_map/ppermute | solution.py:153
  729.9 13.7 %collective-permute-done.60 = bf16[192,2048]{1,0:T(8,128)(2,1)S(1)} collective-permute-done((bf16[192,2048]{1,0:T(8,128)(2,1)S(1)}, bf16[192,2048]{1,0:T(8,128)(2,1)S(1)}, u32[]{:S(2)}, u32[]{:S(2)}) %collective-permute-start.60) | collective-permute-done | bytes 786464 | tf_op jit(solution)/shard_map/ppermute | solution.py:92
  (530 shorter events, 463.5 us)
Async XLA Ops:
  7.2 745.7 %all-gather.3.cloned.1.call-start = ((), (), s32[]{:S(2)}) async-start(), calls=%async_computation | async-start | bytes 6488064 | tf_op jit(solution)/shard_map/all_gather | solution.py:992
  17.2 39.3 %collective-permute-start.2 = (bf16[256,2048]{1,0:T(8,128)(2,1)}, bf16[256,2048]{1,0:T(8,128)(2,1)}, u32[]{:S(2)}, u32[]{:S(2)}) collective-permute-start(bf16[256,2048]{1,0:T(8,128)(2,1)} %slice_bitcast_fusion), channel_id=1, source_target_pairs={{0,1},{1,0},{2,3},{3,2},{4,5},{5,4},{6,7},{7,6},{8,9},{9,8},{10,11... | collective-permute-start | bytes 3145736 | tf_op jit(solution)/shard_map/ppermute | solution.py:92
  27.3 78.0 %collective-permute-start.8 = (bf16[528,2048]{1,0:T(8,128)(2,1)}, bf16[528,2048]{1,0:T(8,128)(2,1)}, u32[]{:S(2)}, u32[]{:S(2)}) collective-permute-start(bf16[528,2048]{1,0:T(8,128)(2,1)} %pad_maximum_fusion.4.refs_6_), channel_id=1, source_target_pairs={{0,4},{4,0},{8,12},{12,8},{16,20},{20,16},{24,28},{28,24},{1,5},{5... | collective-permute-start | bytes 6488072 | tf_op jit(solution)/shard_map/ppermute | solution.py:158
  60.1 78.7 %collective-permute-start.12 = (bf16[528,2048]{1,0:T(8,128)(2,1)}, bf16[528,2048]{1,0:T(8,128)(2,1)}, u32[]{:S(2)}, u32[]{:S(2)}) collective-permute-start(bf16[528,2048]{1,0:T(8,128)(2,1)} %pad_maximum_fusion.2.refs_2_), channel_id=1, source_target_pairs={{0,1},{1,0},{2,3},{3,2},{4,5},{5,4},{6,7},{7,6},{8,9},{9,8},{10,11... | collective-permute-start | bytes 6488072 | tf_op jit(solution)/shard_map/ppermute | solution.py:92
  61.9 43.4 %collective-permute-start.7 = (bf16[528,2048]{1,0:T(8,128)(2,1)}, bf16[528,2048]{1,0:T(8,128)(2,1)}, u32[]{:S(2)}, u32[]{:S(2)}) collective-permute-start(bf16[528,2048]{1,0:T(8,128)(2,1)} %pad_maximum_fusion.2.refs_2_), channel_id=1, source_target_pairs={{0,4},{4,0},{8,12},{12,8},{16,20},{20,16},{24,28},{28,24},{1,5},{5... | collective-permute-start | bytes 6488072 | tf_op jit(solution)/shard_map/ppermute | solution.py:158
  61.9 43.4 %collective-permute-start.9 = (bf16[528,2048]{1,0:T(8,128)(2,1)}, bf16[528,2048]{1,0:T(8,128)(2,1)}, u32[]{:S(2)}, u32[]{:S(2)}) collective-permute-start(bf16[528,2048]{1,0:T(8,128)(2,1)} %pad_maximum_fusion.3.refs_12_), channel_id=1, source_target_pairs={{0,4},{4,0},{8,12},{12,8},{16,20},{20,16},{24,28},{28,24},{1,5},{5... | collective-permute-start | bytes 6488072 | tf_op jit(solution)/shard_map/ppermute | solution.py:158
  115.5 29.2 %collective-permute-start.10 = (bf16[192,2048]{1,0:T(8,128)(2,1)S(1)}, bf16[192,2048]{1,0:T(8,128)(2,1)S(1)}, u32[]{:S(2)}, u32[]{:S(2)}) collective-permute-start(bf16[192,2048]{1,0:T(8,128)(2,1)S(1)} %get-tuple-element.605), channel_id=1, source_target_pairs={{0,2},{1,3},{2,0},{3,1},{4,6},{5,7},{6,4},{7,5},{8,10},{9,11},{10,... | collective-permute-start | bytes 2359304 | tf_op jit(solution)/shard_map/ppermute | solution.py:92
  173.4 49.2 %collective-permute-start.23 = (bf16[528,2048]{1,0:T(8,128)(2,1)}, bf16[528,2048]{1,0:T(8,128)(2,1)}, u32[]{:S(2)}, u32[]{:S(2)}) collective-permute-start(bf16[528,2048]{1,0:T(8,128)(2,1)} %collective-permute-done.12.refs_3_), channel_id=1, source_target_pairs={{0,4},{4,0},{8,12},{12,8},{16,20},{20,16},{24,28},{28,24},{1,5},{5... | collective-permute-start | bytes 6488072 | tf_op jit(solution)/shard_map/ppermute | solution.py:158
  202.2 41.1 %collective-permute-start.22 = (bf16[192,2048]{1,0:T(8,128)(2,1)}, bf16[192,2048]{1,0:T(8,128)(2,1)}, u32[]{:S(2)}, u32[]{:S(2)}) collective-permute-start(bf16[192,2048]{1,0:T(8,128)(2,1)} %collective-permute-done.17.refs_0_.refs_12_.refs_4_), channel_id=1, source_target_pairs={{0,2},{1,3},{2,0},{3,1},{4,6},{5,7},{6,4},{7,5},{8,10},{9,11},{10,... | collective-permute-start | bytes 2359304 | tf_op jit(solution)/shard_map/ppermute | solution.py:92
  382.4 33.0 %collective-permute-start.38 = (bf16[192,2048]{1,0:T(8,128)(2,1)}, bf16[192,2048]{1,0:T(8,128)(2,1)}, u32[]{:S(2)}, u32[]{:S(2)}) collective-permute-start(bf16[192,2048]{1,0:T(8,128)(2,1)} %collective-permute-done.37.refs_0_.refs_4_), channel_id=1, source_target_pairs={{0,2},{1,3},{2,0},{3,1},{4,6},{5,7},{6,4},{7,5},{8,10},{9,11},{10,... | collective-permute-start | bytes 2359304 | tf_op jit(solution)/shard_map/ppermute | solution.py:92
  404.3 34.9 %collective-permute-start.45 = (bf16[192,2048]{1,0:T(8,128)(2,1)}, bf16[192,2048]{1,0:T(8,128)(2,1)}, u32[]{:S(2)}, u32[]{:S(2)}) collective-permute-start(bf16[192,2048]{1,0:T(8,128)(2,1)} %get-tuple-element.361), channel_id=1, source_target_pairs={{0,2},{1,3},{2,0},{3,1},{4,6},{5,7},{6,4},{7,5},{8,10},{9,11},{10,... | collective-permute-start | bytes 2359304 | tf_op jit(solution)/shard_map/ppermute | solution.py:92
  415.4 33.7 %collective-permute-start.43 = (bf16[192,2048]{1,0:T(8,128)(2,1)}, bf16[192,2048]{1,0:T(8,128)(2,1)}, u32[]{:S(2)}, u32[]{:S(2)}) collective-permute-start(bf16[192,2048]{1,0:T(8,128)(2,1)} %collective-permute-done.39.refs_0_.refs_6_), channel_id=1, source_target_pairs={{0,2},{1,3},{2,0},{3,1},{4,6},{5,7},{6,4},{7,5},{8,10},{9,11},{10,... | collective-permute-start | bytes 2359304 | tf_op jit(solution)/shard_map/ppermute | solution.py:92
  438.6 36.7 %collective-permute-start.44 = (bf16[192,2048]{1,0:T(8,128)(2,1)}, bf16[192,2048]{1,0:T(8,128)(2,1)S(1)}, u32[]{:S(2)}, u32[]{:S(2)}) collective-permute-start(bf16[192,2048]{1,0:T(8,128)(2,1)} %get-tuple-element.373), channel_id=1, source_target_pairs={{0,2},{1,3},{2,0},{3,1},{4,6},{5,7},{6,4},{7,5},{8,10},{9,11},{10,... | collective-permute-start | bytes 2359304 | tf_op jit(solution)/shard_map/ppermute | solution.py:92
  528.7 241.0 %all-gather.5.cloned.1.call-start = ((), (), s32[]{:S(2)}) async-start(), calls=%async_computation.1 | async-start | bytes 12976128 | tf_op jit(solution)/shard_map/all_gather | solution.py:1034
  559.9 32.6 %collective-permute-start.57 = (bf16[352,2048]{1,0:T(8,128)(2,1)S(1)}, bf16[352,2048]{1,0:T(8,128)(2,1)S(1)}, u32[]{:S(2)}, u32[]{:S(2)}) collective-permute-start(bf16[352,2048]{1,0:T(8,128)(2,1)S(1)} %add_convert_fusion.5), channel_id=1, source_target_pairs={{0,1},{1,0},{2,3},{3,2},{4,5},{5,4},{6,7},{7,6},{8,9},{9,8},{10,11... | collective-permute-start | bytes 4325384 | tf_op jit(solution)/shard_map/ppermute | solution.py:92
  662.2 102.9 %collective-permute-start.65 = (bf16[704,2048]{1,0:T(8,128)(2,1)}, bf16[704,2048]{1,0:T(8,128)(2,1)}, u32[]{:S(2)}, u32[]{:S(2)}) collective-permute-start(bf16[704,2048]{1,0:T(8,128)(2,1)} %get-tuple-element.504), channel_id=1, source_target_pairs={{0,4},{4,0},{8,12},{12,8},{16,20},{20,16},{24,28},{28,24},{1,5},{5... | collective-permute-start | bytes 8650760 | tf_op jit(solution)/shard_map/ppermute | solution.py:158
  662.7 102.5 %collective-permute-start.66 = (bf16[704,2048]{1,0:T(8,128)(2,1)}, bf16[704,2048]{1,0:T(8,128)(2,1)}, u32[]{:S(2)}, u32[]{:S(2)}) collective-permute-start(bf16[704,2048]{1,0:T(8,128)(2,1)} %get-tuple-element.506), channel_id=1, source_target_pairs={{0,4},{4,0},{8,12},{12,8},{16,20},{20,16},{24,28},{28,24},{1,5},{5... | collective-permute-start | bytes 8650760 | tf_op jit(solution)/shard_map/ppermute | solution.py:158
  665.7 58.5 %collective-permute-start.69 = (bf16[256,2048]{1,0:T(8,128)(2,1)S(1)}, bf16[256,2048]{1,0:T(8,128)(2,1)}, u32[]{:S(2)}, u32[]{:S(2)}) collective-permute-start(bf16[256,2048]{1,0:T(8,128)(2,1)S(1)} %fusion.30), channel_id=1, source_target_pairs={{0,8},{4,12},{8,24},{12,28},{24,16},{28,20},{16,0},{20,4},{1,9},{5... | collective-permute-start | bytes 3145736 | tf_op jit(solution)/shard_map/ppermute | solution.py:153
  692.6 72.5 %collective-permute-start.67 = (bf16[704,2048]{1,0:T(8,128)(2,1)}, bf16[704,2048]{1,0:T(8,128)(2,1)}, u32[]{:S(2)}, u32[]{:S(2)}) collective-permute-start(bf16[704,2048]{1,0:T(8,128)(2,1)} %get-tuple-element.524), channel_id=1, source_target_pairs={{0,4},{4,0},{8,12},{12,8},{16,20},{20,16},{24,28},{28,24},{1,5},{5... | collective-permute-start | bytes 8650760 | tf_op jit(solution)/shard_map/ppermute | solution.py:158
  694.4 35.2 %collective-permute-start.62 = (bf16[192,2048]{1,0:T(8,128)(2,1)S(1)}, bf16[192,2048]{1,0:T(8,128)(2,1)S(1)}, u32[]{:S(2)}, u32[]{:S(2)}) collective-permute-start(bf16[192,2048]{1,0:T(8,128)(2,1)S(1)} %pad_maximum_fusion.7), channel_id=1, source_target_pairs={{0,2},{1,3},{2,0},{3,1},{4,6},{5,7},{6,4},{7,5},{8,10},{9,11},{10,... | collective-permute-start | bytes 2359304 | tf_op jit(solution)/shard_map/ppermute | solution.py:92
  729.6 31.9 %collective-permute-start.70 = (bf16[256,2048]{1,0:T(8,128)(2,1)S(1)}, bf16[256,2048]{1,0:T(8,128)(2,1)}, u32[]{:S(2)}, u32[]{:S(2)}) collective-permute-start(bf16[256,2048]{1,0:T(8,128)(2,1)S(1)} %fusion.10), channel_id=1, source_target_pairs={{0,8},{4,12},{8,24},{12,28},{24,16},{28,20},{16,0},{20,4},{1,9},{5... | collective-permute-start | bytes 3145736 | tf_op jit(solution)/shard_map/ppermute | solution.py:153
  768.2 34.7 %collective-permute-start.74 = (bf16[352,2048]{1,0:T(8,128)(2,1)}, bf16[352,2048]{1,0:T(8,128)(2,1)}, u32[]{:S(2)}, u32[]{:S(2)}) collective-permute-start(bf16[352,2048]{1,0:T(8,128)(2,1)} %add_convert_fusion.3), channel_id=1, source_target_pairs={{0,1},{1,0},{2,3},{3,2},{4,5},{5,4},{6,7},{7,6},{8,9},{9,8},{10,11... | collective-permute-start | bytes 4325384 | tf_op jit(solution)/shard_map/ppermute | solution.py:92
  795.0 38.8 %collective-permute-start.77 = (bf16[352,2048]{1,0:T(8,128)(2,1)}, bf16[352,2048]{1,0:T(8,128)(2,1)}, u32[]{:S(2)}, u32[]{:S(2)}) collective-permute-start(bf16[352,2048]{1,0:T(8,128)(2,1)} %add_convert_fusion.2), channel_id=1, source_target_pairs={{0,1},{1,0},{2,3},{3,2},{4,5},{5,4},{6,7},{7,6},{8,9},{9,8},{10,11... | collective-permute-start | bytes 4325384 | tf_op jit(solution)/shard_map/ppermute | solution.py:92
  822.9 41.3 %collective-permute-start.81 = (bf16[352,2048]{1,0:T(8,128)(2,1)}, bf16[352,2048]{1,0:T(8,128)(2,1)S(1)}, u32[]{:S(2)}, u32[]{:S(2)}) collective-permute-start(bf16[352,2048]{1,0:T(8,128)(2,1)} %add_convert_fusion.1), channel_id=1, source_target_pairs={{0,1},{1,0},{2,3},{3,2},{4,5},{5,4},{6,7},{7,6},{8,9},{9,8},{10,11... | collective-permute-start | bytes 4325384 | tf_op jit(solution)/shard_map/ppermute | solution.py:92
  (157 other events, 2426.9 us)
Sparse Core Ops, SparseCore 0:
  528.8 60.4 all-gather.2
  595.8 124.4 all-gather.4
